TPU v7x, 32 devices: a whole 2x2x4 slice. The times are simulated.
32 devices in a mesh: dp: 16 (over z, y, core), tensor: 2 (over x).
Axes of the slice: x: 2, y: 2, z: 4, core: 2. Of those that a mesh axis runs over, the one named last changes fastest.
Arguments:
- passages: bfloat16 [16384, 768], P('dp'), may hold values from -6 to 6
- corrupted: bfloat16 [16384, 768], P('dp'), may hold values from -6 to 6
- lengths: int32 [16, 8], P('dp'), may hold values from 0 to 512, as said below
- cotangent: bfloat16 [16384, 768], P('dp'), may hold values from -6 to 6
- encoder_query: bfloat16 [768, 768], P(None, 'tensor'), may hold values from -0.21875 to 0.21875
- encoder_key: bfloat16 [768, 768], P(None, 'tensor'), may hold values from -0.21875 to 0.21875
- encoder_value: bfloat16 [768, 768], P(None, 'tensor'), may hold values from -0.21875 to 0.21875
- encoder_project: bfloat16 [768, 768], P(None, 'tensor'), may hold values from -0.875 to 0.875
- encoder_query_bias: float32 [768], P('tensor'), may hold values from -3 to 3
- encoder_value_bias: float32 [768], P('tensor'), may hold values from -3 to 3
- encoder_project_bias: float32 [768], replicated, may hold values from -3 to 3
- encoder_first_gain: float32 [768], replicated, may hold values from 0.5 to 1.5
- encoder_first_shift: float32 [768], replicated, may hold values from -3 to 3
- encoder_inner: bfloat16 [768, 3072], P(None, 'tensor'), may hold values from -0.21875 to 0.21875
- encoder_inner_bias: float32 [3072], P('tensor'), may hold values from -3 to 3
- encoder_outer: bfloat16 [768, 3072], P(None, 'tensor'), may hold values from -0.109375 to 0.109375
- encoder_outer_bias: float32 [768], replicated, may hold values from -3 to 3
- encoder_second_gain: float32 [768], replicated, may hold values from 0.5 to 1.5
- encoder_second_shift: float32 [768], replicated, may hold values from -3 to 3
- decoder_query: bfloat16 [768, 768], P(None, 'tensor'), may hold values from -0.21875 to 0.21875
- decoder_key: bfloat16 [768, 768], P(None, 'tensor'), may hold values from -0.21875 to 0.21875
- decoder_value: bfloat16 [768, 768], P(None, 'tensor'), may hold values from -0.21875 to 0.21875
- decoder_project: bfloat16 [768, 768], P(None, 'tensor'), may hold values from -0.875 to 0.875
- decoder_query_bias: float32 [768], P('tensor'), may hold values from -3 to 3
- decoder_value_bias: float32 [768], P('tensor'), may hold values from -3 to 3
- decoder_project_bias: float32 [768], replicated, may hold values from -3 to 3
- decoder_first_gain: float32 [768], replicated, may hold values from 0.5 to 1.5
- decoder_first_shift: float32 [768], replicated, may hold values from -3 to 3
- decoder_inner: bfloat16 [768, 3072], P(None, 'tensor'), may hold values from -0.21875 to 0.21875
- decoder_inner_bias: float32 [3072], P('tensor'), may hold values from -3 to 3
- decoder_outer: bfloat16 [768, 3072], P(None, 'tensor'), may hold values from -0.109375 to 0.109375
- decoder_outer_bias: float32 [768], replicated, may hold values from -3 to 3
- decoder_second_gain: float32 [768], replicated, may hold values from 0.5 to 1.5
- decoder_second_shift: float32 [768], replicated, may hold values from -3 to 3
Outputs:
- decoded: bfloat16 [16384, 768], P('dp')
- delta_passages: float32 [16384, 768], P('dp')
- delta_corrupted: float32 [16384, 768], P('dp')
- delta_encoder_query: float32 [768, 768], P('dp', 'tensor')
- delta_encoder_key: float32 [768, 768], P('dp', 'tensor')
- delta_encoder_value: float32 [768, 768], P('dp', 'tensor')
- delta_encoder_project: float32 [768, 768], P('dp', 'tensor')
- delta_encoder_query_bias: float32 [768], P('tensor')
- delta_encoder_value_bias: float32 [768], P('tensor')
- delta_encoder_project_bias: float32 [768], replicated
- delta_encoder_first_gain: float32 [768], replicated
- delta_encoder_first_shift: float32 [768], replicated
- delta_encoder_inner: float32 [768, 3072], P('dp', 'tensor')
- delta_encoder_inner_bias: float32 [3072], P('tensor')
- delta_encoder_outer: float32 [768, 3072], P('dp', 'tensor')
- delta_encoder_outer_bias: float32 [768], replicated
- delta_encoder_second_gain: float32 [768], replicated
- delta_encoder_second_shift: float32 [768], replicated
- delta_decoder_query: float32 [768, 768], P('dp', 'tensor')
- delta_decoder_key: float32 [768, 768], P('dp', 'tensor')
- delta_decoder_value: float32 [768, 768], P('dp', 'tensor')
- delta_decoder_project: float32 [768, 768], P('dp', 'tensor')
- delta_decoder_query_bias: float32 [768], P('tensor')
- delta_decoder_value_bias: float32 [768], P('tensor')
- delta_decoder_project_bias: float32 [768], replicated
- delta_decoder_first_gain: float32 [768], replicated
- delta_decoder_first_shift: float32 [768], replicated
- delta_decoder_inner: float32 [768, 3072], P('dp', 'tensor')
- delta_decoder_inner_bias: float32 [3072], P('tensor')
- delta_decoder_outer: float32 [768, 3072], P('dp', 'tensor')
- delta_decoder_outer_bias: float32 [768], replicated
- delta_decoder_second_gain: float32 [768], replicated
- delta_decoder_second_shift: float32 [768], replicated
Inputs may be any that keep to these rules, and one draw needn't show every extreme that they name: Row i holds, in order, the lengths of the passages packed one after another from slot 0 into the 1024 slots of index i; a row sums to at most 1024; zero marks an unused passage slot; some row holds a passage of 512 tokens.
All inputs are finite; a program needn't handle non-finite values.
Results may differ from a plain program's by a relative error of at most 0.04.
Values may be sent and summed in bfloat16 or wider, within the bound.
No kernel may reach another device: no remote copies, remote signals or barrier semaphores. Data moves between devices by JAX's collectives and lax.ppermute only.
A program may use at most 256 MiB of HBM per device.

v0:
```python
import functools

import jax
import jax.numpy as jnp
from jax import lax
from jax.experimental import pallas as pl
from jax.experimental.pallas import tpu as pltpu
from jax.sharding import PartitionSpec as P

HEAD_SIZE = 64
EPSILON = 1e-06
NEGATIVE = -1e30
TILE = 128
CHUNK = 256
STEP = 256
WIDE = 768
AXES = ("dp", "tensor")
VMEM_LIMIT = 56 * 1024 * 1024
F32 = jnp.float32
LOW = jnp.bfloat16


def dot(left, right, contract):
    return lax.dot_general(left, right, ((contract[0:1], contract[1:2]), ((), ())), preferred_element_type=F32)


def call(kernel, name, outs, scalars, arrays, after=(), scratch=(), steps=None, axes=None):
    outs = [jax.ShapeDtypeStruct(shape, kind) for shape, kind in outs]
    count, real = len(scalars) + len(arrays), len(outs)
    passed = [entry for entry in after if hasattr(entry, "held")]
    after = [entry for entry in after if not hasattr(entry, "held")]
    views = [entry.held for entry in passed]
    skip = count + len(views) + len(after)

    def body(*refs):
        kernel(*refs[:count], *refs[skip : skip + real], *refs[skip + real + len(views) :])

    def spec(array):
        if steps is None:
            return pl.BlockSpec(memory_space=pltpu.VMEM)
        axis = axes(array.shape)
        block = [size // steps if d == axis else size for d, size in enumerate(array.shape)]
        return pl.BlockSpec(block, lambda i: tuple(i if d == axis else 0 for d in range(len(block))))

    anywhere = pl.BlockSpec(memory_space=pl.ANY)
    results = pl.pallas_call(
        body,
        out_shape=outs + [jax.ShapeDtypeStruct(view.shape, view.dtype) for view in views],
        grid=() if steps is None else (steps,),
        in_specs=[pl.BlockSpec(memory_space=pltpu.SMEM)] * len(scalars)
        + [spec(array) for array in arrays]
        + [anywhere] * (len(views) + len(after)),
        out_specs=[spec(out) for out in outs] + [anywhere] * len(views),
        scratch_shapes=list(scratch),
        input_output_aliases={count + i: real + i for i in range(len(views))},
        compiler_params=pltpu.CompilerParams(vmem_limit_bytes=VMEM_LIMIT),
        cost_estimate=pl.CostEstimate(flops=0, bytes_accessed=0, transcendentals=0),
        name=name,
    )(*scalars, *arrays, *views, *after)
    for entry, view in zip(passed, results[real:]):
        entry.held = view
    return results[:real]


def copied(arrays, after):
    def kernel(*refs):
        for source, target in zip(refs[: len(arrays)], refs[len(arrays) :]):
            target[...] = source[...]

    return call(kernel, "copied", [(array.shape, array.dtype) for array in arrays], [], arrays, after, steps=4, axes=lambda shape: 0)


def by_rows(rows):
    return lambda shape: 0 if shape[0] == rows else None


def first_step():
    return pl.program_id(0) == 0


def last_step():
    return pl.program_id(0) == pl.num_programs(0) - 1


def over_rows(rows, chunk, body):
    def step(i, carry):
        body(pl.ds(pl.multiple_of(i * chunk, chunk), chunk), i * chunk)
        return carry

    lax.fori_loop(0, rows // chunk, step, 0)


def ends_of(home, own, far):
    ends, end = [], 0
    for p in range(own.shape[1]):
        end = end + (own[0, p] if far is None else jnp.where(home[0] == 1, own[0, p], far[0, p]))
        ends.append(end)
    return ends


def segment_of(place, ends):
    return sum((place >= end).astype(jnp.int32) for end in ends)


def start_of(place, ends):
    start = jnp.zeros_like(place)
    for end in ends:
        start = jnp.where(place >= end, end, start)
    return start


def finish_of(place, ends, rows):
    finish = jnp.full_like(place, rows)
    for end in ends[::-1]:
        finish = jnp.where(place < end, end, finish)
    return finish


def iota(shape, axis):
    return lax.broadcasted_iota(jnp.int32, shape, axis)


def split_low(values):
    first = values.astype(LOW)
    rest = values - first.astype(F32)
    second = rest.astype(LOW)
    third = (rest - second.astype(F32)).astype(LOW)
    return [first, second, third]


def gelu_and_slope(pre):
    phi_sum = 0.5 + 0.5 * lax.erf(pre * 0.7071067811865476)
    density = jnp.exp(-0.5 * pre * pre) * 0.3989422804014327
    return pre * phi_sum, phi_sum + pre * density


def norm(summed):
    center = jnp.mean(summed, axis=-1, keepdims=True)
    offset = summed - center
    scale = lax.rsqrt(jnp.mean(offset * offset, axis=-1, keepdims=True) + EPSILON)
    return offset * scale, scale


def norm_back(grad, unit, scale, gain):
    scaled = grad * gain
    return scale * (
        scaled - jnp.mean(scaled, axis=-1, keepdims=True) - unit * jnp.mean(scaled * unit, axis=-1, keepdims=True)
    )


def column_sum(values):
    return jnp.sum(values, axis=0)


def turned(pieces):
    return jnp.transpose(jnp.concatenate([piece.astype(F32) for piece in pieces], axis=0)).astype(LOW)


def eights(values):
    return jnp.sum(values.reshape(values.shape[0] // 8, 8, values.shape[1]), axis=0)


def encoder_attend(lengths, passages, query, key, value, project, query_bias, value_bias):
    rows, model = passages.shape
    part = query.shape[1]
    heads = part // HEAD_SIZE
    kept = -(-(lengths.shape[1] + 1) // 16) * 16

    def kernel(own, x_ref, q_w, k_w, v_w, p_w, q_b, v_b, xs_ref, q_ref, qk_ref, w_ref, wx_ref, o_ref, share_ref):
        ends = ends_of(None, own, None)
        firsts = [0] + ends
        row, place = iota((kept, rows), 0), iota((kept, rows), 1)
        first = jnp.zeros((kept, rows), jnp.int32)
        for p, at in enumerate(firsts):
            first = jnp.where(row == p, jnp.minimum(at, rows - 1), first)
        xs = dot((place == first).astype(LOW), x_ref[...], (1, 0)).astype(LOW)
        xs_ref[...] = xs
        same = row == segment_of(place, ends)
        queries = (dot(xs, q_w[...], (1, 0)) + q_b[...]).astype(LOW)
        q_ref[...] = queries
        head_of = iota((kept, part), 1) // HEAD_SIZE
        spread = jnp.concatenate(
            [jnp.where(head_of == h, queries, jnp.zeros_like(queries)) for h in range(heads)], axis=0
        )
        q_keys = dot(spread, k_w[...], (1, 1)).astype(LOW)
        qk_ref[...] = q_keys
        score = dot(q_keys, x_ref[...], (1, 1)) * 0.125
        score = jnp.where(same[None], score.reshape(heads, kept, rows), NEGATIVE)
        expo = jnp.exp(score - jnp.max(score, axis=2, keepdims=True))
        weights = (expo / jnp.sum(expo, axis=2, keepdims=True)).reshape(heads * kept, rows)
        w_ref[...] = weights
        low = weights.astype(LOW)
        weight_x = dot(low, x_ref[...], (1, 0)).astype(LOW)
        wx_ref[...] = weight_x
        mixed = dot(weight_x, v_w[...], (1, 0)) + jnp.sum(low.astype(F32), axis=1, keepdims=True) * v_b[...]
        mixed = sum(
            jnp.where(head_of == h, mixed[h * kept : (h + 1) * kept], 0.0) for h in range(heads)
        ).astype(LOW)
        o_ref[...] = mixed
        share_ref[...] = dot(mixed, p_w[...], (1, 1)).astype(LOW)

    return call(
        kernel,
        "encoder_attend",
        [
            ((kept, model), LOW), ((kept, part), LOW), ((heads * kept, model), LOW), ((heads * kept, rows), F32),
            ((heads * kept, model), LOW), ((kept, part), LOW), ((kept, model), LOW),
        ],
        [lengths],
        [passages, query, key, value, project, query_bias, value_bias],
    )


def encoder_feed(xs, share, far, project_bias, gain, shift, inner, inner_bias, outer, weight_x, after):
    kept, model = xs.shape
    hidden = inner.shape[1]

    count = 2 * kept + weight_x.shape[0]

    def kernel(
        xs_ref, s_ref, f_ref, pb, g1, b1, in_w, in_b, out_w, wx_ref,
        unit_ref, scale_ref, y_ref, left_ref, act_ref, slope_ref, share_ref,
    ):
        attended = s_ref[...].astype(F32) + f_ref[...].astype(F32)
        unit, scale = norm(xs_ref[...].astype(F32) + attended + pb[...])
        unit_ref[...] = unit
        scale_ref[...] = scale
        first = unit * g1[...] + b1[...]
        y_ref[...] = first
        first_low = first.astype(LOW)
        left_ref[...] = turned([xs_ref[...], first_low, wx_ref[...]])
        act, slope = gelu_and_slope(dot(first_low, in_w[...], (1, 0)) + in_b[...])
        act_ref[...] = act.astype(LOW)
        slope_ref[...] = slope
        share_ref[...] = dot(act.astype(LOW), out_w[...], (1, 1)).astype(LOW)

    return call(
        kernel,
        "encoder_feed",
        [
            ((kept, model), F32), ((kept, 1), F32), ((kept, model), F32), ((model, count), LOW), ((kept, hidden), LOW),
            ((kept, hidden), F32), ((kept, model), LOW),
        ],
        [],
        [xs, share, far, project_bias, gain, shift, inner, inner_bias, outer, weight_x],
        after,
    )


def encoder_end(first, share, far, outer_bias, gain, shift, after):
    kept, model = first.shape

    def kernel(y_ref, s_ref, f_ref, ob, g2, b2, unit_ref, scale_ref, out_ref):
        fed = s_ref[...].astype(F32) + f_ref[...].astype(F32)
        unit, scale = norm(y_ref[...] + fed + ob[...])
        unit_ref[...] = unit
        scale_ref[...] = scale
        out_ref[...] = unit * g2[...] + b2[...]

    return call(
        kernel,
        "encoder_end",
        [((kept, model), F32), ((kept, 1), F32), ((kept, model), F32)],
        [],
        [first, share, far, outer_bias, gain, shift],
        after,
    )


def encoder_feed_back(totals, unit, scale, gain, outer, slope, inner, after):
    kept, model = totals.shape
    hidden = inner.shape[1]

    def kernel(t_ref, u_ref, r_ref, g2, out_w, slope_ref, in_w, grad_ref, low_ref, pre_ref, sums_ref, bias_ref, share_ref):
        totals, unit = t_ref[...], u_ref[...]
        grad = norm_back(totals, unit, r_ref[...], g2[...])
        grad_ref[...] = grad
        sums_ref[0:1, :] = jnp.sum(grad, axis=0, keepdims=True)
        sums_ref[1:2, :] = jnp.sum(totals * unit, axis=0, keepdims=True)
        sums_ref[2:3, :] = jnp.sum(totals, axis=0, keepdims=True)
        low = grad.astype(LOW)
        low_ref[...] = low
        pre = (dot(low, out_w[...], (1, 0)) * slope_ref[...]).astype(LOW)
        pre_ref[...] = pre
        bias_ref[...] = jnp.sum(pre.astype(F32), axis=0, keepdims=True)
        share_ref[...] = dot(pre, in_w[...], (1, 1)).astype(LOW)

    return call(
        kernel,
        "encoder_feed_back",
        [
            ((kept, model), F32), ((kept, model), LOW), ((kept, hidden), LOW), ((3, model), F32), ((1, hidden), F32),
            ((kept, model), LOW),
        ],
        [],
        [totals, unit, scale, gain, outer, slope, inner],
        after,
    )


def encoder_attend_back(lengths, second, share, far, unit, scale, gain, project, query, key, value, value_bias, passages, weights, q_keys, fed_low, pre_grad, after):
    kept, model = second.shape
    rows = passages.shape[0]
    part = query.shape[1]
    heads = part // HEAD_SIZE
    hidden = pre_grad.shape[1]

    def kernel(
        own, s_grad, s_ref, f_ref, u_ref, r_ref, g1, p_w, q_w, k_w, v_w, v_b, x_ref, w_ref, qk_ref, fed_ref, pre_ref,
        grad_ref, sums_ref, right_ref, left_ref, dq_sum, dv_sum, coef_ref, carried_ref,
    ):
        unit = u_ref[...]
        first_grad = s_grad[...] + (s_ref[...].astype(F32) + f_ref[...].astype(F32))
        grad = norm_back(first_grad, unit, r_ref[...], g1[...])
        grad_ref[...] = grad
        sums_ref[0:1, :] = jnp.sum(grad, axis=0, keepdims=True)
        sums_ref[1:2, :] = jnp.sum(first_grad * unit, axis=0, keepdims=True)
        sums_ref[2:3, :] = jnp.sum(first_grad, axis=0, keepdims=True)
        low = grad.astype(LOW)
        mixed_grad = dot(low, p_w[...], (1, 0)).astype(LOW)
        right_ref[:, part : 2 * part] = mixed_grad
        right_ref[:, 2 * part :] = pre_ref[...]
        head_of = iota((kept, part), 1) // HEAD_SIZE
        spread = jnp.concatenate(
            [jnp.where(head_of == h, mixed_grad, jnp.zeros_like(mixed_grad)) for h in range(heads)], axis=0
        )
        g_values = dot(spread, v_w[...], (1, 1)).astype(LOW)
        weights = w_ref[...]
        weights_low = weights.astype(LOW)
        weight_grad = dot(g_values, x_ref[...], (1, 1)) + jnp.sum(spread.astype(F32) * v_b[...], axis=1, keepdims=True)
        middle = jnp.sum(weights * weight_grad, axis=1, keepdims=True)
        score_grad = (weights * (weight_grad - middle)).astype(LOW)
        score_x = dot(score_grad, x_ref[...], (1, 0)).astype(LOW)
        left_ref[...] = turned([fed_ref[...], low, score_x])
        q_grad = dot(score_x, k_w[...], (1, 0)) * 0.125
        q_grad = sum(jnp.where(head_of == h, q_grad[h * kept : (h + 1) * kept], 0.0) for h in range(heads)).astype(LOW)
        right_ref[:, 0:part] = q_grad
        dq_sum[...] = jnp.sum(q_grad.astype(F32), axis=0, keepdims=True)
        weight_sum = jnp.sum(weights_low.astype(F32), axis=1, keepdims=True)
        dv_sum[...] = jnp.sum(spread.astype(F32) * weight_sum, axis=0, keepdims=True)
        carried_ref[2 * heads * kept :, :] = dot(q_grad, q_w[...], (1, 1)).astype(LOW)
        ends = ends_of(None, own, None)
        same = iota((kept, rows), 0) == segment_of(iota((kept, rows), 1), ends)
        for kind, values in enumerate((score_grad, weights_low)):
            for h in range(heads):
                coefs = jnp.where(same, values[h * kept : (h + 1) * kept].astype(F32), 0.0)
                coef_ref[kind * heads + h : kind * heads + h + 1, :] = jnp.sum(coefs, axis=0, keepdims=True)
        carried_ref[0 : heads * kept, :] = qk_ref[...] * jnp.asarray(0.125, LOW)
        carried_ref[heads * kept : 2 * heads * kept, :] = g_values

    return call(
        kernel,
        "encoder_attend_back",
        [
            ((kept, model), F32), ((3, model), F32), ((kept, 2 * part + hidden), LOW), ((model, (heads + 2) * kept), LOW),
            ((1, part), F32), ((1, part), F32), ((2 * heads, rows), F32), ((2 * heads * kept + kept, model), LOW),
        ],
        [lengths],
        [
            second, share, far, unit, scale, gain, project, query, key, value, value_bias, passages,
            weights, q_keys, fed_low, pre_grad,
        ],
        after,
    )


def passages_back(chip, lengths, coefs, coefs_far, carried, carried_far, picked_grad, after):
    kinds, rows = coefs.shape
    model = carried.shape[1]
    kept = picked_grad.shape[0]
    count = kinds * kept

    def kernel(chip_ref, own, c_ref, cf_ref, v_ref, vf_ref, g_ref, out_ref):
        low_chip = chip_ref[0] == 0
        ends = ends_of(None, own, None)
        row, place = iota((kept, rows), 0), iota((kept, rows), 1)
        same = row == segment_of(place, ends)

        def spread(values):
            return jnp.concatenate(
                [jnp.where(same, values[i : i + 1, :], 0.0).astype(LOW) for i in range(kinds)], axis=0
            )

        mine, other = c_ref[...].astype(F32), cf_ref[...].astype(F32)
        first = spread(jnp.where(low_chip, mine, other))
        second = spread(jnp.where(low_chip, other, mine))
        mine, other = v_ref[0:count, :].astype(F32), vf_ref[0:count, :].astype(F32)
        first = dot(first, jnp.where(low_chip, mine, other).astype(LOW), (0, 0))
        second = dot(second, jnp.where(low_chip, other, mine).astype(LOW), (0, 0))
        leads = (same & (place == start_of(place, ends))).astype(F32).astype(LOW)
        picked = g_ref[...] + (v_ref[count:, :].astype(F32) + vf_ref[count:, :].astype(F32))
        pieces = jnp.concatenate(split_low(picked), axis=0)
        out_ref[...] = (first + second) + dot(jnp.concatenate([leads] * 3, axis=0), pieces, (0, 0))

    return call(
        kernel,
        "passages_back",
        [((rows, model), F32)],
        [chip, lengths],
        [coefs, coefs_far, carried, carried_far, picked_grad],
        after,
    )[0]


def window_sizes(tiles):
    sizes = [2, 3, 4, 6, tiles]
    return sorted({min(s, tiles) for s in sizes})


def for_window(first, last, tiles, body):
    need = last - first
    below = 0
    for size in window_sizes(tiles):
        @pl.when((need > below) & (need <= size))
        def _(size=size):
            body(size, jnp.minimum(first, tiles - size))
        below = size


def tile_window(j, ends, rows):
    low = start_of(j * TILE, ends)
    high = finish_of(j * TILE + TILE - 1, ends, rows)
    return low // TILE, (high + TILE - 1) // TILE


def decoder_attend(home, own, far, corrupt, corrupt_far, encoded, encoded_far, query, key, value, query_bias, value_bias, project, after):
    rows, model = corrupt.shape
    part = query.shape[1]
    kept = encoded.shape[0]
    heads = part // HEAD_SIZE
    tiles = rows // TILE

    def kernel(
        home_ref, own_ref, far_ref, c_ref, cf_ref, e_ref, ef_ref, q_w, k_w, v_w, q_b, v_b, p_w,
        in_ref, low_ref, q_ref, k_ref, v_ref, o_ref, lse_ref, share_ref, table_ref,
    ):
        ends = ends_of(home_ref, own_ref, far_ref)
        at_home = home_ref[0] == 1
        table_ref[...] = jnp.concatenate(split_low(jnp.where(at_home, e_ref[...], ef_ref[...])), axis=0)

        def fill(here, begin):
            place = begin + iota((TILE, 3 * kept), 0)
            lane = iota((TILE, 3 * kept), 1)
            lane = jnp.where(lane >= 2 * kept, lane - 2 * kept, jnp.where(lane >= kept, lane - kept, lane))
            member = (segment_of(place, ends) == lane).astype(F32).astype(LOW)
            corrupt = jnp.where(at_home, c_ref[here, :].astype(F32), cf_ref[here, :].astype(F32))
            d_in = corrupt + dot(member, table_ref[...], (1, 0))
            in_ref[here, :] = d_in
            low_ref[here, :] = d_in.astype(LOW)

        over_rows(rows, TILE, fill)
        q_ref[...] = (dot(low_ref[...], q_w[...], (1, 0)) + q_b[...]).astype(LOW)
        k_ref[...] = dot(low_ref[...], k_w[...], (1, 0)).astype(LOW)
        v_ref[...] = (dot(low_ref[...], v_w[...], (1, 0)) + v_b[...]).astype(LOW)
        first_head = iota((1, TILE), 1) < HEAD_SIZE
        lane = iota((TILE, TILE), 1)

        def step(j, carry):
            def body(size, begin):
                span = size * TILE
                here = pl.ds(pl.multiple_of(j * TILE, TILE), TILE)
                keys = pl.ds(pl.multiple_of(begin * TILE, TILE), span)
                row = j * TILE + iota((TILE, 1), 0)
                row = jnp.concatenate([row, row], axis=0)
                place = begin * TILE + iota((2 * TILE, span), 1)
                inside = (place >= start_of(row, ends)) & (place < finish_of(row, ends, rows))
                logs = jnp.zeros((TILE, TILE), F32)
                for pair in range(part // TILE):
                    cols = pl.ds(pair * TILE, TILE)
                    queries = q_ref[here, cols] * jnp.asarray(0.125, LOW)
                    none = jnp.zeros_like(queries)
                    queries = jnp.concatenate(
                        [jnp.where(first_head, queries, none), jnp.where(first_head, none, queries)], axis=0
                    )
                    score = jnp.where(inside, dot(queries, k_ref[keys, cols], (1, 1)), NEGATIVE)
                    top = jnp.max(score, axis=1, keepdims=True)
                    expo = jnp.exp(score - top)
                    total = jnp.sum(expo, axis=1, keepdims=True)
                    mixed = dot(expo.astype(LOW), v_ref[keys, cols], (1, 0)) * (1.0 / total)
                    log = top + jnp.log(total)
                    logs = jnp.where(lane == 2 * pair, log[0:TILE], logs)
                    logs = jnp.where(lane == 2 * pair + 1, log[TILE:], logs)
                    o_ref[here, cols] = jnp.where(first_head, mixed[0:TILE], mixed[TILE:]).astype(LOW)
                lse_ref[:, here] = jnp.transpose(logs)[0:8, :]

            first, last = tile_window(j, ends, rows)
            for_window(first, last, tiles, body)
            return carry

        lax.fori_loop(0, tiles, step, 0)
        share_ref[...] = dot(o_ref[...], p_w[...], (1, 1)).astype(LOW)

    return call(
        kernel,
        "decoder_attend",
        [
            ((rows, model), F32), ((rows, model), LOW), ((rows, part), LOW), ((rows, part), LOW), ((rows, part), LOW),
            ((rows, part), LOW), ((8, rows), F32), ((rows, model), LOW),
        ],
        [home, own, far],
        [
            corrupt, corrupt_far, encoded, encoded_far, query, key, value, query_bias, value_bias, project,
        ],
        after,
        [pltpu.VMEM((3 * kept, model), LOW)],
    )


def decoder_norm(d_in, share, far, project_bias, gain, shift, after):
    rows, model = d_in.shape

    def kernel(x_ref, s_ref, f_ref, pb, g1, b1, unit_ref, scale_ref, low_ref):
        def part(here, begin):
            attended = s_ref[here, :].astype(F32) + f_ref[here, :].astype(F32)
            unit, scale = norm(x_ref[here, :] + attended + pb[...])
            unit_ref[here, :] = unit
            scale_ref[here, :] = scale
            low_ref[here, :] = (unit * g1[...] + b1[...]).astype(LOW)

        over_rows(unit_ref.shape[0], CHUNK, part)

    return call(
        kernel,
        "decoder_norm",
        [((rows, model), F32), ((rows, 1), F32), ((rows, model), LOW)],
        [],
        [d_in, share, far, project_bias, gain, shift],
        after,
        steps=rows // STEP,
        axes=by_rows(rows),
    )


def decoder_hidden(first_low, inner, inner_bias, after):
    rows, model = first_low.shape
    hidden = inner.shape[1]
    block = 256

    def kernel(low_ref, in_w, in_b, act_ref, slope_ref, pre_ref):
        pre_ref[...] = dot(low_ref[...], in_w[...], (1, 0))

        def activate(here, begin):
            act, slope = gelu_and_slope(pre_ref[here, :] + in_b[...])
            act_ref[here, :] = act.astype(LOW)
            slope_ref[here, :] = slope.astype(LOW)

        over_rows(rows, 64, activate)

    return call(
        kernel,
        "decoder_hidden",
        [((rows, hidden), LOW), ((rows, hidden), LOW)],
        [],
        [first_low, inner, inner_bias[None]],
        after,
        [pltpu.VMEM((rows, block), F32)],
        steps=hidden // block,
        axes=lambda shape: 1 if shape[-1] == hidden else None,
    )


def weight_grads(name, left, right, base):
    rows, model = left.shape
    width = right.shape[1]
    block = WIDE
    steps = width // block
    first = steps if base is None else 0

    def kernel(l_ref, r_ref, *refs):
        refs[-1][...] = dot(l_ref[...], r_ref[...], (0, 0)).astype(LOW)

    return pl.pallas_call(
        kernel,
        out_shape=jax.ShapeDtypeStruct((model, 2 * width), LOW),
        grid=(steps,),
        in_specs=[pl.BlockSpec((rows, model), lambda i: (0, 0)), pl.BlockSpec((rows, block), lambda i: (0, i))]
        + [pl.BlockSpec(memory_space=pl.ANY)] * (base is not None),
        out_specs=pl.BlockSpec((model, block), lambda i: (0, i + first)),
        input_output_aliases={} if base is None else {2: 0},
        compiler_params=pltpu.CompilerParams(vmem_limit_bytes=VMEM_LIMIT),
        cost_estimate=pl.CostEstimate(flops=0, bytes_accessed=0, transcendentals=0),
        name=name,
    )(left, right, *([] if base is None else [base]))


def decoder_norm_back(home, own, far_lengths, unit1, share, far, first_gain, first_shift, outer_bias, gain, shift, cot, cot_far, after):
    rows, model = unit1.shape
    steps = rows // STEP

    def kernel(
        home_ref, own_ref, farl_ref, u_ref, s_ref, f_ref, g1, b1, ob, g2, b2, c_ref, cf_ref,
        out_ref, grad_ref, low_ref, sums_ref, acc_ref,
    ):
        ends = ends_of(home_ref, own_ref, farl_ref)
        at_home = home_ref[0] == 1
        height = u_ref.shape[0]

        @pl.when(first_step())
        def _():
            acc_ref[...] = jnp.zeros_like(acc_ref)

        def part(here, begin):
            fed = s_ref[here, :].astype(F32) + f_ref[here, :].astype(F32)
            first = u_ref[here, :] * g1[...] + b1[...]
            unit, scale = norm(first + fed + ob[...])
            valid = (pl.program_id(0) * height + begin + iota((CHUNK, 1), 0) < ends[-1]).astype(F32)
            out_ref[here, :] = ((unit * g2[...] + b2[...]) * valid).astype(LOW)
            cot = jnp.where(at_home, c_ref[here, :].astype(F32), cf_ref[here, :].astype(F32)) * valid
            grad = norm_back(cot, unit, scale, g2[...])
            grad_ref[here, :] = grad
            low_ref[here, :] = grad.astype(LOW)
            acc_ref[0:8, :] += eights(grad)
            acc_ref[8:16, :] += eights(cot * unit)
            acc_ref[16:24, :] += eights(cot)

        over_rows(height, CHUNK, part)

        @pl.when(last_step())
        def _():
            for i in range(3):
                sums_ref[i : i + 1, :] = jnp.sum(acc_ref[8 * i : 8 * i + 8, :], axis=0, keepdims=True)

    return call(
        kernel,
        "decoder_norm_back",
        [((rows, model), LOW), ((rows, model), F32), ((rows, model), LOW), ((3, model), F32)],
        [home, own, far_lengths],
        [
            unit1, share, far, first_gain, first_shift, outer_bias, gain, shift, cot,
            cot_far,
        ],
        after,
        [pltpu.VMEM((24, model), F32)],
        steps=steps,
        axes=by_rows(rows),
    )


def decoder_feed_back(fed_low, outer, slope, after):
    rows, model = fed_low.shape
    hidden = outer.shape[1]
    block = 256

    def kernel(low_ref, out_w, slope_ref, pre_ref, bias_ref, wide_ref, bias_acc):
        wide_ref[...] = dot(low_ref[...], out_w[...], (1, 0))
        bias_acc[...] = jnp.zeros_like(bias_acc)

        def slopes(here, begin):
            pre = (wide_ref[here, :] * slope_ref[here, :].astype(F32)).astype(LOW)
            pre_ref[here, :] = pre
            bias_acc[...] += eights(pre.astype(F32))

        over_rows(rows, 128, slopes)
        bias_ref[...] = jnp.sum(bias_acc[...], axis=0, keepdims=True)

    return call(
        kernel,
        "decoder_feed_back",
        [((rows, hidden), LOW), ((1, hidden), F32)],
        [],
        [fed_low, outer, slope],
        after,
        [pltpu.VMEM((rows, block), F32), pltpu.VMEM((8, block), F32)],
        steps=hidden // block,
        axes=lambda shape: 1 if shape[-1] == hidden else None,
    )


def decoder_first_back(second, share, far, unit, scale, gain, after):
    rows, model = second.shape

    def kernel(s_grad, s_ref, f_ref, u_ref, r_ref, g1, grad_ref, low_ref, sums_ref, acc_ref):
        @pl.when(first_step())
        def _():
            acc_ref[...] = jnp.zeros_like(acc_ref)

        def part(here, begin):
            unit = u_ref[here, :]
            first_grad = s_grad[here, :] + (s_ref[here, :].astype(F32) + f_ref[here, :].astype(F32))
            grad = norm_back(first_grad, unit, r_ref[here, :], g1[...])
            grad_ref[here, :] = grad
            low_ref[here, :] = grad.astype(LOW)
            acc_ref[0:8, :] += eights(grad)
            acc_ref[8:16, :] += eights(first_grad * unit)
            acc_ref[16:24, :] += eights(first_grad)

        over_rows(u_ref.shape[0], CHUNK, part)

        @pl.when(last_step())
        def _():
            for i in range(3):
                sums_ref[i : i + 1, :] = jnp.sum(acc_ref[8 * i : 8 * i + 8, :], axis=0, keepdims=True)

    return call(
        kernel,
        "decoder_first_back",
        [((rows, model), F32), ((rows, model), LOW), ((3, model), F32)],
        [],
        [second, share, far, unit, scale, gain],
        after,
        [pltpu.VMEM((24, model), F32)],
        steps=rows // STEP,
        axes=by_rows(rows),
    )


def decoder_attend_back(home, own, far_lengths, low, project, lse, query, key, value, query_w, key_w, value_w, after):
    rows, model = low.shape
    part = query.shape[1]
    tiles = rows // TILE

    def kernel(
        home_ref, own_ref, farl_ref, low_ref, p_w, lse_ref, q_ref, k_ref, v_ref, q_w, k_w, v_w,
        all_ref, share_ref, sums_ref, g_ref, kt_ref, dk_sum, dv_sum, acc_ref,
    ):
        ends = ends_of(home_ref, own_ref, farl_ref)
        g_ref[...] = dot(low_ref[...], p_w[...], (1, 0)).astype(LOW)
        first_head = iota((1, TILE), 1) < HEAD_SIZE
        dk_sum[...] = jnp.zeros_like(dk_sum)
        dv_sum[...] = jnp.zeros_like(dv_sum)
        acc_ref[...] = jnp.zeros_like(acc_ref)

        def turn(here, begin):
            for pair in range(part // TILE):
                cols = pl.ds(pair * TILE, TILE)
                kt_ref[cols, here] = jnp.transpose(k_ref[here, cols].astype(F32)).astype(LOW)

        over_rows(rows, TILE, turn)

        def step(j, carry):
            def body(size, begin):
                span = size * TILE
                here = pl.ds(pl.multiple_of(j * TILE, TILE), TILE)
                keys = pl.ds(pl.multiple_of(begin * TILE, TILE), span)
                column = j * TILE + iota((1, TILE), 1)
                column = jnp.concatenate([column, column], axis=1)
                place = begin * TILE + iota((span, 2 * TILE), 0)
                inside = (place >= start_of(column, ends)) & (place < finish_of(column, ends, rows))
                for pair in range(part // TILE):
                    cols = pl.ds(pair * TILE, TILE)
                    queries = q_ref[here, cols] * jnp.asarray(0.125, LOW)
                    grads = g_ref[here, cols]
                    none = jnp.zeros_like(queries)
                    queries = jnp.concatenate(
                        [jnp.where(first_head, queries, none), jnp.where(first_head, none, queries)], axis=0
                    )
                    grads = jnp.concatenate(
                        [jnp.where(first_head, grads, none), jnp.where(first_head, none, grads)], axis=0
                    )
                    log = jnp.concatenate(
                        [lse_ref[2 * pair : 2 * pair + 1, here], lse_ref[2 * pair + 1 : 2 * pair + 2, here]], axis=1
                    )
                    score = dot(k_ref[keys, cols], queries, (1, 1))
                    weight = jnp.exp(jnp.where(inside, score, NEGATIVE) - log)
                    weight_grad = dot(v_ref[keys, cols], grads, (1, 1))
                    middle = jnp.sum(weight * weight_grad, axis=0, keepdims=True)
                    score_grad = (weight * (weight_grad - middle)).astype(LOW)
                    q_grad = dot(kt_ref[cols, keys], score_grad, (1, 0)) * 0.125
                    q_grad = jnp.concatenate([q_grad[0:HEAD_SIZE, 0:TILE], q_grad[HEAD_SIZE:, TILE:]], axis=0)
                    all_ref[here, cols] = jnp.transpose(q_grad).astype(LOW)
                    dk_sum[keys, cols] += dot(score_grad, queries, (1, 0))
                    dv_sum[keys, cols] += dot(weight.astype(LOW), grads, (1, 0))

            first, last = tile_window(j, ends, rows)
            for_window(first, last, tiles, body)
            return carry

        lax.fori_loop(0, tiles, step, 0)

        def close(here, begin):
            all_ref[here, part : 2 * part] = dk_sum[here, :].astype(LOW)
            value_grad = dv_sum[here, :].astype(LOW)
            all_ref[here, 2 * part :] = value_grad
            acc_ref[:, 0:part] += eights(all_ref[here, 0:part].astype(F32))
            acc_ref[:, part:] += eights(value_grad.astype(F32))

        over_rows(rows, TILE, close)
        sums_ref[...] = jnp.sum(acc_ref[...], axis=0, keepdims=True)
        share = dot(all_ref[:, 0:part], q_w[...], (1, 1)) + dot(all_ref[:, part : 2 * part], k_w[...], (1, 1))
        share_ref[...] = (share + dot(all_ref[:, 2 * part :], v_w[...], (1, 1))).astype(LOW)

    return call(
        kernel,
        "decoder_attend_back",
        [((rows, 3 * part), LOW), ((rows, model), LOW), ((1, 2 * part), F32)],
        [home, own, far_lengths],
        [low, project, lse, query, key, value, query_w, key_w, value_w],
        after,
        [
            pltpu.VMEM((rows, part), LOW), pltpu.VMEM((part, rows), LOW), pltpu.VMEM((rows, part), F32),
            pltpu.VMEM((rows, part), F32), pltpu.VMEM((8, 2 * part), F32),
        ],
    )


def attend_weight_grads(d_low, grads, attended_low, mixed, after):
    rows, model = d_low.shape
    part = mixed.shape[1]

    def kernel(x_ref, g_ref, a_ref, o_ref, first_ref, last_ref):
        first_ref[...] = dot(x_ref[...], g_ref[:, 0 : 2 * part], (0, 0)).astype(LOW)
        last_ref[:, 0:part] = dot(x_ref[...], g_ref[:, 2 * part :], (0, 0)).astype(LOW)
        last_ref[:, part:] = dot(a_ref[...], o_ref[...], (0, 0)).astype(LOW)

    return call(
        kernel, "attend_weight_grads", [((model, 2 * part), LOW)] * 2, [], [d_low, grads, attended_low, mixed], after
    )


def pack_vectors(blocks, after):
    model = blocks[0][-1].shape[1]
    part = model // 2
    height = -(-9 * len(blocks) // 8) * 8

    def kernel(*refs):
        out = refs[-1]
        out[...] = jnp.zeros_like(out)
        for i in range(len(blocks)):
            query, value, inner, first, second = refs[5 * i : 5 * i + 5]
            row = 9 * i
            out[row : row + 1, 0:part] = query[...]
            out[row : row + 1, part:] = value[...]
            out[row + 1 : row + 2, :] = inner[:, 0:model]
            out[row + 2 : row + 3, :] = inner[:, model:]
            out[row + 3 : row + 6, :] = first[...]
            out[row + 6 : row + 9, :] = second[...]

    arrays = [array for block in blocks for array in block]
    return call(kernel, "pack_vectors", [((height, model), F32)], [], arrays, after)[0]


def decoder_end(home, own, far_lengths, grad, share, far, kept, after):
    rows, model = grad.shape
    chunk = 256

    def kernel(home_ref, own_ref, farl_ref, g_ref, s_ref, f_ref, low_ref, total_ref):
        ends = ends_of(home_ref, own_ref, farl_ref)

        @pl.when(first_step())
        def _():
            total_ref[...] = jnp.zeros_like(total_ref)

        d_in = g_ref[...] + (s_ref[...].astype(F32) + f_ref[...].astype(F32))
        low_ref[...] = d_in.astype(LOW)
        member = iota((kept, chunk), 0) == segment_of(pl.program_id(0) * chunk + iota((kept, chunk), 1), ends)
        member = member.astype(F32).astype(LOW)
        total_ref[...] += sum(dot(member, piece, (1, 0)) for piece in split_low(d_in))

    return call(
        kernel,
        "decoder_end",
        [((rows, model), LOW), ((kept, model), F32)],
        [home, own, far_lengths],
        [grad, share, far],
        after,
        steps=rows // chunk,
        axes=by_rows(rows),
    )


class Links:
    def __init__(self, mesh):
        self.dp = mesh.shape["dp"]
        self.parts = mesh.shape["tensor"]
        self.bits = (self.dp // 2).bit_length() - 1
        self.core = lax.axis_index("dp") & 1
        self.group = lax.axis_index("dp") >> 1
        self.chip = lax.axis_index("tensor")
        self.home = self.core == self.chip

    def move(self, value, target):
        pairs = []
        for i in range(self.dp):
            for t in range(self.parts):
                place = target(i, t)
                if place is not None:
                    pairs.append((i * self.parts + t, place[0] * self.parts + place[1]))
        return lax.ppermute(value, AXES, pairs)

    def swap_core(self, value):
        return self.move(value, lambda i, t: (i ^ 1, t))

    def swap_tensor(self, value):
        return self.move(value, lambda i, t: (i, t ^ 1))

    def swap_group(self, value, bit):
        return self.move(value, lambda i, t: (i ^ (2 << bit), t))

    def turn(self, value):
        moved = self.move(value, lambda i, t: None if (i & 1) == t else (i ^ 1, t ^ 1))
        return jnp.where(self.home, value, moved)

    def of_chip(self, value):
        return jnp.where(self.home, value, self.swap_core(value))

    def pick(self, value, axis, bit):
        return lax.dynamic_slice_in_dim(value, bit, 1, axis)

    def last_halving(self, value):
        view = value.reshape(2, -1, value.shape[1])
        sent = self.swap_tensor(self.pick(view, 0, 1 - self.chip).astype(LOW))
        return self.turn((self.pick(view, 0, self.chip).astype(F32) + sent.astype(F32))[0].astype(LOW)).astype(F32)

    def copies(self, value, lanes):
        rows = value.shape[0]
        value = value.reshape(rows, -1, lanes).transpose(1, 0, 2).reshape(-1, lanes)
        return jnp.broadcast_to(value[None], (self.dp,) + value.shape)

    def rows_of(self, value, rows):
        lanes = value.shape[2]
        return value.reshape(self.dp, -1, rows, lanes).transpose(0, 2, 1, 3).reshape(self.dp, rows, -1)

    def scatter_groups(self, value):
        cores = [[2 * g + c for g in range(self.dp // 2)] for c in range(2)]
        return lax.psum_scatter(value, "dp", scatter_dimension=0, axis_index_groups=cores, tiled=True)


class Held:
    def __init__(self, view):
        self.held = view


class Total:
    def __init__(self, links, value):
        self.links, self.held, self.done = links, value, 0

    def step(self):
        self.held = self.held + self.links.swap_group(self.held, self.done)
        self.done += 1

    def finish(self):
        while self.done < self.links.bits:
            self.step()
        return self.held


class Halving:
    def __init__(self, links, grad, order):
        self.links, self.order = links, list(order)
        self.width = grad.shape[1]
        self.parts = [(grad.reshape((2,) * links.bits + (-1, self.width)), {})]

    @property
    def held(self):
        return self.parts[-1][0]

    @held.setter
    def held(self, value):
        self.parts[-1] = (value, self.parts[-1][1])

    def cut(self, axis=None, bit=None):
        total = 0
        for view, own in self.parts:
            at = own if axis is None else {**own, axis: bit}
            starts = [at.get(d, 0) if view.shape[d] > 1 else 0 for d in range(view.ndim)]
            sizes = [1 if d in at else view.shape[d] for d in range(view.ndim)]
            total = total + lax.dynamic_slice(view, starts, sizes).astype(F32)
        return total

    def step(self):
        links, step = self.links, self.order.pop(0)
        axis, mine = links.bits - 1 - step, (links.group >> step) & 1
        sent = links.swap_group(self.cut(axis, 1 - mine).astype(LOW), step)
        self.parts = [(view, {**own, axis: mine}) for view, own in self.parts] + [(sent, {})]

    def left(self):
        while self.order:
            self.step()
        return self.cut().reshape(-1, self.width)


def local(mesh, passages, corrupted, lengths, cotangent, *weights):
    (
        e_query, e_key, e_value, e_project, e_query_bias, e_value_bias, e_project_bias, e_first_gain, e_first_shift,
        e_inner, e_inner_bias, e_outer, e_outer_bias, e_second_gain, e_second_shift,
    ) = weights[:15]
    (
        d_query, d_key, d_value, d_project, d_query_bias, d_value_bias, d_project_bias, d_first_gain, d_first_shift,
        d_inner, d_inner_bias, d_outer, d_outer_bias, d_second_gain, d_second_shift,
    ) = weights[15:]
    links = Links(mesh)
    rows, model = passages.shape
    part = e_query.shape[1]
    hidden = e_inner.shape[1]
    heads = part // HEAD_SIZE
    home = links.home.astype(jnp.int32)[None]

    chip = links.chip.astype(jnp.int32)[None]
    deep = model // links.dp

    d_query = links.turn(d_query)
    d_key = links.turn(d_key)
    d_halves = jnp.concatenate([d_query_bias, d_value_bias, d_inner_bias])
    lengths_far = links.swap_core(lengths)
    corrupted_far = links.swap_core(corrupted)

    x_low, e_q, q_keys, e_weights, weight_x, e_mixed, share = encoder_attend(
        lengths, passages, e_query, e_key, e_value, e_project, e_query_bias, e_value_bias
    )
    kept = x_low.shape[0]
    share_far = links.swap_tensor(share)
    d_value = links.turn(d_value)
    d_project = links.turn(d_project)
    d_halves = links.turn(d_halves)
    e_unit1, e_scale1, e_first, left_forward, e_act, e_slope, share = encoder_feed(
        x_low, share, share_far, e_project_bias, e_first_gain, e_first_shift, e_inner, e_inner_bias,
        e_outer, weight_x, (d_query, d_key, d_value, d_project, d_halves, lengths_far),
    )
    inner_held, outer_held = [Held(weight) for weight in copied([d_inner, d_outer], (share_far,))]
    e_unit2, e_scale2, encoded = encoder_end(
        e_first, share, links.swap_tensor(share), e_outer_bias, e_second_gain, e_second_shift,
        (corrupted_far, inner_held, outer_held),
    )
    d_query_bias, d_value_bias, d_inner_bias = d_halves[:part], d_halves[part : 2 * part], d_halves[2 * part :]
    left_forward = lax.all_gather(left_forward, "dp")
    right_forward = lax.all_gather(jnp.concatenate([e_act, e_mixed, e_q], axis=1), "dp")

    encoded_far = links.swap_core(encoded)
    d_inner = links.turn(inner_held.held)
    d_outer = links.turn(outer_held.held)
    d_in, d_low, query, key, value, mixed, lse, share = decoder_attend(
        home, lengths, lengths_far, corrupted, corrupted_far, encoded, encoded_far, d_query, d_key,
        d_value, d_query_bias, d_value_bias, d_project, (),
    )
    cotangent_far = links.swap_core(cotangent)
    unit1, scale1, first_low = decoder_norm(
        d_in, share, links.swap_core(share), d_project_bias, d_first_gain, d_first_shift, ()
    )
    act, slope = decoder_hidden(first_low, d_inner, d_inner_bias, ())
    share = dot(act, d_outer, (1, 1)).astype(LOW)

    decoded, second_grad, fed_low, second_sums = decoder_norm_back(
        home, lengths, lengths_far, unit1, share, links.swap_core(share), d_first_gain, d_first_shift, d_outer_bias,
        d_second_gain, d_second_shift, cotangent, cotangent_far, (),
    )
    decoded = links.turn(decoded)
    outer_grad = weight_grads("outer_grad", fed_low, act, None)
    pre_grad, inner_bias_grad = decoder_feed_back(fed_low, d_outer, slope, (outer_grad,))
    share = dot(pre_grad, d_inner, (1, 1)).astype(LOW)
    share_far = links.swap_core(share)
    feed_grads = weight_grads("inner_grad", first_low, pre_grad, outer_grad)
    first_grad, attended_low, first_sums = decoder_first_back(
        second_grad, share, share_far, unit1, scale1, d_first_gain, (feed_grads,)
    )
    feed_grads = links.scatter_groups(feed_grads)
    attend_grads, share, attend_sums = decoder_attend_back(
        home, lengths, lengths_far, attended_low, d_project, lse, query, key, value, d_query, d_key, d_value,
        (),
    )
    share_far = links.swap_core(share)
    attend_held = Held(attend_grads)
    corrupted_low, totals = decoder_end(
        home, lengths, lengths_far, first_grad, share, share_far, kept, (attend_held, decoded)
    )
    totals = links.turn(totals)
    attend_grads = attend_weight_grads(d_low, attend_held.held, attended_low, mixed, ())
    across = list(range(links.bits))
    pairs = [
        Halving(links, attend_grads[0], across),
        Halving(links, attend_grads[1], across[1:2] + across[:1] + across[2:]),
    ]
    corrupted_low = Held(corrupted_low)

    e_second_grad, e_fed_low, e_pre_grad, e_second_sums, e_inner_bias_grad, share = encoder_feed_back(
        totals, e_unit2, e_scale2, e_second_gain, e_outer, e_slope, e_inner, (*pairs,)
    )
    share_far = links.swap_tensor(share)
    for pair in pairs:
        pair.step()
    (
        e_first_grad, e_first_sums, right_back, left_back, e_query_sum, e_value_sum, coefs, carried,
    ) = encoder_attend_back(
        lengths, e_second_grad, share, share_far, e_unit1, e_scale1, e_first_gain, e_project, e_query,
        e_key, e_value, e_value_bias, passages, e_weights, q_keys, e_fed_low, e_pre_grad, (left_forward, right_forward),
    )
    vectors = pack_vectors([
        (e_query_sum, e_value_sum, e_inner_bias_grad, e_first_sums, e_second_sums),
        (attend_sums[:, :part], attend_sums[:, part:], inner_bias_grad, first_sums, second_sums),
    ], (*pairs,))
    mine = jnp.arange(vectors.shape[0])[:, None] < 9
    vectors = Total(links, vectors + jnp.where(mine, links.swap_core(vectors), links.swap_tensor(vectors)))
    for pair in pairs:
        pair.step()
    coefs = coefs.astype(LOW)
    coefs_far = links.swap_tensor(coefs)
    carried_far = links.swap_tensor(carried)
    left_back = left_back.reshape(links.dp, deep, -1)
    both = jnp.concatenate([left_back, links.copies(right_back, left_back.shape[2])], axis=1)
    both = lax.all_to_all(both, "dp", 0, 0, tiled=True)
    vectors.step()
    passages_grad = passages_back(
        chip, lengths, coefs, coefs_far, carried, carried_far, e_first_grad, (vectors, corrupted_low, *pairs),
    )
    corrupted_grad = links.turn(corrupted_low.held).astype(F32)
    d_grads = links.last_halving(jnp.concatenate([feed_grads.astype(F32)] + [pair.left() for pair in pairs], axis=1))
    edges = [0, hidden, 2 * hidden, 2 * hidden + part, 2 * hidden + 2 * part, 2 * hidden + 3 * part, d_grads.shape[1]]
    d_grads = [d_grads[:, low:high] for low, high in zip(edges, edges[1:])]
    d_grads = d_grads[2:] + d_grads[:2]
    vectors = vectors.finish()

    def cut_vectors(rows):
        return [rows[0, :part], rows[0, part:], rows[1:3].reshape(-1)] + [rows[i] for i in range(3, 9)]

    e_vectors = cut_vectors(vectors[:9])
    d_vectors = vectors[9:18]
    d_vectors = cut_vectors(jnp.concatenate([links.of_chip(d_vectors[:3]), d_vectors[3:]], axis=0))

    left_back, right_back = both[:, :deep], links.rows_of(both[:, deep:], kept)
    left_forward = lax.dynamic_slice_in_dim(left_forward, lax.axis_index("dp") * deep, deep, 1)

    def product(left, right):
        return lax.dot_general(left, right, (((0, 2), (0, 1)), ((), ())), preferred_element_type=F32)

    e_outer_grad = product(left_back[:, :, :kept], right_forward[:, :, :hidden])
    e_inner_grad = product(left_forward[:, :, kept : 2 * kept], right_back[:, :, 2 * part :])
    e_project_grad = product(left_back[:, :, kept : 2 * kept], right_forward[:, :, hidden : hidden + part])
    e_query_grad = product(left_forward[:, :, :kept], right_back[:, :, :part])
    head_of = jnp.arange(part, dtype=jnp.int32) // HEAD_SIZE

    def by_head(values):
        mine = jnp.arange(heads, dtype=jnp.int32)[None, :, None, None] == head_of[None, None, None, :]
        return jnp.where(mine, values[:, None], jnp.zeros((), LOW)).reshape(links.dp, heads * kept, part)

    e_key_grad = product(left_back[:, :, 2 * kept :], by_head(right_forward[:, :, hidden + part :])) * 0.125
    e_value_grad = product(left_forward[:, :, 2 * kept :], by_head(right_back[:, :, part : 2 * part]))

    def ordered(matrices, small):
        query_g, key_g, value_g, project_g, inner_g, outer_g = matrices
        query_b, value_b, inner_b, project_b, gain1, shift1, outer_b, gain2, shift2 = small
        return (
            query_g, key_g, value_g, project_g, query_b, value_b, project_b, gain1, shift1,
            inner_g, inner_b, outer_g, outer_b, gain2, shift2,
        )

    return (
        (decoded, passages_grad, corrupted_grad)
        + ordered((e_query_grad, e_key_grad, e_value_grad, e_project_grad, e_inner_grad, e_outer_grad), e_vectors)
        + ordered(d_grads, d_vectors)
    )


def solution(mesh):
    rows = P("dp", None)
    columns, half, whole = P(None, "tensor"), P("tensor"), P()
    block_in = (columns,) * 4 + (half, half, whole, whole, whole, columns, half, columns, whole, whole, whole)
    split = P("dp", "tensor")
    block_out = (split,) * 4 + (half, half, whole, whole, whole, split, half, split, whole, whole, whole)
    return jax.shard_map(
        functools.partial(local, mesh),
        mesh=mesh,
        in_specs=(rows,) * 4 + block_in * 2,
        out_specs=(rows,) * 3 + block_out * 2,
        check_vma=False,
    )
```

profile of v0, /device:TPU:1, one launch (start us, length us, event | category | flops | bytes accessed | tf_op | source)
XLA Modules:
  0.0 359.9 jit_solution(4122750592092569786)
XLA Ops:
  8.1 4.5 %collective-permute-start.6 = (bf16[768,384]{1,0:T(8,128)(2,1)}, bf16[768,384]{1,0:T(8,128)(2,1)S(1)}, u32[]{:S(2)}, u32[]{:S(2)}) collective-permute-start(bf16[768,384]{1,0:T(8,128)(2,1)} %param.56), channel_id=1, source_target_pairs={{1,2},{2,1},{5,6},{6,5},{9,10},{10,9},{13,14},{14,13},{17,18},{18,... | collective-permute-start | bytes 1769480 | tf_op jit(solution)/shard_map/ppermute | solution.py:878
  16.6 3.6 %collective-permute-start.7 = (f32[2304]{0:T(1024)S(1)}, f32[2304]{0:T(1024)S(1)}, u32[]{:S(2)}, u32[]{:S(2)}) collective-permute-start(f32[2304]{0:T(1024)S(1)} %constant_dynamic-update-slice_fusion), channel_id=1, source_target_pairs={{1,2},{2,1},{5,6},{6,5},{9,10},{10,9},{13,14},{14,13},{17,18},{18,... | collective-permute-start | bytes 27656 | tf_op jit(solution)/shard_map/ppermute | solution.py:878
  22.3 5.1 %encoder_attend.1 = (bf16[16,768]{1,0:T(8,128)(2,1)}, bf16[16,384]{1,0:T(8,128)(2,1)}, bf16[96,768]{1,0:T(8,128)(2,1)}, f32[96,1024]{1,0:T(8,128)}, bf16[96,768]...) custom-call(s32[1,8]{1,0:T(1,128)} %refs_1_.13, bf16[1024,768]{1,0:T(8,128)(2,1)} %refs_12_.1, ...), custom_call_target="tpu_custom_call" | custom-call | tf_op jit(solution)/shard_map/encoder_attend/pallas_call | solution.py:46
  27.4 3.8 %collective-permute-start.3 = (bf16[768,384]{1,0:T(8,128)(2,1)S(1)}, bf16[768,384]{1,0:T(8,128)(2,1)S(1)}, u32[]{:S(2)}, u32[]{:S(2)}) collective-permute-start(bf16[768,384]{1,0:T(8,128)(2,1)S(1)} %copy-done.31), channel_id=1, source_target_pairs={{1,2},{2,1},{5,6},{6,5},{9,10},{10,9},{13,14},{14,13},{17,18},{18,... | collective-permute-start | bytes 1769480 | tf_op jit(solution)/shard_map/ppermute | solution.py:878
  34.5 5.2 %collective-permute-done.3 = bf16[768,384]{1,0:T(8,128)(2,1)S(1)} collective-permute-done((bf16[768,384]{1,0:T(8,128)(2,1)S(1)}, bf16[768,384]{1,0:T(8,128)(2,1)S(1)}, u32[]{:S(2)}, u32[]{:S(2)}) %collective-permute-start.3) | collective-permute-done | bytes 589856 | tf_op jit(solution)/shard_map/ppermute | solution.py:878
  41.3 4.4 %encoder_feed.1 = (f32[16,768]{1,0:T(8,128)}, f32[16,1]{1,0:T(8,128)}, f32[16,768]{1,0:T(8,128)}, bf16[768,128]{1,0:T(8,128)(2,1)}, bf16[16,1536]{1,0:T(8,128)(2...) custom-call(bf16[16,768]{1,0:T(8,128)(2,1)} %get-tuple-element.108.refs_0_, ...), custom_call_target="tpu_custom_call" | custom-call | tf_op jit(solution)/shard_map/encoder_feed/pallas_call | solution.py:46
  49.2 5.0 %copied.1 = (bf16[768,1536]{1,0:T(8,128)(2,1)}, bf16[768,1536]{1,0:T(8,128)(2,1)}) custom-call(bf16[768,1536]{1,0:T(8,128)(2,1)} %refs_0_.4, bf16[768,1536]{1,0:T(8,128)(2,1)} %refs_1_.8, bf16[16,768]{1,0:T(8,128)(2,1)} %copy-done.36), custom_call_target="tpu_custom_call" | custom-call | tf_op jit(solution)/shard_map/copied/pallas_call | solution.py:46
  57.1 2.2 collective-permute-start.11
  59.4 3.6 collective-permute-start.12
  64.2 19.4 %decoder_attend.1 = (f32[1024,768]{1,0:T(8,128)}, bf16[1024,768]{1,0:T(8,128)(2,1)}, bf16[1024,384]{1,0:T(8,128)(2,1)}, bf16[1024,384]{1,0:T(8,128)(2,1)}, bf16[...) custom-call(s32[1]{0:T(128)} %bitcast.refs_0_, ...), custom_call_target="tpu_custom_call" | custom-call | tf_op jit(solution)/shard_map/decoder_attend/pallas_call | solution.py:46
  84.8 3.9 %collective-permute-done.10.refs_2_ = bf16[1024,768]{1,0:T(8,128)(2,1)S(1)} collective-permute-done((bf16[1024,768]{1,0:T(8,128)(2,1)}, bf16[1024,768]{1,0:T(8,128)(2,1)S(1)}, u32[]{:S(2)}, u32[]{:S(2)}) %collective-permute-start.10) | collective-permute-done | bytes 1572896 | tf_op jit(solution)/shard_map/ppermute | solution.py:878
  89.8 6.1 %decoder_norm.1 = (f32[1024,768]{1,0:T(8,128)}, f32[1024,1]{1,0:T(8,128)}, bf16[1024,768]{1,0:T(8,128)(2,1)}) custom-call(f32[1024,768]{1,0:T(8,128)} %get-tuple-element.116.refs_0_, bf16[1024,768]{1,0:T(8,128)(2,1)} %get-tuple-element.117.refs_1_, bf16[1024,768]{1,0:T(8,128)(2,1)} %copy-done.18, f32[768]{0:T(1024)} %refs_3_.10, f32[768]{0:T(1024)} %refs_5_.9, ...), custom_call_target="tpu_custom_call" | custom-call | tf_op jit(solution)/shard_map/decoder_norm/pallas_call | solution.py:46
  97.5 10.5 %decoder_hidden.1 = (bf16[1024,1536]{1,0:T(8,128)(2,1)}, bf16[1024,1536]{1,0:T(8,128)(2,1)}) custom-call(bf16[1024,768]{1,0:T(8,128)(2,1)} %get-tuple-element.119.refs_0_.l_ref, bf16[768,1536]{1,0:T(8,128)(2,1)} %broadcast_select_fusion.1.refs_1_, f32[1,1536]{1,0:T(1,128)} %broadcast_in_dim.78.refs_2_), custom_call_target="tpu_custom_call" | custom-call | tf_op jit(solution)/shard_map/decoder_hidden/pallas_call | solution.py:46
  108.1 4.7 %collective-permute-done.12 = bf16[768,1536]{1,0:T(8,128)(2,1)} collective-permute-done((bf16[768,1536]{1,0:T(8,128)(2,1)}, bf16[768,1536]{1,0:T(8,128)(2,1)}, u32[]{:S(2)}, u32[]{:S(2)}) %collective-permute-start.12) | collective-permute-done | bytes 2359328 | tf_op jit(solution)/shard_map/ppermute | solution.py:878
  114.7 2.6 convolution_convert_fusion.1.refs_4_
  117.5 3.4 collective-permute-done.13.refs_5_
  122.1 8.9 %decoder_norm_back.1 = (bf16[1024,768]{1,0:T(8,128)(2,1)}, f32[1024,768]{1,0:T(8,128)}, bf16[1024,768]{1,0:T(8,128)(2,1)}, f32[3,768]{1,0:T(4,128)}) custom-call(s32[1]{0:T(128)} %bitcast.refs_0_, s32[1,8]{1,0:T(1,128)} %refs_1_.13, s32[1,8]{1,0:T(1,128)} %copy-done.45, f32[1024,768]{1,0:T(8,128)} %get-tuple-element.118.refs_3_, ...), custom_call_target="tpu_custom_call" | custom-call | tf_op jit(solution)/shard_map/decoder_norm_back/pallas_call | solution.py:46
  131.0 5.9 %outer_grad.1.refs_3_.refs_0_ = bf16[768,3072]{1,0:T(8,128)(2,1)} custom-call(bf16[1024,768]{1,0:T(8,128)(2,1)} %get-tuple-element.125.l_ref.refs_0_, bf16[1024,1536]{1,0:T(8,128)(2,1)} %get-tuple-element.121.r_ref), custom_call_target="tpu_custom_call" | custom-call | tf_op jit(solution)/shard_map/outer_grad/pallas_call | solution.py:572
  136.9 8.6 %decoder_feed_back.1 = (bf16[1024,1536]{1,0:T(8,128)(2,1)}, f32[1,1536]{1,0:T(1,128)}) custom-call(bf16[1024,768]{1,0:T(8,128)(2,1)} %get-tuple-element.125.l_ref.refs_0_, bf16[768,1536]{1,0:T(8,128)(2,1)} %copy-done.3, bf16[1024,1536]{1,0:T(8,128)(2,1)} %get-tuple-element.126.refs_2_, bf16[768,3072]{1,0:T(8,128)(2,1)} %outer_grad.1.refs_3_.refs_0_), custom_call_target="tpu_custom_call" | custom-call | tf_op jit(solution)/shard_map/decoder_feed_back/pallas_call | solution.py:46
  145.6 5.8 %inner_grad.1.refs_6_ = bf16[768,3072]{1,0:T(8,128)(2,1)} custom-call(bf16[1024,768]{1,0:T(8,128)(2,1)} %get-tuple-element.119.refs_0_.l_ref, bf16[1024,1536]{1,0:T(8,128)(2,1)} %get-tuple-element.127.r_ref, bf16[768,3072]{1,0:T(8,128)(2,1)} %outer_grad.1.refs_3_.refs_0_), custom_call_target="tpu_custom_call", output_to_operand_aliasing={{}: (2, {})} | custom-call | tf_op jit(solution)/shard_map/inner_grad/pallas_call | solution.py:572
  153.1 4.6 %convolution_convert_fusion.refs_1_ = bf16[1024,768]{1,0:T(8,128)(2,1)S(1)} fusion(bf16[1024,1536]{1,0:T(8,128)(2,1)} %get-tuple-element.127.r_ref, bf16[768,1536]{1,0:T(8,128)(2,1)S(1)} %copy-done), kind=kOutput, calls=%fused_computation.5 | convolution fusion | flops 2416705536 | bytes 7077888 | tf_op jit(solution)/shard_map/dot_general | solution.py:24
  157.9 3.0 collective-permute-start.15
  162.4 7.3 %decoder_first_back.1 = (f32[1024,768]{1,0:T(8,128)}, bf16[1024,768]{1,0:T(8,128)(2,1)}, f32[3,768]{1,0:T(4,128)}) custom-call(f32[1024,768]{1,0:T(8,128)} %get-tuple-element.124.refs_0_, bf16[1024,768]{1,0:T(8,128)(2,1)} %copy-done.19, bf16[1024,768]{1,0:T(8,128)(2,1)} %copy-done.21, f32[1024,768]{1,0:T(8,128)} %get-tuple-element.118.refs_3_, ...), custom_call_target="tpu_custom_call" | custom-call | tf_op jit(solution)/shard_map/decoder_first_back/pallas_call | solution.py:46
  169.7 22.2 %decoder_attend_back.1 = (bf16[1024,1152]{1,0:T(8,128)(2,1)}, bf16[1024,768]{1,0:T(8,128)(2,1)}, f32[1,768]{1,0:T(1,128)}) custom-call(s32[1]{0:T(128)} %bitcast.refs_0_, s32[1,8]{1,0:T(1,128)} %refs_1_.13, s32[1,8]{1,0:T(1,128)} %copy-done.45, bf16[1024,768]{1,0:T(8,128)(2,1)} %get-tuple-element.130.refs_3_.refs_2_, ...), custom_call_target="tpu_custom_call" | custom-call | tf_op jit(solution)/shard_map/decoder_attend_back/pallas_call | solution.py:46
  193.3 2.2 collective-permute-done.17.refs_5_
  196.6 5.0 %decoder_end.1 = (bf16[1024,768]{1,0:T(8,128)(2,1)}, f32[16,768]{1,0:T(8,128)}, bf16[1024,1152]{1,0:T(8,128)(2,1)}) custom-call(s32[1]{0:T(128)} %bitcast.refs_0_, s32[1,8]{1,0:T(1,128)} %refs_1_.13, s32[1,8]{1,0:T(1,128)} %copy-done.45, f32[1024,768]{1,0:T(8,128)} %get-tuple-element.129.refs_3_, ...), custom_call_target="tpu_custom_call", output_to_operand_aliasing={{2}: (6, {})} | custom-call | tf_op jit(solution)/shard_map/decoder_end/pallas_call | solution.py:46
  201.6 6.5 %collective-permute-start.18 = (f32[16,768]{1,0:T(8,128)}, f32[16,768]{1,0:T(8,128)S(1)}, u32[]{:S(2)}, u32[]{:S(2)}) collective-permute-start(f32[16,768]{1,0:T(8,128)} %get-tuple-element.137), channel_id=1, source_target_pairs={{1,2},{2,1},{5,6},{6,5},{9,10},{10,9},{13,14},{14,13},{17,18},{18,... | collective-permute-start | bytes 147464 | tf_op jit(solution)/shard_map/ppermute | solution.py:878
  208.1 6.9 %attend_weight_grads.1 = (bf16[768,768]{1,0:T(8,128)(2,1)}, bf16[768,768]{1,0:T(8,128)(2,1)}) custom-call(bf16[1024,768]{1,0:T(8,128)(2,1)} %get-tuple-element.141.refs_0_, bf16[1024,1152]{1,0:T(8,128)(2,1)} %get-tuple-element.142.refs_1_, bf16[1024,768]{1,0:T(8,128)(2,1)} %get-tuple-element.130.refs_3_.refs_2_, bf16[1024,384]{1,0:T(8,128)(2,1)} %get-tuple-element.143.refs_3_), custom_call_target="tpu_custom_call" | custom-call | tf_op jit(solution)/shard_map/attend_weight_grads/pallas_call | solution.py:46
  215.7 4.2 %encoder_feed_back.1 = (f32[16,768]{1,0:T(8,128)}, bf16[16,768]{1,0:T(8,128)(2,1)}, bf16[16,1536]{1,0:T(8,128)(2,1)}, f32[3,768]{1,0:T(4,128)}, f32[1,1536]{1,0:...) custom-call(f32[16,768]{1,0:T(8,128)} %broadcast_select_fusion.7.ref, ...), custom_call_target="tpu_custom_call", output_to_operand_aliasing={{6}: (7, {}), {7}: (8, {})} | custom-call | tf_op jit(solution)/shard_map/encoder_feed_back/pallas_call | solution.py:46
  220.0 2.0 constant_dynamic-slice_fusion.1
  223.1 3.0 collective-permute-done.19.refs_3_
  226.7 5.0 %encoder_attend_back.1 = (f32[16,768]{1,0:T(8,128)}, f32[3,768]{1,0:T(4,128)}, bf16[16,2304]{1,0:T(8,128)(2,1)}, bf16[768,128]{1,0:T(8,128)(2,1)}, f32[1,384]{1,...) custom-call(s32[1,8]{1,0:T(1,128)} %refs_1_.13, ...), custom_call_target="tpu_custom_call" | custom-call | tf_op jit(solution)/shard_map/encoder_attend_back/pallas_call | solution.py:46
  234.1 6.4 %all-to-all-start = ((bf16[16,336,128]{2,1,0:T(8,128)(2,1)}), bf16[16,336,128]{2,1,0:T(8,128)(2,1)S(1)}, u32[]{:S(2)}, u32[]{:S(2)}) async-start(bf16[16,336,128]{2,1,0:T(8,128)(2,1)} %pad_maximum_fusion.1), calls=%async_computation | async-start | bytes 2752512 | tf_op jit(solution)/shard_map/all_to_all | solution.py:1089
  242.7 22.2 %collective-permute-done.23.refs_11_ = bf16[2,1,2,96,768]{4,3,2,1,0:T(8,128)(2,1)} collective-permute-done((bf16[2,1,2,96,768]{4,3,2,1,0:T(8,128)(2,1)}, bf16[2,1,2,96,768]{4,3,2,1,0:T(8,128)(2,1)}, u32[]{:S(2)}, u32[]{:S(2)}) %collective-permute-start.23) | collective-permute-done | bytes 589856 | tf_op jit(solution)/shard_map/ppermute | solution.py:878
  266.4 2.3 collective-permute-start.25
  273.4 10.3 %collective-permute-done.26 = f32[24,768]{1,0:T(8,128)S(1)} collective-permute-done((f32[24,768]{1,0:T(8,128)S(1)}, f32[24,768]{1,0:T(8,128)S(1)}, u32[]{:S(2)}, u32[]{:S(2)}) %collective-permute-start.26) | collective-permute-done | bytes 73760 | tf_op jit(solution)/shard_map/ppermute | solution.py:878
  286.1 4.3 %passages_back.1 = (f32[1024,768]{1,0:T(8,128)}, f32[24,768]{1,0:T(8,128)}, bf16[1024,768]{1,0:T(8,128)(2,1)}, bf16[2,1,1,96,768]{4,3,2,1,0:T(8,128)(2,1)}, bf16[2,1,1,96,768]{4,3,2,1,0:T(8,128)(2,1)}) custom-call(s32[1]{0:T(128)} %bitcast.1.refs_0_, s32[1,8]{1,0:T(1,128)} %refs_1_.13, ...), custom_call_target="tpu_custom_call", output_to_operand_aliasing={{1}: (7, {}), {2}: (8, {}), {3}: (9, {}), {4}: (10, {})} | custom-call | tf_op jit(solution)/shard_map/passages_back/pallas_call | solution.py:46
  290.4 2.1 collective-permute-start.29
  294.2 3.0 collective-permute-start.32
  298.9 2.1 collective-permute-start.30
  302.2 3.2 collective-permute-done.30
  308.3 5.2 %collective-permute-done.33 = bf16[1,1,1,96,768]{4,3,2,1,0:T(8,128)(2,1)S(1)} collective-permute-done((bf16[1,1,1,96,768]{4,3,2,1,0:T(8,128)(2,1)S(1)}, bf16[1,1,1,96,768]{4,3,2,1,0:T(8,128)(2,1)S(1)}, u32[]{:S(2)}, u32[]{:S(2)}) %collective-permute-start.33) | collective-permute-done | bytes 147488 | tf_op jit(solution)/shard_map/ppermute | solution.py:878
  319.0 3.3 select_convert_fusion
  332.7 2.1 convolution_bitcast_fusion.2
  335.9 4.9 %collective-permute-done.34 = bf16[1,48,4608]{2,1,0:T(8,128)(2,1)S(1)} collective-permute-done((bf16[1,48,4608]{2,1,0:T(8,128)(2,1)S(1)}, bf16[1,48,4608]{2,1,0:T(8,128)(2,1)S(1)}, u32[]{:S(2)}, u32[]{:S(2)}) %collective-permute-start.34) | collective-permute-done | bytes 442400 | tf_op jit(solution)/shard_map/ppermute | solution.py:878
  341.0 3.4 collective-permute-start.35
  344.4 2.2 convolution_bitcast_fusion.1
  347.7 2.9 collective-permute-done.35
  (224 shorter events, 74.1 us)
Async XLA Ops:
  8.0 215.1 %all-gather.7.cloned.1.call-start = ((), (), s32[]{:S(2)}) async-start(), calls=%async_computation.4 | async-start | bytes 1253376 | tf_op jit(solution)/shard_map/all_gather | solution.py:1016
  8.1 23.7 %collective-permute-start.6 = (bf16[768,384]{1,0:T(8,128)(2,1)}, bf16[768,384]{1,0:T(8,128)(2,1)S(1)}, u32[]{:S(2)}, u32[]{:S(2)}) collective-permute-start(bf16[768,384]{1,0:T(8,128)(2,1)} %param.56), channel_id=1, source_target_pairs={{1,2},{2,1},{5,6},{6,5},{9,10},{10,9},{13,14},{14,13},{17,18},{18,... | collective-permute-start | bytes 1769480 | tf_op jit(solution)/shard_map/ppermute | solution.py:878
  12.6 20.1 %collective-permute-start.5 = (bf16[768,384]{1,0:T(8,128)(2,1)}, bf16[768,384]{1,0:T(8,128)(2,1)S(1)}, u32[]{:S(2)}, u32[]{:S(2)}) collective-permute-start(bf16[768,384]{1,0:T(8,128)(2,1)} %param.55), channel_id=1, source_target_pairs={{1,2},{2,1},{5,6},{6,5},{9,10},{10,9},{13,14},{14,13},{17,18},{18,... | collective-permute-start | bytes 1769480 | tf_op jit(solution)/shard_map/ppermute | solution.py:878
  16.6 10.8 %collective-permute-start.7 = (f32[2304]{0:T(1024)S(1)}, f32[2304]{0:T(1024)S(1)}, u32[]{:S(2)}, u32[]{:S(2)}) collective-permute-start(f32[2304]{0:T(1024)S(1)} %constant_dynamic-update-slice_fusion), channel_id=1, source_target_pairs={{1,2},{2,1},{5,6},{6,5},{9,10},{10,9},{13,14},{14,13},{17,18},{18,... | collective-permute-start | bytes 27656 | tf_op jit(solution)/shard_map/ppermute | solution.py:878
  20.3 13.4 %collective-permute-start.4 = (bf16[768,384]{1,0:T(8,128)(2,1)}, bf16[768,384]{1,0:T(8,128)(2,1)S(1)}, u32[]{:S(2)}, u32[]{:S(2)}) collective-permute-start(bf16[768,384]{1,0:T(8,128)(2,1)} %param.54), channel_id=1, source_target_pairs={{1,2},{2,1},{5,6},{6,5},{9,10},{10,9},{13,14},{14,13},{17,18},{18,... | collective-permute-start | bytes 1769480 | tf_op jit(solution)/shard_map/ppermute | solution.py:878
  22.2 18.4 %collective-permute-start = (s32[1,8]{1,0:T(1,128)}, s32[1,8]{1,0:T(1,128)S(1)}, u32[]{:S(2)}, u32[]{:S(2)}) collective-permute-start(s32[1,8]{1,0:T(1,128)} %refs_1_.13), channel_id=1, source_target_pairs={{0,2},{1,3},{2,0},{3,1},{4,6},{5,7},{6,4},{7,5},{8,10},{9,11},{10,... | collective-permute-start | bytes 104 | tf_op jit(solution)/shard_map/ppermute | solution.py:878
  27.4 12.3 %collective-permute-start.3 = (bf16[768,384]{1,0:T(8,128)(2,1)S(1)}, bf16[768,384]{1,0:T(8,128)(2,1)S(1)}, u32[]{:S(2)}, u32[]{:S(2)}) collective-permute-start(bf16[768,384]{1,0:T(8,128)(2,1)S(1)} %copy-done.31), channel_id=1, source_target_pairs={{1,2},{2,1},{5,6},{6,5},{9,10},{10,9},{13,14},{14,13},{17,18},{18,... | collective-permute-start | bytes 1769480 | tf_op jit(solution)/shard_map/ppermute | solution.py:878
  31.8 8.9 %collective-permute-start.2 = (bf16[16,768]{1,0:T(8,128)(2,1)}, bf16[16,768]{1,0:T(8,128)(2,1)S(1)}, u32[]{:S(2)}, u32[]{:S(2)}) collective-permute-start(bf16[16,768]{1,0:T(8,128)(2,1)} %get-tuple-element.109.refs_1_), channel_id=1, source_target_pairs={{0,1},{1,0},{2,3},{3,2},{4,5},{5,4},{6,7},{7,6},{8,9},{9,8},{10,11... | collective-permute-start | bytes 73736 | tf_op jit(solution)/shard_map/ppermute | solution.py:878
  47.2 175.9 %all-gather.5.cloned.1.call-start = ((), (), s32[]{:S(2)}) async-start(), calls=%async_computation.3 | async-start | bytes 3342336 | tf_op jit(solution)/shard_map/all_gather | solution.py:1015
  47.2 7.0 %collective-permute-start.1 = (bf16[1024,768]{1,0:T(8,128)(2,1)S(1)}, bf16[1024,768]{1,0:T(8,128)(2,1)S(1)}, u32[]{:S(2)}, u32[]{:S(2)}) collective-permute-start(bf16[1024,768]{1,0:T(8,128)(2,1)S(1)} %copy-done.17), channel_id=1, source_target_pairs={{0,2},{1,3},{2,0},{3,1},{4,6},{5,7},{6,4},{7,5},{8,10},{9,11},{10,... | collective-permute-start | bytes 4718600 | tf_op jit(solution)/shard_map/ppermute | solution.py:878
  47.3 6.9 %collective-permute-start.8 = (bf16[16,768]{1,0:T(8,128)(2,1)}, bf16[16,768]{1,0:T(8,128)(2,1)S(1)}, u32[]{:S(2)}, u32[]{:S(2)}) collective-permute-start(bf16[16,768]{1,0:T(8,128)(2,1)} %get-tuple-element.112.refs_1_), channel_id=1, source_target_pairs={{0,1},{1,0},{2,3},{3,2},{4,5},{5,4},{6,7},{7,6},{8,9},{9,8},{10,11... | collective-permute-start | bytes 73736 | tf_op jit(solution)/shard_map/ppermute | solution.py:878
  57.1 38.8 %collective-permute-start.11 = (bf16[768,1536]{1,0:T(8,128)(2,1)}, bf16[768,1536]{1,0:T(8,128)(2,1)S(1)}, u32[]{:S(2)}, u32[]{:S(2)}) collective-permute-start(bf16[768,1536]{1,0:T(8,128)(2,1)} %get-tuple-element.120), channel_id=1, source_target_pairs={{1,2},{2,1},{5,6},{6,5},{9,10},{10,9},{13,14},{14,13},{17,18},{18,... | collective-permute-start | bytes 7077896 | tf_op jit(solution)/shard_map/ppermute | solution.py:878
  59.3 269.2 %reduce-scatter.2.cloned.1.call-start = ((), (), s32[]{:S(2)}) async-start(), calls=%async_computation.2 | async-start | bytes 5308416 | tf_op jit(solution)/shard_map/reduce_scatter | solution.py:915
  59.3 4.3 %collective-permute-start.9 = (f32[16,768]{1,0:T(8,128)}, f32[16,768]{1,0:T(8,128)S(1)}, u32[]{:S(2)}, u32[]{:S(2)}) collective-permute-start(f32[16,768]{1,0:T(8,128)} %get-tuple-element.115.refs_5_), channel_id=1, source_target_pairs={{0,2},{1,3},{2,0},{3,1},{4,6},{5,7},{6,4},{7,5},{8,10},{9,11},{10,... | collective-permute-start | bytes 147464 | tf_op jit(solution)/shard_map/ppermute | solution.py:878
  59.4 53.4 %collective-permute-start.12 = (bf16[768,1536]{1,0:T(8,128)(2,1)}, bf16[768,1536]{1,0:T(8,128)(2,1)}, u32[]{:S(2)}, u32[]{:S(2)}) collective-permute-start(bf16[768,1536]{1,0:T(8,128)(2,1)} %get-tuple-element.122), channel_id=1, source_target_pairs={{1,2},{2,1},{5,6},{6,5},{9,10},{10,9},{13,14},{14,13},{17,18},{18,... | collective-permute-start | bytes 7077896 | tf_op jit(solution)/shard_map/ppermute | solution.py:878
  64.2 19.4 %copy-start.13 = (bf16[1024,768]{1,0:T(8,128)(2,1)S(1)}, bf16[1024,768]{1,0:T(8,128)(2,1)}, u32[]{:S(2)}) copy-start(bf16[1024,768]{1,0:T(8,128)(2,1)} %refs_11_.2) | copy-start | bytes 4718596
  83.6 5.0 %collective-permute-start.10 = (bf16[1024,768]{1,0:T(8,128)(2,1)}, bf16[1024,768]{1,0:T(8,128)(2,1)S(1)}, u32[]{:S(2)}, u32[]{:S(2)}) collective-permute-start(bf16[1024,768]{1,0:T(8,128)(2,1)} %get-tuple-element.117.refs_1_), channel_id=1, source_target_pairs={{0,2},{1,3},{2,0},{3,1},{4,6},{5,7},{6,4},{7,5},{8,10},{9,11},{10,... | collective-permute-start | bytes 4718600 | tf_op jit(solution)/shard_map/ppermute | solution.py:878
  83.7 33.8 %collective-permute-start.14 = (bf16[1024,768]{1,0:T(8,128)(2,1)S(1)}, bf16[1024,768]{1,0:T(8,128)(2,1)}, u32[]{:S(2)}, u32[]{:S(2)}) collective-permute-start(bf16[1024,768]{1,0:T(8,128)(2,1)S(1)} %copy-done.13), channel_id=1, source_target_pairs={{0,2},{1,3},{2,0},{3,1},{4,6},{5,7},{6,4},{7,5},{8,10},{9,11},{10,... | collective-permute-start | bytes 4718600 | tf_op jit(solution)/shard_map/ppermute | solution.py:878
  97.5 15.3 %copy-start.2 = (bf16[768,1536]{1,0:T(8,128)(2,1)S(1)}, bf16[768,1536]{1,0:T(8,128)(2,1)}, u32[]{:S(2)}) copy-start(bf16[768,1536]{1,0:T(8,128)(2,1)} %get-tuple-element.122) | copy-start | bytes 7077892
  117.4 3.5 collective-permute-start.13
  157.7 3.5 collective-permute-start.16
  157.9 34.1 %collective-permute-start.15 = (bf16[1024,768]{1,0:T(8,128)(2,1)S(1)}, bf16[1024,768]{1,0:T(8,128)(2,1)S(1)}, u32[]{:S(2)}, u32[]{:S(2)}) collective-permute-start(bf16[1024,768]{1,0:T(8,128)(2,1)S(1)} %copy-done.14), channel_id=1, source_target_pairs={{1,2},{2,1},{5,6},{6,5},{9,10},{10,9},{13,14},{14,13},{17,18},{18,... | collective-permute-start | bytes 4718600 | tf_op jit(solution)/shard_map/ppermute | solution.py:878
  191.8 3.6 %collective-permute-start.17 = (bf16[1024,768]{1,0:T(8,128)(2,1)}, bf16[1024,768]{1,0:T(8,128)(2,1)S(1)}, u32[]{:S(2)}, u32[]{:S(2)}) collective-permute-start(bf16[1024,768]{1,0:T(8,128)(2,1)} %get-tuple-element.135.refs_4_), channel_id=1, source_target_pairs={{0,2},{1,3},{2,0},{3,1},{4,6},{5,7},{6,4},{7,5},{8,10},{9,11},{10,... | collective-permute-start | bytes 4718600 | tf_op jit(solution)/shard_map/ppermute | solution.py:878
  201.6 13.5 %collective-permute-start.18 = (f32[16,768]{1,0:T(8,128)}, f32[16,768]{1,0:T(8,128)S(1)}, u32[]{:S(2)}, u32[]{:S(2)}) collective-permute-start(f32[16,768]{1,0:T(8,128)} %get-tuple-element.137), channel_id=1, source_target_pairs={{1,2},{2,1},{5,6},{6,5},{9,10},{10,9},{13,14},{14,13},{17,18},{18,... | collective-permute-start | bytes 147464 | tf_op jit(solution)/shard_map/ppermute | solution.py:878
  222.0 20.7 %collective-permute-start.22 = (bf16[2,2,1,96,768]{4,3,2,1,0:T(8,128)(2,1)}, bf16[2,2,1,96,768]{4,3,2,1,0:T(8,128)(2,1)S(1)}, u32[]{:S(2)}, u32[]{:S(2)}) collective-permute-start(bf16[2,2,1,96,768]{4,3,2,1,0:T(8,128)(2,1)} %constant_dynamic-slice_fusion.1), channel_id=1, source_target_pairs={{0,4},{1,5},{2,6},{3,7},{4,0},{5,1},{6,2},{7,3},{8,12},{9,13},{10,... | collective-permute-start | bytes 1769480 | tf_op jit(solution)/shard_map/ppermute | solution.py:878
  223.1 41.8 %collective-permute-start.23 = (bf16[2,1,2,96,768]{4,3,2,1,0:T(8,128)(2,1)}, bf16[2,1,2,96,768]{4,3,2,1,0:T(8,128)(2,1)}, u32[]{:S(2)}, u32[]{:S(2)}) collective-permute-start(bf16[2,1,2,96,768]{4,3,2,1,0:T(8,128)(2,1)} %constant_dynamic-slice_fusion), channel_id=1, source_target_pairs={{0,8},{1,9},{2,10},{3,11},{4,12},{5,13},{6,14},{7,15},{8,0},{9,1},... | collective-permute-start | bytes 1769480 | tf_op jit(solution)/shard_map/ppermute | solution.py:878
  223.1 3.1 collective-permute-start.19
  234.1 88.2 %all-to-all-start = ((bf16[16,336,128]{2,1,0:T(8,128)(2,1)}), bf16[16,336,128]{2,1,0:T(8,128)(2,1)S(1)}, u32[]{:S(2)}, u32[]{:S(2)}) async-start(bf16[16,336,128]{2,1,0:T(8,128)(2,1)} %pad_maximum_fusion.1), calls=%async_computation | async-start | bytes 2752512 | tf_op jit(solution)/shard_map/all_to_all | solution.py:1089
  241.1 43.1 %collective-permute-start.21 = (bf16[208,768]{1,0:T(8,128)(2,1)S(1)}, bf16[208,768]{1,0:T(8,128)(2,1)}, u32[]{:S(2)}, u32[]{:S(2)}) collective-permute-start(bf16[208,768]{1,0:T(8,128)(2,1)S(1)} %copy-done.32), channel_id=1, source_target_pairs={{0,1},{1,0},{2,3},{3,2},{4,5},{5,4},{6,7},{7,6},{8,9},{9,8},{10,11... | collective-permute-start | bytes 958472 | tf_op jit(solution)/shard_map/ppermute | solution.py:878
  242.7 22.2 %copy-start.9 = (bf16[2,2,1,96,768]{4,3,2,1,0:T(8,128)(2,1)}, bf16[2,2,1,96,768]{4,3,2,1,0:T(8,128)(2,1)S(1)}, u32[]{:S(2)}) copy-start(bf16[2,2,1,96,768]{4,3,2,1,0:T(8,128)(2,1)S(1)} %collective-permute-done.22.refs_10_) | copy-start | bytes 1769476
  266.4 5.3 %collective-permute-start.24 = (f32[24,768]{1,0:T(8,128)}, f32[24,768]{1,0:T(8,128)S(1)}, u32[]{:S(2)}, u32[]{:S(2)}) collective-permute-start(f32[24,768]{1,0:T(8,128)} %get-tuple-element.172), channel_id=1, source_target_pairs={{0,2},{1,3},{2,0},{3,1},{4,6},{5,7},{6,4},{7,5},{8,10},{9,11},{10,... | collective-permute-start | bytes 221192 | tf_op jit(solution)/shard_map/ppermute | solution.py:878
  266.4 5.3 %collective-permute-start.25 = (f32[24,768]{1,0:T(8,128)}, f32[24,768]{1,0:T(8,128)S(1)}, u32[]{:S(2)}, u32[]{:S(2)}) collective-permute-start(f32[24,768]{1,0:T(8,128)} %get-tuple-element.172), channel_id=1, source_target_pairs={{0,1},{1,0},{2,3},{3,2},{4,5},{5,4},{6,7},{7,6},{8,9},{9,8},{10,11... | collective-permute-start | bytes 221192 | tf_op jit(solution)/shard_map/ppermute | solution.py:878
  269.7 14.5 %collective-permute-start.28 = (bf16[2,1,1,96,768]{4,3,2,1,0:T(8,128)(2,1)S(1)}, bf16[2,1,1,96,768]{4,3,2,1,0:T(8,128)(2,1)S(1)}, u32[]{:S(2)}, u32[]{:S(2)}) collective-permute-start(bf16[2,1,1,96,768]{4,3,2,1,0:T(8,128)(2,1)S(1)} %add_convert_fusion.1), channel_id=1, source_target_pairs={{0,4},{1,5},{2,6},{3,7},{4,0},{5,1},{6,2},{7,3},{8,12},{9,13},{10,... | collective-permute-start | bytes 884744 | tf_op jit(solution)/shard_map/ppermute | solution.py:878
  271.7 13.7 %collective-permute-start.27 = (bf16[2,1,1,96,768]{4,3,2,1,0:T(8,128)(2,1)}, bf16[2,1,1,96,768]{4,3,2,1,0:T(8,128)(2,1)S(1)}, u32[]{:S(2)}, u32[]{:S(2)}) collective-permute-start(bf16[2,1,1,96,768]{4,3,2,1,0:T(8,128)(2,1)} %add_convert_fusion.2), channel_id=1, source_target_pairs={{0,8},{1,9},{2,10},{3,11},{4,12},{5,13},{6,14},{7,15},{8,0},{9,1},... | collective-permute-start | bytes 884744 | tf_op jit(solution)/shard_map/ppermute | solution.py:878
  271.8 11.8 %collective-permute-start.26 = (f32[24,768]{1,0:T(8,128)S(1)}, f32[24,768]{1,0:T(8,128)S(1)}, u32[]{:S(2)}, u32[]{:S(2)}) collective-permute-start(f32[24,768]{1,0:T(8,128)S(1)} %select_add_fusion), channel_id=1, source_target_pairs={{0,4},{1,5},{2,6},{3,7},{4,0},{5,1},{6,2},{7,3},{8,12},{9,13},{10,... | collective-permute-start | bytes 221192 | tf_op jit(solution)/shard_map/ppermute | solution.py:878
  273.2 12.2 %copy-start.34 = (bf16[12,1024]{1,0:T(8,128)(2,1)}, bf16[12,1024]{1,0:T(8,128)(2,1)S(1)}, u32[]{:S(2)}) copy-start(bf16[12,1024]{1,0:T(8,128)(2,1)S(1)} %convert_element_type.101.refs_2_) | copy-start | bytes 73732
  273.3 11.0 %collective-permute-start.20 = (bf16[12,1024]{1,0:T(8,128)(2,1)S(1)}, bf16[12,1024]{1,0:T(8,128)(2,1)S(1)}, u32[]{:S(2)}, u32[]{:S(2)}) collective-permute-start(bf16[12,1024]{1,0:T(8,128)(2,1)S(1)} %convert_element_type.101.refs_2_), channel_id=1, source_target_pairs={{0,1},{1,0},{2,3},{3,2},{4,5},{5,4},{6,7},{7,6},{8,9},{9,8},{10,11... | collective-permute-start | bytes 73736 | tf_op jit(solution)/shard_map/ppermute | solution.py:878
  273.3 19.2 %copy-start.10 = (bf16[2,2,1,96,768]{4,3,2,1,0:T(8,128)(2,1)S(1)}, bf16[2,2,1,96,768]{4,3,2,1,0:T(8,128)(2,1)}, u32[]{:S(2)}) copy-start(bf16[2,2,1,96,768]{4,3,2,1,0:T(8,128)(2,1)} %get-tuple-element.174) | copy-start | bytes 1769476
  290.4 28.6 %collective-permute-start.29 = (bf16[1024,768]{1,0:T(8,128)(2,1)}, bf16[1024,768]{1,0:T(8,128)(2,1)}, u32[]{:S(2)}, u32[]{:S(2)}) collective-permute-start(bf16[1024,768]{1,0:T(8,128)(2,1)} %get-tuple-element.177), channel_id=1, source_target_pairs={{1,2},{2,1},{5,6},{6,5},{9,10},{10,9},{13,14},{14,13},{17,18},{18,... | collective-permute-start | bytes 4718600 | tf_op jit(solution)/shard_map/ppermute | solution.py:878
  294.2 12.2 %collective-permute-start.32 = (bf16[1,1,1,96,768]{4,3,2,1,0:T(8,128)(2,1)}, bf16[1,1,1,96,768]{4,3,2,1,0:T(8,128)(2,1)}, u32[]{:S(2)}, u32[]{:S(2)}) collective-permute-start(bf16[1,1,1,96,768]{4,3,2,1,0:T(8,128)(2,1)} %add_convert_fusion.4), channel_id=1, source_target_pairs={{0,16},{1,17},{2,18},{3,19},{4,20},{5,21},{6,22},{7,23},{8,24},{9,... | collective-permute-start | bytes 442376 | tf_op jit(solution)/shard_map/ppermute | solution.py:878
  297.3 16.2 %copy-start.25 = (bf16[2,1,1,96,768]{4,3,2,1,0:T(8,128)(2,1)S(1)}, bf16[2,1,1,96,768]{4,3,2,1,0:T(8,128)(2,1)}, u32[]{:S(2)}) copy-start(bf16[2,1,1,96,768]{4,3,2,1,0:T(8,128)(2,1)} %get-tuple-element.182) | copy-start | bytes 884740
  298.9 20.1 %copy-start.4 = (bf16[1024,768]{1,0:T(8,128)(2,1)S(1)}, bf16[1024,768]{1,0:T(8,128)(2,1)}, u32[]{:S(2)}) copy-start(bf16[1024,768]{1,0:T(8,128)(2,1)} %get-tuple-element.177) | copy-start | bytes 4718596
  298.9 6.5 %collective-permute-start.30 = (f32[24,768]{1,0:T(8,128)}, f32[24,768]{1,0:T(8,128)S(1)}, u32[]{:S(2)}, u32[]{:S(2)}) collective-permute-start(f32[24,768]{1,0:T(8,128)} %get-tuple-element.180), channel_id=1, source_target_pairs={{0,8},{1,9},{2,10},{3,11},{4,12},{5,13},{6,14},{7,15},{8,0},{9,1},... | collective-permute-start | bytes 221192 | tf_op jit(solution)/shard_map/ppermute | solution.py:878
  302.1 11.4 %collective-permute-start.33 = (bf16[1,1,1,96,768]{4,3,2,1,0:T(8,128)(2,1)S(1)}, bf16[1,1,1,96,768]{4,3,2,1,0:T(8,128)(2,1)S(1)}, u32[]{:S(2)}, u32[]{:S(2)}) collective-permute-start(bf16[1,1,1,96,768]{4,3,2,1,0:T(8,128)(2,1)S(1)} %add_convert_fusion.3), channel_id=1, source_target_pairs={{0,16},{1,17},{2,18},{3,19},{4,20},{5,21},{6,22},{7,23},{8,24},{9,... | collective-permute-start | bytes 442376 | tf_op jit(solution)/shard_map/ppermute | solution.py:878
  306.3 8.9 %collective-permute-start.31 = (f32[24,768]{1,0:T(8,128)S(1)}, f32[24,768]{1,0:T(8,128)S(1)}, u32[]{:S(2)}, u32[]{:S(2)}) collective-permute-start(f32[24,768]{1,0:T(8,128)S(1)} %add.124), channel_id=1, source_target_pairs={{0,16},{1,17},{2,18},{3,19},{4,20},{5,21},{6,22},{7,23},{8,24},{9,... | collective-permute-start | bytes 221192 | tf_op jit(solution)/shard_map/ppermute | solution.py:878
  315.3 2.5 collective-permute-start.36
  329.8 11.0 %collective-permute-start.34 = (bf16[1,48,4608]{2,1,0:T(8,128)(2,1)S(1)}, bf16[1,48,4608]{2,1,0:T(8,128)(2,1)S(1)}, u32[]{:S(2)}, u32[]{:S(2)}) collective-permute-start(bf16[1,48,4608]{2,1,0:T(8,128)(2,1)S(1)} %dynamic-slice_convert_fusion), channel_id=1, source_target_pairs={{0,1},{1,0},{2,3},{3,2},{4,5},{5,4},{6,7},{7,6},{8,9},{9,8},{10,11... | collective-permute-start | bytes 1327112 | tf_op jit(solution)/shard_map/ppermute | solution.py:878
  341.0 9.6 %collective-permute-start.35 = (bf16[48,4608]{1,0:T(8,128)(2,1)S(1)}, bf16[48,4608]{1,0:T(8,128)(2,1)S(1)}, u32[]{:S(2)}, u32[]{:S(2)}) collective-permute-start(bf16[48,4608]{1,0:T(8,128)(2,1)S(1)} %fusion.3), channel_id=1, source_target_pairs={{1,2},{2,1},{5,6},{6,5},{9,10},{10,9},{13,14},{14,13},{17,18},{18,... | collective-permute-start | bytes 1327112 | tf_op jit(solution)/shard_map/ppermute | solution.py:878
  (42 other events, 143.4 us)
Sparse Core Ops, SparseCore 0:
  47.3 41.7 all-gather.6
  92.0 44.5 all-gather.4
Sparse Core Ops, SparseCore 1:
  151.5 112.4 reduce-scatter.1
where the time goes:
time: 365 us; the launch traced here: 360 us
  Pallas kernels  138 us (38%)
  waiting for transfers between devices  72.6 us (20%)
  starting transfers between devices  57.7 us (16%)
  other arithmetic  29.3 us (8%)
  local copies, waits for them, and re-layouts  28.2 us (8%)
  matrix products  17.6 us (5%)
  between operations  16.5 us (5%)
    pallas_call x17, Pallas kernels, call(): pl.pallas_call(body, out_shape=outs + [jax.ShapeDtypeStruct(view.shape, v...  126 us
    ppermute x37, waiting for transfers between devices, move(): return lax.ppermute(value, AXES, pairs)  72.5 us
    ppermute x37, starting transfers between devices, move(): return lax.ppermute(value, AXES, pairs)  51.2 us
    unnamed x100, local copies, waits for them, and re-layouts  12.4 us
    pallas_call x2, Pallas kernels, weight_grads(): pl.pallas_call(kernel, out_shape=jax.ShapeDtypeStruct((model, 2 * width),...  11.8 us
    dot_general x6, matrix products, product(): lax.dot_general(left, right, (((0, 2), (0, 1)), ((), ())), preferred_elem...  10.3 us
    select_n x9, other arithmetic, turn(): return jnp.where(self.home, value, moved)  9.72 us
  transfers between devices with their start and end apart: 41, of which 14 were waited for; matrix products, arithmetic and copies ran while one was open for 17% of the time, Pallas kernels for 37%

commit v1 on v0

--- a/solution.py
+++ b/solution.py
@@ -559,7 +559,7 @@
     )
 
 
-def weight_grads(name, left, right, base):
+def weight_grads(name, left, right, base, after=()):
     rows, model = left.shape
     width = right.shape[1]
     block = WIDE
@@ -574,13 +574,13 @@
         out_shape=jax.ShapeDtypeStruct((model, 2 * width), LOW),
         grid=(steps,),
         in_specs=[pl.BlockSpec((rows, model), lambda i: (0, 0)), pl.BlockSpec((rows, block), lambda i: (0, i))]
-        + [pl.BlockSpec(memory_space=pl.ANY)] * (base is not None),
+        + [pl.BlockSpec(memory_space=pl.ANY)] * ((base is not None) + len(after)),
         out_specs=pl.BlockSpec((model, block), lambda i: (0, i + first)),
         input_output_aliases={} if base is None else {2: 0},
         compiler_params=pltpu.CompilerParams(vmem_limit_bytes=VMEM_LIMIT),
         cost_estimate=pl.CostEstimate(flops=0, bytes_accessed=0, transcendentals=0),
         name=name,
-    )(left, right, *([] if base is None else [base]))
+    )(left, right, *([] if base is None else [base]), *after)
 
 
 def decoder_norm_back(home, own, far_lengths, unit1, share, far, first_gain, first_shift, outer_bias, gain, shift, cot, cot_far, after):
@@ -899,7 +899,7 @@
     def last_halving(self, value):
         view = value.reshape(2, -1, value.shape[1])
         sent = self.swap_tensor(self.pick(view, 0, 1 - self.chip).astype(LOW))
-        return self.turn((self.pick(view, 0, self.chip).astype(F32) + sent.astype(F32))[0].astype(LOW)).astype(F32)
+        return (self.pick(view, 0, self.chip).astype(F32) + sent.astype(F32))[0]
 
     def copies(self, value, lanes):
         rows = value.shape[0]
@@ -938,7 +938,7 @@
     def __init__(self, links, grad, order):
         self.links, self.order = links, list(order)
         self.width = grad.shape[1]
-        self.parts = [(grad.reshape((2,) * links.bits + (-1, self.width)), {})]
+        self.parts = [(grad.reshape((2,) * links.bits + (2, -1, self.width)), {})]
 
     @property
     def held(self):
@@ -959,8 +959,12 @@
 
     def step(self):
         links, step = self.links, self.order.pop(0)
-        axis, mine = links.bits - 1 - step, (links.group >> step) & 1
-        sent = links.swap_group(self.cut(axis, 1 - mine).astype(LOW), step)
+        if step < 0:
+            axis, mine, swap = links.bits, links.chip, links.swap_tensor
+        else:
+            axis, mine = links.bits - 1 - step, (links.group >> step) & 1
+            swap = lambda value: links.swap_group(value, step)
+        sent = swap(self.cut(axis, 1 - mine).astype(LOW))
         self.parts = [(view, {**own, axis: mine}) for view, own in self.parts] + [(sent, {})]
 
     def left(self):
@@ -998,6 +1002,7 @@
         lengths, passages, e_query, e_key, e_value, e_project, e_query_bias, e_value_bias
     )
     kept = x_low.shape[0]
+    inner_held, outer_held = [Held(weight) for weight in copied([d_inner, d_outer], (share,))]
     share_far = links.swap_tensor(share)
     d_value = links.turn(d_value)
     d_project = links.turn(d_project)
@@ -1006,7 +1011,6 @@
         x_low, share, share_far, e_project_bias, e_first_gain, e_first_shift, e_inner, e_inner_bias,
         e_outer, weight_x, (d_query, d_key, d_value, d_project, d_halves, lengths_far),
     )
-    inner_held, outer_held = [Held(weight) for weight in copied([d_inner, d_outer], (share_far,))]
     e_unit2, e_scale2, encoded = encoder_end(
         e_first, share, links.swap_tensor(share), e_outer_bias, e_second_gain, e_second_shift,
         (corrupted_far, inner_held, outer_held),
@@ -1056,8 +1060,8 @@
     attend_grads = attend_weight_grads(d_low, attend_held.held, attended_low, mixed, ())
     across = list(range(links.bits))
     pairs = [
-        Halving(links, attend_grads[0], across),
-        Halving(links, attend_grads[1], across[1:2] + across[:1] + across[2:]),
+        Halving(links, attend_grads[0], [-1] + across),
+        Halving(links, attend_grads[1], [-1] + across[1:2] + across[:1] + across[2:]),
     ]
     corrupted_low = Held(corrupted_low)
 
@@ -1065,18 +1069,16 @@
         totals, e_unit2, e_scale2, e_second_gain, e_outer, e_slope, e_inner, (*pairs,)
     )
     share_far = links.swap_tensor(share)
-    for pair in pairs:
-        pair.step()
     (
         e_first_grad, e_first_sums, right_back, left_back, e_query_sum, e_value_sum, coefs, carried,
     ) = encoder_attend_back(
         lengths, e_second_grad, share, share_far, e_unit1, e_scale1, e_first_gain, e_project, e_query,
-        e_key, e_value, e_value_bias, passages, e_weights, q_keys, e_fed_low, e_pre_grad, (left_forward, right_forward),
+        e_key, e_value, e_value_bias, passages, e_weights, q_keys, e_fed_low, e_pre_grad, (left_forward, right_forward, *pairs),
     )
     vectors = pack_vectors([
         (e_query_sum, e_value_sum, e_inner_bias_grad, e_first_sums, e_second_sums),
         (attend_sums[:, :part], attend_sums[:, part:], inner_bias_grad, first_sums, second_sums),
-    ], (*pairs,))
+    ], ())
     mine = jnp.arange(vectors.shape[0])[:, None] < 9
     vectors = Total(links, vectors + jnp.where(mine, links.swap_core(vectors), links.swap_tensor(vectors)))
     for pair in pairs:
@@ -1087,12 +1089,12 @@
     left_back = left_back.reshape(links.dp, deep, -1)
     both = jnp.concatenate([left_back, links.copies(right_back, left_back.shape[2])], axis=1)
     both = lax.all_to_all(both, "dp", 0, 0, tiled=True)
-    vectors.step()
     passages_grad = passages_back(
-        chip, lengths, coefs, coefs_far, carried, carried_far, e_first_grad, (vectors, corrupted_low, *pairs),
+        chip, lengths, coefs, coefs_far, carried, carried_far, e_first_grad, (corrupted_low, vectors),
     )
     corrupted_grad = links.turn(corrupted_low.held).astype(F32)
-    d_grads = links.last_halving(jnp.concatenate([feed_grads.astype(F32)] + [pair.left() for pair in pairs], axis=1))
+    d_grads = jnp.concatenate([links.last_halving(feed_grads)] + [pair.left() for pair in pairs], axis=1)
+    d_grads = links.turn(d_grads.astype(LOW)).astype(F32)
     edges = [0, hidden, 2 * hidden, 2 * hidden + part, 2 * hidden + 2 * part, 2 * hidden + 3 * part, d_grads.shape[1]]
     d_grads = [d_grads[:, low:high] for low, high in zip(edges, edges[1:])]
     d_grads = d_grads[2:] + d_grads[:2]

time: 365 us -> 364 us (level)
  waiting for transfers between devices: 72.6 us -> 48.5 us
  other arithmetic: 29.3 us -> 35.4 us
  Pallas kernels: 138 us -> 144 us
  starting transfers between devices: 57.7 us -> 62.5 us
    ppermute x37 -> x39, waiting for transfers between devices: 72.5 us -> 48.4 us  [move(): return lax.ppermute(value, AXES, pairs)]
    pallas_call x17, Pallas kernels: 126 us -> 132 us  [call(): pl.pallas_call(body, out_shape=outs + [jax.ShapeDtypeStruct(view.shape, v...]
    ppermute x37 -> x39, starting transfers between devices: 51.2 us -> 56.4 us  [move(): return lax.ppermute(value, AXES, pairs)]
    convert_element_type x6 -> x7, other arithmetic: 5.84 us -> 7.64 us  [the longest x6 7.55 us: step(): sent = swap(self.cut(axis, 1 - mine).astype(LOW))]
    unnamed x100 -> x92, local copies, waits for them, and re-layouts: 12.4 us -> 12.2 us
  transfers between devices with their start and end apart: 41 -> 43, of which waited for: 14 -> 14; matrix products, arithmetic and copies ran while one was open for 17% -> 20% of each run, Pallas kernels for 37% -> 39%
where the time goes in v1:
time: 364 us; the launch traced here: 358 us
  Pallas kernels  144 us (40%)
  starting transfers between devices  62.5 us (17%)
  waiting for transfers between devices  48.5 us (13%)
  other arithmetic  35.4 us (10%)
  local copies, waits for them, and re-layouts  31.6 us (9%)
  matrix products  19.6 us (5%)
  between operations  16.3 us (4%)
    pallas_call x17, Pallas kernels, call(): pl.pallas_call(body, out_shape=outs + [jax.ShapeDtypeStruct(view.shape, v...  132 us
    ppermute x39, starting transfers between devices, move(): return lax.ppermute(value, AXES, pairs)  56.4 us
    ppermute x39, waiting for transfers between devices, move(): return lax.ppermute(value, AXES, pairs)  48.4 us
    select_n x9, other arithmetic, turn(): return jnp.where(self.home, value, moved)  12.5 us
    dot_general x6, matrix products, product(): lax.dot_general(left, right, (((0, 2), (0, 1)), ((), ())), preferred_elem...  12.3 us
    unnamed x92, local copies, waits for them, and re-layouts  12.2 us
    pallas_call x2, Pallas kernels, weight_grads(): pl.pallas_call(kernel, out_shape=jax.ShapeDtypeStruct((model, 2 * width),...  11.7 us
    convert_element_type x6, other arithmetic, step(): sent = swap(self.cut(axis, 1 - mine).astype(LOW))  7.55 us
  transfers between devices with their start and end apart: 43, of which 14 were waited for; matrix products, arithmetic and copies ran while one was open for 20% of the time, Pallas kernels for 39%

profile of v1, /device:TPU:1, one launch (start us, length us, event | category | flops | bytes accessed | tf_op | source)
XLA Modules:
  0.0 358.0 jit_solution(1106651374193493180)
XLA Ops:
  8.1 4.5 %collective-permute-start.6 = (bf16[768,384]{1,0:T(8,128)(2,1)}, bf16[768,384]{1,0:T(8,128)(2,1)S(1)}, u32[]{:S(2)}, u32[]{:S(2)}) collective-permute-start(bf16[768,384]{1,0:T(8,128)(2,1)} %param.56), channel_id=1, source_target_pairs={{1,2},{2,1},{5,6},{6,5},{9,10},{10,9},{13,14},{14,13},{17,18},{18,... | collective-permute-start | bytes 1769480 | tf_op jit(solution)/shard_map/ppermute | solution.py:878
  16.6 3.6 %collective-permute-start.7 = (f32[2304]{0:T(1024)S(1)}, f32[2304]{0:T(1024)S(1)}, u32[]{:S(2)}, u32[]{:S(2)}) collective-permute-start(f32[2304]{0:T(1024)S(1)} %constant_dynamic-update-slice_fusion), channel_id=1, source_target_pairs={{1,2},{2,1},{5,6},{6,5},{9,10},{10,9},{13,14},{14,13},{17,18},{18,... | collective-permute-start | bytes 27656 | tf_op jit(solution)/shard_map/ppermute | solution.py:878
  22.3 5.1 %encoder_attend.1 = (bf16[16,768]{1,0:T(8,128)(2,1)}, bf16[16,384]{1,0:T(8,128)(2,1)}, bf16[96,768]{1,0:T(8,128)(2,1)}, f32[96,1024]{1,0:T(8,128)}, bf16[96,768]...) custom-call(s32[1,8]{1,0:T(1,128)} %refs_1_.13, bf16[1024,768]{1,0:T(8,128)(2,1)} %refs_12_.1, ...), custom_call_target="tpu_custom_call" | custom-call | tf_op jit(solution)/shard_map/encoder_attend/pallas_call | solution.py:46
  27.4 3.8 %collective-permute-start.3 = (bf16[768,384]{1,0:T(8,128)(2,1)S(1)}, bf16[768,384]{1,0:T(8,128)(2,1)S(1)}, u32[]{:S(2)}, u32[]{:S(2)}) collective-permute-start(bf16[768,384]{1,0:T(8,128)(2,1)S(1)} %copy-done.26), channel_id=1, source_target_pairs={{1,2},{2,1},{5,6},{6,5},{9,10},{10,9},{13,14},{14,13},{17,18},{18,... | collective-permute-start | bytes 1769480 | tf_op jit(solution)/shard_map/ppermute | solution.py:878
  33.6 2.0 broadcast_select_fusion.5.refs_11_.refs_8_.refs_10_
  35.6 4.1 %collective-permute-done.3 = bf16[768,384]{1,0:T(8,128)(2,1)S(1)} collective-permute-done((bf16[768,384]{1,0:T(8,128)(2,1)S(1)}, bf16[768,384]{1,0:T(8,128)(2,1)S(1)}, u32[]{:S(2)}, u32[]{:S(2)}) %collective-permute-start.3) | collective-permute-done | bytes 589856 | tf_op jit(solution)/shard_map/ppermute | solution.py:878
  41.3 4.4 %encoder_feed.1 = (f32[16,768]{1,0:T(8,128)}, f32[16,1]{1,0:T(8,128)}, f32[16,768]{1,0:T(8,128)}, bf16[768,128]{1,0:T(8,128)(2,1)}, bf16[16,1536]{1,0:T(8,128)(2...) custom-call(bf16[16,768]{1,0:T(8,128)(2,1)} %get-tuple-element.105.refs_0_, ...), custom_call_target="tpu_custom_call" | custom-call | tf_op jit(solution)/shard_map/encoder_feed/pallas_call | solution.py:46
  49.2 5.0 %copied.1 = (bf16[768,1536]{1,0:T(8,128)(2,1)}, bf16[768,1536]{1,0:T(8,128)(2,1)}) custom-call(bf16[768,1536]{1,0:T(8,128)(2,1)} %refs_0_.4, bf16[768,1536]{1,0:T(8,128)(2,1)} %refs_1_.8, bf16[16,768]{1,0:T(8,128)(2,1)} %get-tuple-element.106.refs_1_.refs_2_), custom_call_target="tpu_custom_call" | custom-call | tf_op jit(solution)/shard_map/copied/pallas_call | solution.py:46
  57.0 2.2 collective-permute-start.11
  59.7 3.3 collective-permute-start.12
  64.2 21.4 %decoder_attend.1 = (f32[1024,768]{1,0:T(8,128)}, bf16[1024,768]{1,0:T(8,128)(2,1)}, bf16[1024,384]{1,0:T(8,128)(2,1)}, bf16[1024,384]{1,0:T(8,128)(2,1)}, bf16[...) custom-call(s32[1]{0:T(128)} %bitcast.refs_0_, ...), custom_call_target="tpu_custom_call" | custom-call | tf_op jit(solution)/shard_map/decoder_attend/pallas_call | solution.py:46
  86.7 4.0 %collective-permute-done.10.refs_2_ = bf16[1024,768]{1,0:T(8,128)(2,1)S(1)} collective-permute-done((bf16[1024,768]{1,0:T(8,128)(2,1)}, bf16[1024,768]{1,0:T(8,128)(2,1)S(1)}, u32[]{:S(2)}, u32[]{:S(2)}) %collective-permute-start.10) | collective-permute-done | bytes 1572896 | tf_op jit(solution)/shard_map/ppermute | solution.py:878
  91.9 6.1 %decoder_norm.1 = (f32[1024,768]{1,0:T(8,128)}, f32[1024,1]{1,0:T(8,128)}, bf16[1024,768]{1,0:T(8,128)(2,1)}) custom-call(f32[1024,768]{1,0:T(8,128)} %get-tuple-element.113.refs_0_, bf16[1024,768]{1,0:T(8,128)(2,1)} %get-tuple-element.114.refs_1_, bf16[1024,768]{1,0:T(8,128)(2,1)} %copy-done.16, f32[768]{0:T(1024)} %refs_3_.10, f32[768]{0:T(1024)} %refs_5_.9, ...), custom_call_target="tpu_custom_call" | custom-call | tf_op jit(solution)/shard_map/decoder_norm/pallas_call | solution.py:46
  98.0 3.4 broadcast_select_fusion.1.refs_1_
  101.3 10.5 %decoder_hidden.1 = (bf16[1024,1536]{1,0:T(8,128)(2,1)}, bf16[1024,1536]{1,0:T(8,128)(2,1)}) custom-call(bf16[1024,768]{1,0:T(8,128)(2,1)} %get-tuple-element.116.refs_0_.l_ref, bf16[768,1536]{1,0:T(8,128)(2,1)} %broadcast_select_fusion.1.refs_1_, f32[1,1536]{1,0:T(1,128)} %broadcast_in_dim.78.refs_2_), custom_call_target="tpu_custom_call" | custom-call | tf_op jit(solution)/shard_map/decoder_hidden/pallas_call | solution.py:46
  114.8 2.6 convolution_convert_fusion.1.refs_4_
  117.5 3.4 collective-permute-done.13.refs_5_
  122.1 8.9 %decoder_norm_back.1 = (bf16[1024,768]{1,0:T(8,128)(2,1)}, f32[1024,768]{1,0:T(8,128)}, bf16[1024,768]{1,0:T(8,128)(2,1)}, f32[3,768]{1,0:T(4,128)}) custom-call(s32[1]{0:T(128)} %bitcast.refs_0_, s32[1,8]{1,0:T(1,128)} %refs_1_.13, s32[1,8]{1,0:T(1,128)} %copy-done.41, f32[1024,768]{1,0:T(8,128)} %get-tuple-element.115.refs_3_, ...), custom_call_target="tpu_custom_call" | custom-call | tf_op jit(solution)/shard_map/decoder_norm_back/pallas_call | solution.py:46
  131.0 5.9 %outer_grad.1.refs_3_.refs_0_ = bf16[768,3072]{1,0:T(8,128)(2,1)} custom-call(bf16[1024,768]{1,0:T(8,128)(2,1)} %get-tuple-element.122.l_ref.refs_0_, bf16[1024,1536]{1,0:T(8,128)(2,1)} %get-tuple-element.118.r_ref), custom_call_target="tpu_custom_call" | custom-call | tf_op jit(solution)/shard_map/outer_grad/pallas_call | solution.py:572
  136.9 8.6 %decoder_feed_back.1 = (bf16[1024,1536]{1,0:T(8,128)(2,1)}, f32[1,1536]{1,0:T(1,128)}) custom-call(bf16[1024,768]{1,0:T(8,128)(2,1)} %get-tuple-element.122.l_ref.refs_0_, bf16[768,1536]{1,0:T(8,128)(2,1)} %copy-done.5, bf16[1024,1536]{1,0:T(8,128)(2,1)} %get-tuple-element.123.refs_2_, bf16[768,3072]{1,0:T(8,128)(2,1)} %outer_grad.1.refs_3_.refs_0_), custom_call_target="tpu_custom_call" | custom-call | tf_op jit(solution)/shard_map/decoder_feed_back/pallas_call | solution.py:46
  145.5 5.8 %inner_grad.1.refs_6_ = bf16[768,3072]{1,0:T(8,128)(2,1)} custom-call(bf16[1024,768]{1,0:T(8,128)(2,1)} %get-tuple-element.116.refs_0_.l_ref, bf16[1024,1536]{1,0:T(8,128)(2,1)} %get-tuple-element.124.r_ref, bf16[768,3072]{1,0:T(8,128)(2,1)} %outer_grad.1.refs_3_.refs_0_), custom_call_target="tpu_custom_call", output_to_operand_aliasing={{}: (2, {})} | custom-call | tf_op jit(solution)/shard_map/inner_grad/pallas_call | solution.py:572
  153.0 4.6 %convolution_convert_fusion.refs_1_ = bf16[1024,768]{1,0:T(8,128)(2,1)S(1)} fusion(bf16[1024,1536]{1,0:T(8,128)(2,1)} %get-tuple-element.124.r_ref, bf16[768,1536]{1,0:T(8,128)(2,1)S(1)} %copy-done.2), kind=kOutput, calls=%fused_computation.4 | convolution fusion | flops 2416705536 | bytes 7077888 | tf_op jit(solution)/shard_map/dot_general | solution.py:24
  158.1 2.0 collective-permute-start.15
  162.3 7.3 %decoder_first_back.1 = (f32[1024,768]{1,0:T(8,128)}, bf16[1024,768]{1,0:T(8,128)(2,1)}, f32[3,768]{1,0:T(4,128)}) custom-call(f32[1024,768]{1,0:T(8,128)} %get-tuple-element.121.refs_0_, bf16[1024,768]{1,0:T(8,128)(2,1)} %copy-done.17, bf16[1024,768]{1,0:T(8,128)(2,1)} %copy-done.19, f32[1024,768]{1,0:T(8,128)} %get-tuple-element.115.refs_3_, ...), custom_call_target="tpu_custom_call" | custom-call | tf_op jit(solution)/shard_map/decoder_first_back/pallas_call | solution.py:46
  169.6 26.1 %decoder_attend_back.1 = (bf16[1024,1152]{1,0:T(8,128)(2,1)}, bf16[1024,768]{1,0:T(8,128)(2,1)}, f32[1,768]{1,0:T(1,128)}) custom-call(s32[1]{0:T(128)} %bitcast.refs_0_, s32[1,8]{1,0:T(1,128)} %refs_1_.13, s32[1,8]{1,0:T(1,128)} %copy-done.41, bf16[1024,768]{1,0:T(8,128)(2,1)} %get-tuple-element.127.refs_3_.refs_2_, ...), custom_call_target="tpu_custom_call" | custom-call | tf_op jit(solution)/shard_map/decoder_attend_back/pallas_call | solution.py:46
  197.3 2.0 collective-permute-done.17.refs_5_
  200.5 4.9 %decoder_end.1 = (bf16[1024,768]{1,0:T(8,128)(2,1)}, f32[16,768]{1,0:T(8,128)}, bf16[1024,1152]{1,0:T(8,128)(2,1)}) custom-call(s32[1]{0:T(128)} %bitcast.refs_0_, s32[1,8]{1,0:T(1,128)} %refs_1_.13, s32[1,8]{1,0:T(1,128)} %copy-done.41, f32[1024,768]{1,0:T(8,128)} %get-tuple-element.126.refs_3_, ...), custom_call_target="tpu_custom_call", output_to_operand_aliasing={{2}: (6, {})} | custom-call | tf_op jit(solution)/shard_map/decoder_end/pallas_call | solution.py:46
  205.4 2.2 collective-permute-start.18
  207.6 7.0 %attend_weight_grads.1 = (bf16[768,768]{1,0:T(8,128)(2,1)}, bf16[768,768]{1,0:T(8,128)(2,1)}) custom-call(bf16[1024,768]{1,0:T(8,128)(2,1)} %get-tuple-element.138.refs_0_, bf16[1024,1152]{1,0:T(8,128)(2,1)} %get-tuple-element.139.refs_1_, bf16[1024,768]{1,0:T(8,128)(2,1)} %get-tuple-element.127.refs_3_.refs_2_, bf16[1024,384]{1,0:T(8,128)(2,1)} %get-tuple-element.140.refs_3_), custom_call_target="tpu_custom_call" | custom-call | tf_op jit(solution)/shard_map/attend_weight_grads/pallas_call | solution.py:46
  215.2 4.3 %encoder_feed_back.1 = (f32[16,768]{1,0:T(8,128)}, bf16[16,768]{1,0:T(8,128)(2,1)}, bf16[16,1536]{1,0:T(8,128)(2,1)}, f32[3,768]{1,0:T(4,128)}, f32[1,1536]{1,0:...) custom-call(f32[16,768]{1,0:T(8,128)} %broadcast_select_fusion.7.ref, ...), custom_call_target="tpu_custom_call", output_to_operand_aliasing={{6}: (7, {}), {7}: (8, {})} | custom-call | tf_op jit(solution)/shard_map/encoder_feed_back/pallas_call | solution.py:46
  220.0 2.3 collective-permute-done.19.refs_3_
  222.9 5.3 %encoder_attend_back.1 = (f32[16,768]{1,0:T(8,128)}, f32[3,768]{1,0:T(4,128)}, bf16[16,2304]{1,0:T(8,128)(2,1)}, bf16[768,128]{1,0:T(8,128)(2,1)}, f32[1,384]{1,...) custom-call(s32[1,8]{1,0:T(1,128)} %refs_1_.13, ...), custom_call_target="tpu_custom_call", output_to_operand_aliasing={{8}: (17, {}), {9}: (18, {})} | custom-call | tf_op jit(solution)/shard_map/encoder_attend_back/pallas_call | solution.py:46
  239.2 5.9 %all-to-all-start = ((bf16[16,336,128]{2,1,0:T(8,128)(2,1)}), bf16[16,336,128]{2,1,0:T(8,128)(2,1)}, u32[]{:S(2)}, u32[]{:S(2)}) async-start(bf16[16,336,128]{2,1,0:T(8,128)(2,1)} %pad_maximum_fusion), calls=%async_computation | async-start | bytes 2752512 | tf_op jit(solution)/shard_map/all_to_all | solution.py:1091
  245.8 11.2 %collective-permute-done.20.refs_3_ = bf16[12,1024]{1,0:T(8,128)(2,1)S(1)} collective-permute-done((bf16[12,1024]{1,0:T(8,128)(2,1)S(1)}, bf16[12,1024]{1,0:T(8,128)(2,1)S(1)}, u32[]{:S(2)}, u32[]{:S(2)}) %collective-permute-start.20) | collective-permute-done | bytes 24608 | tf_op jit(solution)/shard_map/ppermute | solution.py:878
  257.8 4.3 %passages_back.1 = (f32[1024,768]{1,0:T(8,128)}, bf16[1024,768]{1,0:T(8,128)(2,1)}, f32[24,768]{1,0:T(8,128)}) custom-call(s32[1]{0:T(128)} %bitcast.1.refs_0_, s32[1,8]{1,0:T(1,128)} %refs_1_.13, bf16[12,1024]{1,0:T(8,128)(2,1)} %copy-done.33, bf16[12,1024]{1,0:T(8,128)(2,1)} %copy-done.37, ...), custom_call_target="tpu_custom_call", output_to_operand_aliasing={{1}: (7, {}), {2}: (8, {})} | custom-call | tf_op jit(solution)/shard_map/passages_back/pallas_call | solution.py:46
  263.3 3.4 collective-permute-done.25
  268.3 6.2 %collective-permute-done.26 = f32[24,768]{1,0:T(8,128)S(1)} collective-permute-done((f32[24,768]{1,0:T(8,128)S(1)}, f32[24,768]{1,0:T(8,128)S(1)}, u32[]{:S(2)}, u32[]{:S(2)}) %collective-permute-start.26) | collective-permute-done | bytes 73760 | tf_op jit(solution)/shard_map/ppermute | solution.py:878
  276.8 4.1 %collective-permute-start.24 = (bf16[1024,768]{1,0:T(8,128)(2,1)}, bf16[1024,768]{1,0:T(8,128)(2,1)}, u32[]{:S(2)}, u32[]{:S(2)}) collective-permute-start(bf16[1024,768]{1,0:T(8,128)(2,1)} %get-tuple-element.171), channel_id=1, source_target_pairs={{1,2},{2,1},{5,6},{6,5},{9,10},{10,9},{13,14},{14,13},{17,18},{18,... | collective-permute-start | bytes 4718600 | tf_op jit(solution)/shard_map/ppermute | solution.py:878
  282.5 2.3 collective-permute-start.38
  293.7 4.9 %collective-permute-done.30 = bf16[2,2,1,1,48,768]{5,4,3,2,1,0:T(8,128)(2,1)S(1)} collective-permute-done((bf16[2,2,1,1,48,768]{5,4,3,2,1,0:T(8,128)(2,1)S(1)}, bf16[2,2,1,1,48,768]{5,4,3,2,1,0:T(8,128)(2,1)S(1)}, u32[]{:S(2)}, u32[]{:S(2)}) %collective-permute-start.30) | collective-permute-done | bytes 294944 | tf_op jit(solution)/shard_map/ppermute | solution.py:878
  307.1 2.6 collective-permute-start.32
  316.6 3.3 select_convert_fusion
  327.1 2.1 convolution_bitcast_fusion.2
  332.4 2.2 convolution_bitcast_fusion
  334.6 2.2 collective-permute-done.28
  337.0 5.8 %collective-permute-start.37 = (bf16[48,4608]{1,0:T(8,128)(2,1)S(1)}, bf16[48,4608]{1,0:T(8,128)(2,1)S(1)}, u32[]{:S(2)}, u32[]{:S(2)}) collective-permute-start(bf16[48,4608]{1,0:T(8,128)(2,1)S(1)} %pad_maximum_fusion.1), channel_id=1, source_target_pairs={{1,2},{2,1},{5,6},{6,5},{9,10},{10,9},{13,14},{14,13},{17,18},{18,... | collective-permute-start | bytes 1327112 | tf_op jit(solution)/shard_map/ppermute | solution.py:878
  342.8 2.2 convolution_bitcast_fusion.1
  344.9 2.1 fusion
  (221 shorter events, 90.4 us)
Async XLA Ops:
  8.0 212.0 %all-gather.7.cloned.1.call-start = ((), (), s32[]{:S(2)}) async-start(), calls=%async_computation.4 | async-start | bytes 1253376 | tf_op jit(solution)/shard_map/all_gather | solution.py:1020
  8.1 23.7 %collective-permute-start.6 = (bf16[768,384]{1,0:T(8,128)(2,1)}, bf16[768,384]{1,0:T(8,128)(2,1)S(1)}, u32[]{:S(2)}, u32[]{:S(2)}) collective-permute-start(bf16[768,384]{1,0:T(8,128)(2,1)} %param.56), channel_id=1, source_target_pairs={{1,2},{2,1},{5,6},{6,5},{9,10},{10,9},{13,14},{14,13},{17,18},{18,... | collective-permute-start | bytes 1769480 | tf_op jit(solution)/shard_map/ppermute | solution.py:878
  12.6 20.1 %collective-permute-start.5 = (bf16[768,384]{1,0:T(8,128)(2,1)}, bf16[768,384]{1,0:T(8,128)(2,1)S(1)}, u32[]{:S(2)}, u32[]{:S(2)}) collective-permute-start(bf16[768,384]{1,0:T(8,128)(2,1)} %param.55), channel_id=1, source_target_pairs={{1,2},{2,1},{5,6},{6,5},{9,10},{10,9},{13,14},{14,13},{17,18},{18,... | collective-permute-start | bytes 1769480 | tf_op jit(solution)/shard_map/ppermute | solution.py:878
  16.6 10.8 %collective-permute-start.7 = (f32[2304]{0:T(1024)S(1)}, f32[2304]{0:T(1024)S(1)}, u32[]{:S(2)}, u32[]{:S(2)}) collective-permute-start(f32[2304]{0:T(1024)S(1)} %constant_dynamic-update-slice_fusion), channel_id=1, source_target_pairs={{1,2},{2,1},{5,6},{6,5},{9,10},{10,9},{13,14},{14,13},{17,18},{18,... | collective-permute-start | bytes 27656 | tf_op jit(solution)/shard_map/ppermute | solution.py:878
  20.3 13.4 %collective-permute-start.4 = (bf16[768,384]{1,0:T(8,128)(2,1)}, bf16[768,384]{1,0:T(8,128)(2,1)}, u32[]{:S(2)}, u32[]{:S(2)}) collective-permute-start(bf16[768,384]{1,0:T(8,128)(2,1)} %param.54), channel_id=1, source_target_pairs={{1,2},{2,1},{5,6},{6,5},{9,10},{10,9},{13,14},{14,13},{17,18},{18,... | collective-permute-start | bytes 1769480 | tf_op jit(solution)/shard_map/ppermute | solution.py:878
  22.2 18.4 %collective-permute-start = (s32[1,8]{1,0:T(1,128)}, s32[1,8]{1,0:T(1,128)S(1)}, u32[]{:S(2)}, u32[]{:S(2)}) collective-permute-start(s32[1,8]{1,0:T(1,128)} %refs_1_.13), channel_id=1, source_target_pairs={{0,2},{1,3},{2,0},{3,1},{4,6},{5,7},{6,4},{7,5},{8,10},{9,11},{10,... | collective-permute-start | bytes 104 | tf_op jit(solution)/shard_map/ppermute | solution.py:878
  27.4 12.3 %collective-permute-start.3 = (bf16[768,384]{1,0:T(8,128)(2,1)S(1)}, bf16[768,384]{1,0:T(8,128)(2,1)S(1)}, u32[]{:S(2)}, u32[]{:S(2)}) collective-permute-start(bf16[768,384]{1,0:T(8,128)(2,1)S(1)} %copy-done.26), channel_id=1, source_target_pairs={{1,2},{2,1},{5,6},{6,5},{9,10},{10,9},{13,14},{14,13},{17,18},{18,... | collective-permute-start | bytes 1769480 | tf_op jit(solution)/shard_map/ppermute | solution.py:878
  31.8 8.8 %collective-permute-start.2 = (bf16[16,768]{1,0:T(8,128)(2,1)}, bf16[16,768]{1,0:T(8,128)(2,1)S(1)}, u32[]{:S(2)}, u32[]{:S(2)}) collective-permute-start(bf16[16,768]{1,0:T(8,128)(2,1)} %get-tuple-element.106.refs_1_.refs_2_), channel_id=1, source_target_pairs={{0,1},{1,0},{2,3},{3,2},{4,5},{5,4},{6,7},{7,6},{8,9},{9,8},{10,11... | collective-permute-start | bytes 73736 | tf_op jit(solution)/shard_map/ppermute | solution.py:878
  47.2 172.9 %all-gather.5.cloned.1.call-start = ((), (), s32[]{:S(2)}) async-start(), calls=%async_computation.3 | async-start | bytes 3342336 | tf_op jit(solution)/shard_map/all_gather | solution.py:1019
  47.2 7.0 %collective-permute-start.1 = (bf16[1024,768]{1,0:T(8,128)(2,1)S(1)}, bf16[1024,768]{1,0:T(8,128)(2,1)S(1)}, u32[]{:S(2)}, u32[]{:S(2)}) collective-permute-start(bf16[1024,768]{1,0:T(8,128)(2,1)S(1)} %copy-done.15), channel_id=1, source_target_pairs={{0,2},{1,3},{2,0},{3,1},{4,6},{5,7},{6,4},{7,5},{8,10},{9,11},{10,... | collective-permute-start | bytes 4718600 | tf_op jit(solution)/shard_map/ppermute | solution.py:878
  47.3 6.9 %collective-permute-start.8 = (bf16[16,768]{1,0:T(8,128)(2,1)}, bf16[16,768]{1,0:T(8,128)(2,1)S(1)}, u32[]{:S(2)}, u32[]{:S(2)}) collective-permute-start(bf16[16,768]{1,0:T(8,128)(2,1)} %get-tuple-element.109.refs_1_), channel_id=1, source_target_pairs={{0,1},{1,0},{2,3},{3,2},{4,5},{5,4},{6,7},{7,6},{8,9},{9,8},{10,11... | collective-permute-start | bytes 73736 | tf_op jit(solution)/shard_map/ppermute | solution.py:878
  57.0 40.9 %collective-permute-start.11 = (bf16[768,1536]{1,0:T(8,128)(2,1)}, bf16[768,1536]{1,0:T(8,128)(2,1)}, u32[]{:S(2)}, u32[]{:S(2)}) collective-permute-start(bf16[768,1536]{1,0:T(8,128)(2,1)} %get-tuple-element.117), channel_id=1, source_target_pairs={{1,2},{2,1},{5,6},{6,5},{9,10},{10,9},{13,14},{14,13},{17,18},{18,... | collective-permute-start | bytes 7077896 | tf_op jit(solution)/shard_map/ppermute | solution.py:878
  59.3 270.0 %reduce-scatter.2.cloned.1.call-start = ((), (), s32[]{:S(2)}) async-start(), calls=%async_computation.2 | async-start | bytes 5308416 | tf_op jit(solution)/shard_map/reduce_scatter | solution.py:915
  59.3 4.3 %collective-permute-start.9 = (f32[16,768]{1,0:T(8,128)}, f32[16,768]{1,0:T(8,128)S(1)}, u32[]{:S(2)}, u32[]{:S(2)}) collective-permute-start(f32[16,768]{1,0:T(8,128)} %get-tuple-element.112.refs_5_), channel_id=1, source_target_pairs={{0,2},{1,3},{2,0},{3,1},{4,6},{5,7},{6,4},{7,5},{8,10},{9,11},{10,... | collective-permute-start | bytes 147464 | tf_op jit(solution)/shard_map/ppermute | solution.py:878
  59.7 53.1 %collective-permute-start.12 = (bf16[768,1536]{1,0:T(8,128)(2,1)}, bf16[768,1536]{1,0:T(8,128)(2,1)}, u32[]{:S(2)}, u32[]{:S(2)}) collective-permute-start(bf16[768,1536]{1,0:T(8,128)(2,1)} %get-tuple-element.119), channel_id=1, source_target_pairs={{1,2},{2,1},{5,6},{6,5},{9,10},{10,9},{13,14},{14,13},{17,18},{18,... | collective-permute-start | bytes 7077896 | tf_op jit(solution)/shard_map/ppermute | solution.py:878
  64.2 21.4 %copy-start.11 = (bf16[1024,768]{1,0:T(8,128)(2,1)S(1)}, bf16[1024,768]{1,0:T(8,128)(2,1)}, u32[]{:S(2)}) copy-start(bf16[1024,768]{1,0:T(8,128)(2,1)} %refs_11_.2) | copy-start | bytes 4718596
  85.6 5.1 %collective-permute-start.10 = (bf16[1024,768]{1,0:T(8,128)(2,1)}, bf16[1024,768]{1,0:T(8,128)(2,1)S(1)}, u32[]{:S(2)}, u32[]{:S(2)}) collective-permute-start(bf16[1024,768]{1,0:T(8,128)(2,1)} %get-tuple-element.114.refs_1_), channel_id=1, source_target_pairs={{0,2},{1,3},{2,0},{3,1},{4,6},{5,7},{6,4},{7,5},{8,10},{9,11},{10,... | collective-permute-start | bytes 4718600 | tf_op jit(solution)/shard_map/ppermute | solution.py:878
  85.6 31.9 %collective-permute-start.14 = (bf16[1024,768]{1,0:T(8,128)(2,1)S(1)}, bf16[1024,768]{1,0:T(8,128)(2,1)}, u32[]{:S(2)}, u32[]{:S(2)}) collective-permute-start(bf16[1024,768]{1,0:T(8,128)(2,1)S(1)} %copy-done.11), channel_id=1, source_target_pairs={{0,2},{1,3},{2,0},{3,1},{4,6},{5,7},{6,4},{7,5},{8,10},{9,11},{10,... | collective-permute-start | bytes 4718600 | tf_op jit(solution)/shard_map/ppermute | solution.py:878
  101.3 11.5 %copy-start.4 = (bf16[768,1536]{1,0:T(8,128)(2,1)S(1)}, bf16[768,1536]{1,0:T(8,128)(2,1)}, u32[]{:S(2)}) copy-start(bf16[768,1536]{1,0:T(8,128)(2,1)} %get-tuple-element.119) | copy-start | bytes 7077892
  117.4 3.5 collective-permute-start.13
  157.7 3.5 collective-permute-start.16
  158.1 37.9 %collective-permute-start.15 = (bf16[1024,768]{1,0:T(8,128)(2,1)S(1)}, bf16[1024,768]{1,0:T(8,128)(2,1)S(1)}, u32[]{:S(2)}, u32[]{:S(2)}) collective-permute-start(bf16[1024,768]{1,0:T(8,128)(2,1)S(1)} %copy-done.12), channel_id=1, source_target_pairs={{1,2},{2,1},{5,6},{6,5},{9,10},{10,9},{13,14},{14,13},{17,18},{18,... | collective-permute-start | bytes 4718600 | tf_op jit(solution)/shard_map/ppermute | solution.py:878
  195.7 3.6 %collective-permute-start.17 = (bf16[1024,768]{1,0:T(8,128)(2,1)}, bf16[1024,768]{1,0:T(8,128)(2,1)S(1)}, u32[]{:S(2)}, u32[]{:S(2)}) collective-permute-start(bf16[1024,768]{1,0:T(8,128)(2,1)} %get-tuple-element.132.refs_4_), channel_id=1, source_target_pairs={{0,2},{1,3},{2,0},{3,1},{4,6},{5,7},{6,4},{7,5},{8,10},{9,11},{10,... | collective-permute-start | bytes 4718600 | tf_op jit(solution)/shard_map/ppermute | solution.py:878
  205.4 9.2 %collective-permute-start.18 = (f32[16,768]{1,0:T(8,128)}, f32[16,768]{1,0:T(8,128)S(1)}, u32[]{:S(2)}, u32[]{:S(2)}) collective-permute-start(f32[16,768]{1,0:T(8,128)} %get-tuple-element.134), channel_id=1, source_target_pairs={{1,2},{2,1},{5,6},{6,5},{9,10},{10,9},{13,14},{14,13},{17,18},{18,... | collective-permute-start | bytes 147464 | tf_op jit(solution)/shard_map/ppermute | solution.py:878
  219.5 2.9 collective-permute-start.19
  229.8 15.3 %collective-permute-start.22 = (f32[24,768]{1,0:T(8,128)}, f32[24,768]{1,0:T(8,128)S(1)}, u32[]{:S(2)}, u32[]{:S(2)}) collective-permute-start(f32[24,768]{1,0:T(8,128)} %pack_vectors.1), channel_id=1, source_target_pairs={{0,2},{1,3},{2,0},{3,1},{4,6},{5,7},{6,4},{7,5},{8,10},{9,11},{10,... | collective-permute-start | bytes 221192 | tf_op jit(solution)/shard_map/ppermute | solution.py:878
  230.9 14.2 %collective-permute-start.23 = (f32[24,768]{1,0:T(8,128)}, f32[24,768]{1,0:T(8,128)S(1)}, u32[]{:S(2)}, u32[]{:S(2)}) collective-permute-start(f32[24,768]{1,0:T(8,128)} %pack_vectors.1), channel_id=1, source_target_pairs={{0,1},{1,0},{2,3},{3,2},{4,5},{5,4},{6,7},{7,6},{8,9},{9,8},{10,11... | collective-permute-start | bytes 221192 | tf_op jit(solution)/shard_map/ppermute | solution.py:878
  234.5 54.0 %collective-permute-start.29 = (bf16[2,2,2,1,48,768]{5,4,3,2,1,0:T(8,128)(2,1)}, bf16[2,2,2,1,48,768]{5,4,3,2,1,0:T(8,128)(2,1)}, u32[]{:S(2)}, u32[]{:S(2)}) collective-permute-start(bf16[2,2,2,1,48,768]{5,4,3,2,1,0:T(8,128)(2,1)} %constant_dynamic-slice_fusion.1), channel_id=1, source_target_pairs={{0,1},{1,0},{2,3},{3,2},{4,5},{5,4},{6,7},{7,6},{8,9},{9,8},{10,11... | collective-permute-start | bytes 1769480 | tf_op jit(solution)/shard_map/ppermute | solution.py:878
  234.5 22.5 %collective-permute-start.21 = (bf16[208,768]{1,0:T(8,128)(2,1)}, bf16[208,768]{1,0:T(8,128)(2,1)S(1)}, u32[]{:S(2)}, u32[]{:S(2)}) collective-permute-start(bf16[208,768]{1,0:T(8,128)(2,1)} %get-tuple-element.158.refs_4_), channel_id=1, source_target_pairs={{0,1},{1,0},{2,3},{3,2},{4,5},{5,4},{6,7},{7,6},{8,9},{9,8},{10,11... | collective-permute-start | bytes 958472 | tf_op jit(solution)/shard_map/ppermute | solution.py:878
  236.8 20.2 %collective-permute-start.20 = (bf16[12,1024]{1,0:T(8,128)(2,1)S(1)}, bf16[12,1024]{1,0:T(8,128)(2,1)S(1)}, u32[]{:S(2)}, u32[]{:S(2)}) collective-permute-start(bf16[12,1024]{1,0:T(8,128)(2,1)S(1)} %convert_element_type.131.refs_2_), channel_id=1, source_target_pairs={{0,1},{1,0},{2,3},{3,2},{4,5},{5,4},{6,7},{7,6},{8,9},{9,8},{10,11... | collective-permute-start | bytes 73736 | tf_op jit(solution)/shard_map/ppermute | solution.py:878
  239.2 80.7 %all-to-all-start = ((bf16[16,336,128]{2,1,0:T(8,128)(2,1)}), bf16[16,336,128]{2,1,0:T(8,128)(2,1)}, u32[]{:S(2)}, u32[]{:S(2)}) async-start(bf16[16,336,128]{2,1,0:T(8,128)(2,1)} %pad_maximum_fusion), calls=%async_computation | async-start | bytes 2752512 | tf_op jit(solution)/shard_map/all_to_all | solution.py:1091
  245.1 17.1 %copy-start.1 = (bf16[2,2,2,2,48,768]{5,4,3,2,1,0:T(8,128)(2,1)S(1)}, bf16[2,2,2,2,48,768]{5,4,3,2,1,0:T(8,128)(2,1)}, u32[]{:S(2)}) copy-start(bf16[2,2,2,2,48,768]{5,4,3,2,1,0:T(8,128)(2,1)} %get-tuple-element.176) | copy-start | bytes 3538948
  257.8 18.3 %copy-start.9 = (bf16[256,2304]{1,0:T(8,128)(2,1)S(1)}, bf16[256,2304]{1,0:T(8,128)(2,1)}, u32[]{:S(2)}) copy-start(bf16[256,2304]{1,0:T(8,128)(2,1)} %all-gather.7.cloned.1.call-done) | copy-start | bytes 3538948
  262.1 26.4 %copy-start = (bf16[2,2,2,2,48,768]{5,4,3,2,1,0:T(8,128)(2,1)S(1)}, bf16[2,2,2,2,48,768]{5,4,3,2,1,0:T(8,128)(2,1)}, u32[]{:S(2)}) copy-start(bf16[2,2,2,2,48,768]{5,4,3,2,1,0:T(8,128)(2,1)} %get-tuple-element.175) | copy-start | bytes 3538948
  262.2 4.5 %collective-permute-start.25 = (f32[24,768]{1,0:T(8,128)}, f32[24,768]{1,0:T(8,128)S(1)}, u32[]{:S(2)}, u32[]{:S(2)}) collective-permute-start(f32[24,768]{1,0:T(8,128)} %get-tuple-element.174), channel_id=1, source_target_pairs={{0,4},{1,5},{2,6},{3,7},{4,0},{5,1},{6,2},{7,3},{8,12},{9,13},{10,... | collective-permute-start | bytes 221192 | tf_op jit(solution)/shard_map/ppermute | solution.py:878
  263.0 28.3 %collective-permute-start.33 = (bf16[2,2,2,1,48,768]{5,4,3,2,1,0:T(8,128)(2,1)}, bf16[2,2,2,1,48,768]{5,4,3,2,1,0:T(8,128)(2,1)}, u32[]{:S(2)}, u32[]{:S(2)}) collective-permute-start(bf16[2,2,2,1,48,768]{5,4,3,2,1,0:T(8,128)(2,1)} %constant_dynamic-slice_fusion), channel_id=1, source_target_pairs={{0,1},{1,0},{2,3},{3,2},{4,5},{5,4},{6,7},{7,6},{8,9},{9,8},{10,11... | collective-permute-start | bytes 1769480 | tf_op jit(solution)/shard_map/ppermute | solution.py:878
  267.6 6.9 %collective-permute-start.26 = (f32[24,768]{1,0:T(8,128)S(1)}, f32[24,768]{1,0:T(8,128)S(1)}, u32[]{:S(2)}, u32[]{:S(2)}) collective-permute-start(f32[24,768]{1,0:T(8,128)S(1)} %add.81), channel_id=1, source_target_pairs={{0,8},{1,9},{2,10},{3,11},{4,12},{5,13},{6,14},{7,15},{8,0},{9,1},... | collective-permute-start | bytes 221192 | tf_op jit(solution)/shard_map/ppermute | solution.py:878
  275.1 5.8 %collective-permute-start.27 = (f32[24,768]{1,0:T(8,128)}, f32[24,768]{1,0:T(8,128)}, u32[]{:S(2)}, u32[]{:S(2)}) collective-permute-start(f32[24,768]{1,0:T(8,128)} %add.82), channel_id=1, source_target_pairs={{0,16},{1,17},{2,18},{3,19},{4,20},{5,21},{6,22},{7,23},{8,24},{9,... | collective-permute-start | bytes 221192 | tf_op jit(solution)/shard_map/ppermute | solution.py:878
  276.8 39.7 %collective-permute-start.24 = (bf16[1024,768]{1,0:T(8,128)(2,1)}, bf16[1024,768]{1,0:T(8,128)(2,1)}, u32[]{:S(2)}, u32[]{:S(2)}) collective-permute-start(bf16[1024,768]{1,0:T(8,128)(2,1)} %get-tuple-element.171), channel_id=1, source_target_pairs={{1,2},{2,1},{5,6},{6,5},{9,10},{10,9},{13,14},{14,13},{17,18},{18,... | collective-permute-start | bytes 4718600 | tf_op jit(solution)/shard_map/ppermute | solution.py:878
  282.5 10.4 %collective-permute-start.38 = (f32[3,768]{1,0:T(4,128)}, f32[3,768]{1,0:T(4,128)}, u32[]{:S(2)}, u32[]{:S(2)}) collective-permute-start(f32[3,768]{1,0:T(4,128)} %slice.222), channel_id=1, source_target_pairs={{0,2},{1,3},{2,0},{3,1},{4,6},{5,7},{6,4},{7,5},{8,10},{9,11},{10,... | collective-permute-start | bytes 27656 | tf_op jit(solution)/shard_map/ppermute | solution.py:878
  289.6 9.0 %collective-permute-start.30 = (bf16[2,2,1,1,48,768]{5,4,3,2,1,0:T(8,128)(2,1)S(1)}, bf16[2,2,1,1,48,768]{5,4,3,2,1,0:T(8,128)(2,1)S(1)}, u32[]{:S(2)}, u32[]{:S(2)}) collective-permute-start(bf16[2,2,1,1,48,768]{5,4,3,2,1,0:T(8,128)(2,1)S(1)} %add_convert_fusion.1), channel_id=1, source_target_pairs={{0,4},{1,5},{2,6},{3,7},{4,0},{5,1},{6,2},{7,3},{8,12},{9,13},{10,... | collective-permute-start | bytes 884744 | tf_op jit(solution)/shard_map/ppermute | solution.py:878
  292.4 9.8 %collective-permute-start.34 = (bf16[2,1,2,1,48,768]{5,4,3,2,1,0:T(8,128)(2,1)S(1)}, bf16[2,1,2,1,48,768]{5,4,3,2,1,0:T(8,128)(2,1)S(1)}, u32[]{:S(2)}, u32[]{:S(2)}) collective-permute-start(bf16[2,1,2,1,48,768]{5,4,3,2,1,0:T(8,128)(2,1)S(1)} %add_convert_fusion), channel_id=1, source_target_pairs={{0,8},{1,9},{2,10},{3,11},{4,12},{5,13},{6,14},{7,15},{8,0},{9,1},... | collective-permute-start | bytes 884744 | tf_op jit(solution)/shard_map/ppermute | solution.py:878
  300.4 5.6 %collective-permute-start.31 = (bf16[2,1,1,1,48,768]{5,4,3,2,1,0:T(8,128)(2,1)}, bf16[2,1,1,1,48,768]{5,4,3,2,1,0:T(8,128)(2,1)}, u32[]{:S(2)}, u32[]{:S(2)}) collective-permute-start(bf16[2,1,1,1,48,768]{5,4,3,2,1,0:T(8,128)(2,1)} %add_convert_fusion.4), channel_id=1, source_target_pairs={{0,8},{1,9},{2,10},{3,11},{4,12},{5,13},{6,14},{7,15},{8,0},{9,1},... | collective-permute-start | bytes 442376 | tf_op jit(solution)/shard_map/ppermute | solution.py:878
  304.6 5.2 %collective-permute-start.35 = (bf16[2,1,1,1,48,768]{5,4,3,2,1,0:T(8,128)(2,1)}, bf16[2,1,1,1,48,768]{5,4,3,2,1,0:T(8,128)(2,1)}, u32[]{:S(2)}, u32[]{:S(2)}) collective-permute-start(bf16[2,1,1,1,48,768]{5,4,3,2,1,0:T(8,128)(2,1)} %add_convert_fusion.3), channel_id=1, source_target_pairs={{0,4},{1,5},{2,6},{3,7},{4,0},{5,1},{6,2},{7,3},{8,12},{9,13},{10,... | collective-permute-start | bytes 442376 | tf_op jit(solution)/shard_map/ppermute | solution.py:878
  307.1 5.4 %collective-permute-start.32 = (bf16[1,1,1,1,48,768]{5,4,3,2,1,0:T(8,128)(2,1)S(1)}, bf16[1,1,1,1,48,768]{5,4,3,2,1,0:T(8,128)(2,1)S(1)}, u32[]{:S(2)}, u32[]{:S(2)}) collective-permute-start(bf16[1,1,1,1,48,768]{5,4,3,2,1,0:T(8,128)(2,1)S(1)} %add_convert_fusion.8), channel_id=1, source_target_pairs={{0,16},{1,17},{2,18},{3,19},{4,20},{5,21},{6,22},{7,23},{8,24},{9,... | collective-permute-start | bytes 221192 | tf_op jit(solution)/shard_map/ppermute | solution.py:878
  310.7 4.2 %collective-permute-start.36 = (bf16[1,1,1,1,48,768]{5,4,3,2,1,0:T(8,128)(2,1)S(1)}, bf16[1,1,1,1,48,768]{5,4,3,2,1,0:T(8,128)(2,1)S(1)}, u32[]{:S(2)}, u32[]{:S(2)}) collective-permute-start(bf16[1,1,1,1,48,768]{5,4,3,2,1,0:T(8,128)(2,1)S(1)} %add_convert_fusion.6), channel_id=1, source_target_pairs={{0,16},{1,17},{2,18},{3,19},{4,20},{5,21},{6,22},{7,23},{8,24},{9,... | collective-permute-start | bytes 221192 | tf_op jit(solution)/shard_map/ppermute | solution.py:878
  330.3 6.6 %collective-permute-start.28 = (bf16[1,48,3072]{2,1,0:T(8,128)(2,1)S(1)}, bf16[1,48,3072]{2,1,0:T(8,128)(2,1)S(1)}, u32[]{:S(2)}, u32[]{:S(2)}) collective-permute-start(bf16[1,48,3072]{2,1,0:T(8,128)(2,1)S(1)} %constant_dynamic-slice_fusion.2), channel_id=1, source_target_pairs={{0,1},{1,0},{2,3},{3,2},{4,5},{5,4},{6,7},{7,6},{8,9},{9,8},{10,11... | collective-permute-start | bytes 884744 | tf_op jit(solution)/shard_map/ppermute | solution.py:878
  337.0 11.7 %collective-permute-start.37 = (bf16[48,4608]{1,0:T(8,128)(2,1)S(1)}, bf16[48,4608]{1,0:T(8,128)(2,1)S(1)}, u32[]{:S(2)}, u32[]{:S(2)}) collective-permute-start(bf16[48,4608]{1,0:T(8,128)(2,1)S(1)} %pad_maximum_fusion.1), channel_id=1, source_target_pairs={{1,2},{2,1},{5,6},{6,5},{9,10},{10,9},{13,14},{14,13},{17,18},{18,... | collective-permute-start | bytes 1327112 | tf_op jit(solution)/shard_map/ppermute | solution.py:878
  (40 other events, 153.9 us)
Sparse Core Ops, SparseCore 0:
  47.3 41.3 all-gather.6
  91.5 45.4 all-gather.4
Sparse Core Ops, SparseCore 1:
  151.5 94.8 reduce-scatter.1

commit v2 on v1

--- a/solution.py
+++ b/solution.py
@@ -544,7 +544,7 @@
             act_ref[here, :] = act.astype(LOW)
             slope_ref[here, :] = slope.astype(LOW)
 
-        over_rows(rows, 64, activate)
+        over_rows(rows, 128, activate)
 
     return call(
         kernel,

time: 364 us -> 364 us (level)
  starting transfers between devices: 62.5 us -> 69.5 us
  Pallas kernels: 144 us -> 138 us
    pallas_call x17, Pallas kernels: 132 us -> 126 us  [call(): pl.pallas_call(body, out_shape=outs + [jax.ShapeDtypeStruct(view.shape, v...]
    all_to_all x1, starting transfers between devices: 5.93 us -> 10.4 us  [local(): both = lax.all_to_all(both, 'dp', 0, 0, tiled=True)]
  transfers between devices with their start and end apart: 43 -> 43, of which waited for: 14 -> 14; matrix products, arithmetic and copies ran while one was open for 20% -> 20% of each run, Pallas kernels for 39% -> 37%
where the time goes in v2:
time: 364 us; the launch traced here: 359 us
  Pallas kernels  138 us (38%)
  starting transfers between devices  69.5 us (19%)
  waiting for transfers between devices  48.4 us (13%)
  other arithmetic  35.3 us (10%)
  local copies, waits for them, and re-layouts  31.6 us (9%)
  matrix products  19.6 us (5%)
  between operations  16.4 us (5%)
    pallas_call x17, Pallas kernels, call(): pl.pallas_call(body, out_shape=outs + [jax.ShapeDtypeStruct(view.shape, v...  126 us
    ppermute x39, starting transfers between devices, move(): return lax.ppermute(value, AXES, pairs)  59 us
    ppermute x39, waiting for transfers between devices, move(): return lax.ppermute(value, AXES, pairs)  48.4 us
    select_n x9, other arithmetic, turn(): return jnp.where(self.home, value, moved)  12.4 us
    dot_general x6, matrix products, product(): lax.dot_general(left, right, (((0, 2), (0, 1)), ((), ())), preferred_elem...  12.3 us
    unnamed x92, local copies, waits for them, and re-layouts  12.2 us
    pallas_call x2, Pallas kernels, weight_grads(): pl.pallas_call(kernel, out_shape=jax.ShapeDtypeStruct((model, 2 * width),...  11.8 us
    all_to_all x1, starting transfers between devices, local(): both = lax.all_to_all(both, 'dp', 0, 0, tiled=True)  10.4 us
  transfers between devices with their start and end apart: 43, of which 14 were waited for; matrix products, arithmetic and copies ran while one was open for 20% of the time, Pallas kernels for 37%

profile of v2, /device:TPU:1, one launch (start us, length us, event | category | flops | bytes accessed | tf_op | source)
XLA Modules:
  0.0 358.8 jit_solution(3748058024533607914)
XLA Ops:
  8.1 4.5 %collective-permute-start.6 = (bf16[768,384]{1,0:T(8,128)(2,1)}, bf16[768,384]{1,0:T(8,128)(2,1)S(1)}, u32[]{:S(2)}, u32[]{:S(2)}) collective-permute-start(bf16[768,384]{1,0:T(8,128)(2,1)} %param.56), channel_id=1, source_target_pairs={{1,2},{2,1},{5,6},{6,5},{9,10},{10,9},{13,14},{14,13},{17,18},{18,... | collective-permute-start | bytes 1769480 | tf_op jit(solution)/shard_map/ppermute | solution.py:878
  16.6 3.6 %collective-permute-start.7 = (f32[2304]{0:T(1024)S(1)}, f32[2304]{0:T(1024)S(1)}, u32[]{:S(2)}, u32[]{:S(2)}) collective-permute-start(f32[2304]{0:T(1024)S(1)} %constant_dynamic-update-slice_fusion), channel_id=1, source_target_pairs={{1,2},{2,1},{5,6},{6,5},{9,10},{10,9},{13,14},{14,13},{17,18},{18,... | collective-permute-start | bytes 27656 | tf_op jit(solution)/shard_map/ppermute | solution.py:878
  22.3 5.1 %encoder_attend.1 = (bf16[16,768]{1,0:T(8,128)(2,1)}, bf16[16,384]{1,0:T(8,128)(2,1)}, bf16[96,768]{1,0:T(8,128)(2,1)}, f32[96,1024]{1,0:T(8,128)}, bf16[96,768]...) custom-call(s32[1,8]{1,0:T(1,128)} %refs_1_.13, bf16[1024,768]{1,0:T(8,128)(2,1)} %refs_12_.1, ...), custom_call_target="tpu_custom_call" | custom-call | tf_op jit(solution)/shard_map/encoder_attend/pallas_call | solution.py:46
  27.4 3.8 %collective-permute-start.3 = (bf16[768,384]{1,0:T(8,128)(2,1)S(1)}, bf16[768,384]{1,0:T(8,128)(2,1)S(1)}, u32[]{:S(2)}, u32[]{:S(2)}) collective-permute-start(bf16[768,384]{1,0:T(8,128)(2,1)S(1)} %copy-done.26), channel_id=1, source_target_pairs={{1,2},{2,1},{5,6},{6,5},{9,10},{10,9},{13,14},{14,13},{17,18},{18,... | collective-permute-start | bytes 1769480 | tf_op jit(solution)/shard_map/ppermute | solution.py:878
  35.6 4.1 %collective-permute-done.3 = bf16[768,384]{1,0:T(8,128)(2,1)S(1)} collective-permute-done((bf16[768,384]{1,0:T(8,128)(2,1)S(1)}, bf16[768,384]{1,0:T(8,128)(2,1)S(1)}, u32[]{:S(2)}, u32[]{:S(2)}) %collective-permute-start.3) | collective-permute-done | bytes 589856 | tf_op jit(solution)/shard_map/ppermute | solution.py:878
  41.3 4.4 %encoder_feed.1 = (f32[16,768]{1,0:T(8,128)}, f32[16,1]{1,0:T(8,128)}, f32[16,768]{1,0:T(8,128)}, bf16[768,128]{1,0:T(8,128)(2,1)}, bf16[16,1536]{1,0:T(8,128)(2...) custom-call(bf16[16,768]{1,0:T(8,128)(2,1)} %get-tuple-element.105.refs_0_, ...), custom_call_target="tpu_custom_call" | custom-call | tf_op jit(solution)/shard_map/encoder_feed/pallas_call | solution.py:46
  49.2 5.0 %copied.1 = (bf16[768,1536]{1,0:T(8,128)(2,1)}, bf16[768,1536]{1,0:T(8,128)(2,1)}) custom-call(bf16[768,1536]{1,0:T(8,128)(2,1)} %refs_0_.4, bf16[768,1536]{1,0:T(8,128)(2,1)} %refs_1_.8, bf16[16,768]{1,0:T(8,128)(2,1)} %get-tuple-element.106.refs_1_.refs_2_), custom_call_target="tpu_custom_call" | custom-call | tf_op jit(solution)/shard_map/copied/pallas_call | solution.py:46
  57.0 2.2 collective-permute-start.11
  59.7 3.3 collective-permute-start.12
  64.2 19.3 %decoder_attend.1 = (f32[1024,768]{1,0:T(8,128)}, bf16[1024,768]{1,0:T(8,128)(2,1)}, bf16[1024,384]{1,0:T(8,128)(2,1)}, bf16[1024,384]{1,0:T(8,128)(2,1)}, bf16[...) custom-call(s32[1]{0:T(128)} %bitcast.refs_0_, ...), custom_call_target="tpu_custom_call" | custom-call | tf_op jit(solution)/shard_map/decoder_attend/pallas_call | solution.py:46
  84.6 3.9 %collective-permute-done.10.refs_2_ = bf16[1024,768]{1,0:T(8,128)(2,1)S(1)} collective-permute-done((bf16[1024,768]{1,0:T(8,128)(2,1)}, bf16[1024,768]{1,0:T(8,128)(2,1)S(1)}, u32[]{:S(2)}, u32[]{:S(2)}) %collective-permute-start.10) | collective-permute-done | bytes 1572896 | tf_op jit(solution)/shard_map/ppermute | solution.py:878
  89.7 6.1 %decoder_norm.1 = (f32[1024,768]{1,0:T(8,128)}, f32[1024,1]{1,0:T(8,128)}, bf16[1024,768]{1,0:T(8,128)(2,1)}) custom-call(f32[1024,768]{1,0:T(8,128)} %get-tuple-element.113.refs_0_, bf16[1024,768]{1,0:T(8,128)(2,1)} %get-tuple-element.114.refs_1_, bf16[1024,768]{1,0:T(8,128)(2,1)} %copy-done.16, f32[768]{0:T(1024)} %refs_3_.10, f32[768]{0:T(1024)} %refs_5_.9, ...), custom_call_target="tpu_custom_call" | custom-call | tf_op jit(solution)/shard_map/decoder_norm/pallas_call | solution.py:46
  95.8 3.3 broadcast_select_fusion.1.refs_1_
  99.1 10.2 %decoder_hidden.1 = (bf16[1024,1536]{1,0:T(8,128)(2,1)}, bf16[1024,1536]{1,0:T(8,128)(2,1)}) custom-call(bf16[1024,768]{1,0:T(8,128)(2,1)} %get-tuple-element.116.refs_0_.l_ref, bf16[768,1536]{1,0:T(8,128)(2,1)} %broadcast_select_fusion.1.refs_1_, f32[1,1536]{1,0:T(1,128)} %broadcast_in_dim.78.refs_2_), custom_call_target="tpu_custom_call" | custom-call | tf_op jit(solution)/shard_map/decoder_hidden/pallas_call | solution.py:46
  109.2 3.6 collective-permute-done.12
  114.7 2.6 convolution_convert_fusion.1.refs_4_
  117.5 3.4 collective-permute-done.13.refs_5_
  122.0 8.9 %decoder_norm_back.1 = (bf16[1024,768]{1,0:T(8,128)(2,1)}, f32[1024,768]{1,0:T(8,128)}, bf16[1024,768]{1,0:T(8,128)(2,1)}, f32[3,768]{1,0:T(4,128)}) custom-call(s32[1]{0:T(128)} %bitcast.refs_0_, s32[1,8]{1,0:T(1,128)} %refs_1_.13, s32[1,8]{1,0:T(1,128)} %copy-done.41, f32[1024,768]{1,0:T(8,128)} %get-tuple-element.115.refs_3_, ...), custom_call_target="tpu_custom_call" | custom-call | tf_op jit(solution)/shard_map/decoder_norm_back/pallas_call | solution.py:46
  131.0 6.0 %outer_grad.1.refs_3_.refs_0_ = bf16[768,3072]{1,0:T(8,128)(2,1)} custom-call(bf16[1024,768]{1,0:T(8,128)(2,1)} %get-tuple-element.122.l_ref.refs_0_, bf16[1024,1536]{1,0:T(8,128)(2,1)} %get-tuple-element.118.r_ref), custom_call_target="tpu_custom_call" | custom-call | tf_op jit(solution)/shard_map/outer_grad/pallas_call | solution.py:572
  136.9 8.6 %decoder_feed_back.1 = (bf16[1024,1536]{1,0:T(8,128)(2,1)}, f32[1,1536]{1,0:T(1,128)}) custom-call(bf16[1024,768]{1,0:T(8,128)(2,1)} %get-tuple-element.122.l_ref.refs_0_, bf16[768,1536]{1,0:T(8,128)(2,1)} %copy-done.5, bf16[1024,1536]{1,0:T(8,128)(2,1)} %get-tuple-element.123.refs_2_, bf16[768,3072]{1,0:T(8,128)(2,1)} %outer_grad.1.refs_3_.refs_0_), custom_call_target="tpu_custom_call" | custom-call | tf_op jit(solution)/shard_map/decoder_feed_back/pallas_call | solution.py:46
  145.6 5.8 %inner_grad.1.refs_6_ = bf16[768,3072]{1,0:T(8,128)(2,1)} custom-call(bf16[1024,768]{1,0:T(8,128)(2,1)} %get-tuple-element.116.refs_0_.l_ref, bf16[1024,1536]{1,0:T(8,128)(2,1)} %get-tuple-element.124.r_ref, bf16[768,3072]{1,0:T(8,128)(2,1)} %outer_grad.1.refs_3_.refs_0_), custom_call_target="tpu_custom_call", output_to_operand_aliasing={{}: (2, {})} | custom-call | tf_op jit(solution)/shard_map/inner_grad/pallas_call | solution.py:572
  153.1 4.6 %convolution_convert_fusion.refs_1_ = bf16[1024,768]{1,0:T(8,128)(2,1)S(1)} fusion(bf16[1024,1536]{1,0:T(8,128)(2,1)} %get-tuple-element.124.r_ref, bf16[768,1536]{1,0:T(8,128)(2,1)S(1)} %copy-done.2), kind=kOutput, calls=%fused_computation.4 | convolution fusion | flops 2416705536 | bytes 7077888 | tf_op jit(solution)/shard_map/dot_general | solution.py:24
  157.9 3.0 collective-permute-start.15
  162.4 7.3 %decoder_first_back.1 = (f32[1024,768]{1,0:T(8,128)}, bf16[1024,768]{1,0:T(8,128)(2,1)}, f32[3,768]{1,0:T(4,128)}) custom-call(f32[1024,768]{1,0:T(8,128)} %get-tuple-element.121.refs_0_, bf16[1024,768]{1,0:T(8,128)(2,1)} %copy-done.17, bf16[1024,768]{1,0:T(8,128)(2,1)} %copy-done.19, f32[1024,768]{1,0:T(8,128)} %get-tuple-element.115.refs_3_, ...), custom_call_target="tpu_custom_call" | custom-call | tf_op jit(solution)/shard_map/decoder_first_back/pallas_call | solution.py:46
  169.6 22.6 %decoder_attend_back.1 = (bf16[1024,1152]{1,0:T(8,128)(2,1)}, bf16[1024,768]{1,0:T(8,128)(2,1)}, f32[1,768]{1,0:T(1,128)}) custom-call(s32[1]{0:T(128)} %bitcast.refs_0_, s32[1,8]{1,0:T(1,128)} %refs_1_.13, s32[1,8]{1,0:T(1,128)} %copy-done.41, bf16[1024,768]{1,0:T(8,128)(2,1)} %get-tuple-element.127.refs_3_.refs_2_, ...), custom_call_target="tpu_custom_call" | custom-call | tf_op jit(solution)/shard_map/decoder_attend_back/pallas_call | solution.py:46
  193.7 2.2 collective-permute-done.17.refs_5_
  197.0 5.0 %decoder_end.1 = (bf16[1024,768]{1,0:T(8,128)(2,1)}, f32[16,768]{1,0:T(8,128)}, bf16[1024,1152]{1,0:T(8,128)(2,1)}) custom-call(s32[1]{0:T(128)} %bitcast.refs_0_, s32[1,8]{1,0:T(1,128)} %refs_1_.13, s32[1,8]{1,0:T(1,128)} %copy-done.41, f32[1024,768]{1,0:T(8,128)} %get-tuple-element.126.refs_3_, ...), custom_call_target="tpu_custom_call", output_to_operand_aliasing={{2}: (6, {})} | custom-call | tf_op jit(solution)/shard_map/decoder_end/pallas_call | solution.py:46
  202.0 2.9 collective-permute-start.18
  204.9 7.0 %attend_weight_grads.1 = (bf16[768,768]{1,0:T(8,128)(2,1)}, bf16[768,768]{1,0:T(8,128)(2,1)}) custom-call(bf16[1024,768]{1,0:T(8,128)(2,1)} %get-tuple-element.138.refs_0_, bf16[1024,1152]{1,0:T(8,128)(2,1)} %get-tuple-element.139.refs_1_, bf16[1024,768]{1,0:T(8,128)(2,1)} %get-tuple-element.127.refs_3_.refs_2_, bf16[1024,384]{1,0:T(8,128)(2,1)} %get-tuple-element.140.refs_3_), custom_call_target="tpu_custom_call" | custom-call | tf_op jit(solution)/shard_map/attend_weight_grads/pallas_call | solution.py:46
  212.6 4.3 %encoder_feed_back.1 = (f32[16,768]{1,0:T(8,128)}, bf16[16,768]{1,0:T(8,128)(2,1)}, bf16[16,1536]{1,0:T(8,128)(2,1)}, f32[3,768]{1,0:T(4,128)}, f32[1,1536]{1,0:...) custom-call(f32[16,768]{1,0:T(8,128)} %broadcast_select_fusion.7.ref, ...), custom_call_target="tpu_custom_call", output_to_operand_aliasing={{6}: (7, {}), {7}: (8, {})} | custom-call | tf_op jit(solution)/shard_map/encoder_feed_back/pallas_call | solution.py:46
  217.4 2.3 collective-permute-done.19.refs_3_
  220.3 4.9 %encoder_attend_back.1 = (f32[16,768]{1,0:T(8,128)}, f32[3,768]{1,0:T(4,128)}, bf16[16,2304]{1,0:T(8,128)(2,1)}, bf16[768,128]{1,0:T(8,128)(2,1)}, f32[1,384]{1,...) custom-call(s32[1,8]{1,0:T(1,128)} %refs_1_.13, ...), custom_call_target="tpu_custom_call", output_to_operand_aliasing={{8}: (17, {}), {9}: (18, {})} | custom-call | tf_op jit(solution)/shard_map/encoder_attend_back/pallas_call | solution.py:46
  235.3 10.4 %all-to-all-start = ((bf16[16,336,128]{2,1,0:T(8,128)(2,1)}), bf16[16,336,128]{2,1,0:T(8,128)(2,1)}, u32[]{:S(2)}, u32[]{:S(2)}) async-start(bf16[16,336,128]{2,1,0:T(8,128)(2,1)} %pad_maximum_fusion), calls=%async_computation | async-start | bytes 2752512 | tf_op jit(solution)/shard_map/all_to_all | solution.py:1091
  246.4 6.7 %collective-permute-done.20.refs_3_ = bf16[12,1024]{1,0:T(8,128)(2,1)S(1)} collective-permute-done((bf16[12,1024]{1,0:T(8,128)(2,1)S(1)}, bf16[12,1024]{1,0:T(8,128)(2,1)S(1)}, u32[]{:S(2)}, u32[]{:S(2)}) %collective-permute-start.20) | collective-permute-done | bytes 24608 | tf_op jit(solution)/shard_map/ppermute | solution.py:878
  253.9 4.3 %passages_back.1 = (f32[1024,768]{1,0:T(8,128)}, bf16[1024,768]{1,0:T(8,128)(2,1)}, f32[24,768]{1,0:T(8,128)}) custom-call(s32[1]{0:T(128)} %bitcast.1.refs_0_, s32[1,8]{1,0:T(1,128)} %refs_1_.13, bf16[12,1024]{1,0:T(8,128)(2,1)} %copy-done.33, bf16[12,1024]{1,0:T(8,128)(2,1)} %copy-done.37, ...), custom_call_target="tpu_custom_call", output_to_operand_aliasing={{1}: (7, {}), {2}: (8, {})} | custom-call | tf_op jit(solution)/shard_map/passages_back/pallas_call | solution.py:46
  258.3 5.2 %collective-permute-start.25 = (f32[24,768]{1,0:T(8,128)}, f32[24,768]{1,0:T(8,128)S(1)}, u32[]{:S(2)}, u32[]{:S(2)}) collective-permute-start(f32[24,768]{1,0:T(8,128)} %get-tuple-element.174), channel_id=1, source_target_pairs={{0,4},{1,5},{2,6},{3,7},{4,0},{5,1},{6,2},{7,3},{8,12},{9,13},{10,... | collective-permute-start | bytes 221192 | tf_op jit(solution)/shard_map/ppermute | solution.py:878
  264.6 2.8 collective-permute-done.25
  268.4 7.6 %collective-permute-done.26 = f32[24,768]{1,0:T(8,128)S(1)} collective-permute-done((f32[24,768]{1,0:T(8,128)S(1)}, f32[24,768]{1,0:T(8,128)S(1)}, u32[]{:S(2)}, u32[]{:S(2)}) %collective-permute-start.26) | collective-permute-done | bytes 73760 | tf_op jit(solution)/shard_map/ppermute | solution.py:878
  277.4 4.3 %collective-permute-start.24 = (bf16[1024,768]{1,0:T(8,128)(2,1)}, bf16[1024,768]{1,0:T(8,128)(2,1)}, u32[]{:S(2)}, u32[]{:S(2)}) collective-permute-start(bf16[1024,768]{1,0:T(8,128)(2,1)} %get-tuple-element.171), channel_id=1, source_target_pairs={{1,2},{2,1},{5,6},{6,5},{9,10},{10,9},{13,14},{14,13},{17,18},{18,... | collective-permute-start | bytes 4718600 | tf_op jit(solution)/shard_map/ppermute | solution.py:878
  289.8 2.1 collective-permute-start.30
  294.0 5.3 %collective-permute-done.30 = bf16[2,2,1,1,48,768]{5,4,3,2,1,0:T(8,128)(2,1)S(1)} collective-permute-done((bf16[2,2,1,1,48,768]{5,4,3,2,1,0:T(8,128)(2,1)S(1)}, bf16[2,2,1,1,48,768]{5,4,3,2,1,0:T(8,128)(2,1)S(1)}, u32[]{:S(2)}, u32[]{:S(2)}) %collective-permute-start.30) | collective-permute-done | bytes 294944 | tf_op jit(solution)/shard_map/ppermute | solution.py:878
  307.3 2.6 collective-permute-start.32
  317.7 3.3 select_convert_fusion
  328.3 2.1 convolution_bitcast_fusion.2
  333.4 2.2 convolution_bitcast_fusion
  335.6 2.7 collective-permute-done.28
  338.4 5.1 %collective-permute-start.37 = (bf16[48,4608]{1,0:T(8,128)(2,1)S(1)}, bf16[48,4608]{1,0:T(8,128)(2,1)S(1)}, u32[]{:S(2)}, u32[]{:S(2)}) collective-permute-start(bf16[48,4608]{1,0:T(8,128)(2,1)S(1)} %pad_maximum_fusion.1), channel_id=1, source_target_pairs={{1,2},{2,1},{5,6},{6,5},{9,10},{10,9},{13,14},{14,13},{17,18},{18,... | collective-permute-start | bytes 1327112 | tf_op jit(solution)/shard_map/ppermute | solution.py:878
  343.6 2.2 convolution_bitcast_fusion.1
  (221 shorter events, 89.8 us)
Async XLA Ops:
  8.0 209.4 %all-gather.7.cloned.1.call-start = ((), (), s32[]{:S(2)}) async-start(), calls=%async_computation.4 | async-start | bytes 1253376 | tf_op jit(solution)/shard_map/all_gather | solution.py:1020
  8.1 23.7 %collective-permute-start.6 = (bf16[768,384]{1,0:T(8,128)(2,1)}, bf16[768,384]{1,0:T(8,128)(2,1)S(1)}, u32[]{:S(2)}, u32[]{:S(2)}) collective-permute-start(bf16[768,384]{1,0:T(8,128)(2,1)} %param.56), channel_id=1, source_target_pairs={{1,2},{2,1},{5,6},{6,5},{9,10},{10,9},{13,14},{14,13},{17,18},{18,... | collective-permute-start | bytes 1769480 | tf_op jit(solution)/shard_map/ppermute | solution.py:878
  12.6 20.1 %collective-permute-start.5 = (bf16[768,384]{1,0:T(8,128)(2,1)}, bf16[768,384]{1,0:T(8,128)(2,1)S(1)}, u32[]{:S(2)}, u32[]{:S(2)}) collective-permute-start(bf16[768,384]{1,0:T(8,128)(2,1)} %param.55), channel_id=1, source_target_pairs={{1,2},{2,1},{5,6},{6,5},{9,10},{10,9},{13,14},{14,13},{17,18},{18,... | collective-permute-start | bytes 1769480 | tf_op jit(solution)/shard_map/ppermute | solution.py:878
  16.6 10.8 %collective-permute-start.7 = (f32[2304]{0:T(1024)S(1)}, f32[2304]{0:T(1024)S(1)}, u32[]{:S(2)}, u32[]{:S(2)}) collective-permute-start(f32[2304]{0:T(1024)S(1)} %constant_dynamic-update-slice_fusion), channel_id=1, source_target_pairs={{1,2},{2,1},{5,6},{6,5},{9,10},{10,9},{13,14},{14,13},{17,18},{18,... | collective-permute-start | bytes 27656 | tf_op jit(solution)/shard_map/ppermute | solution.py:878
  20.3 13.4 %collective-permute-start.4 = (bf16[768,384]{1,0:T(8,128)(2,1)}, bf16[768,384]{1,0:T(8,128)(2,1)}, u32[]{:S(2)}, u32[]{:S(2)}) collective-permute-start(bf16[768,384]{1,0:T(8,128)(2,1)} %param.54), channel_id=1, source_target_pairs={{1,2},{2,1},{5,6},{6,5},{9,10},{10,9},{13,14},{14,13},{17,18},{18,... | collective-permute-start | bytes 1769480 | tf_op jit(solution)/shard_map/ppermute | solution.py:878
  22.2 18.4 %collective-permute-start = (s32[1,8]{1,0:T(1,128)}, s32[1,8]{1,0:T(1,128)S(1)}, u32[]{:S(2)}, u32[]{:S(2)}) collective-permute-start(s32[1,8]{1,0:T(1,128)} %refs_1_.13), channel_id=1, source_target_pairs={{0,2},{1,3},{2,0},{3,1},{4,6},{5,7},{6,4},{7,5},{8,10},{9,11},{10,... | collective-permute-start | bytes 104 | tf_op jit(solution)/shard_map/ppermute | solution.py:878
  27.4 12.3 %collective-permute-start.3 = (bf16[768,384]{1,0:T(8,128)(2,1)S(1)}, bf16[768,384]{1,0:T(8,128)(2,1)S(1)}, u32[]{:S(2)}, u32[]{:S(2)}) collective-permute-start(bf16[768,384]{1,0:T(8,128)(2,1)S(1)} %copy-done.26), channel_id=1, source_target_pairs={{1,2},{2,1},{5,6},{6,5},{9,10},{10,9},{13,14},{14,13},{17,18},{18,... | collective-permute-start | bytes 1769480 | tf_op jit(solution)/shard_map/ppermute | solution.py:878
  31.8 8.8 %collective-permute-start.2 = (bf16[16,768]{1,0:T(8,128)(2,1)}, bf16[16,768]{1,0:T(8,128)(2,1)S(1)}, u32[]{:S(2)}, u32[]{:S(2)}) collective-permute-start(bf16[16,768]{1,0:T(8,128)(2,1)} %get-tuple-element.106.refs_1_.refs_2_), channel_id=1, source_target_pairs={{0,1},{1,0},{2,3},{3,2},{4,5},{5,4},{6,7},{7,6},{8,9},{9,8},{10,11... | collective-permute-start | bytes 73736 | tf_op jit(solution)/shard_map/ppermute | solution.py:878
  47.2 170.2 %all-gather.5.cloned.1.call-start = ((), (), s32[]{:S(2)}) async-start(), calls=%async_computation.3 | async-start | bytes 3342336 | tf_op jit(solution)/shard_map/all_gather | solution.py:1019
  47.2 7.0 %collective-permute-start.1 = (bf16[1024,768]{1,0:T(8,128)(2,1)S(1)}, bf16[1024,768]{1,0:T(8,128)(2,1)S(1)}, u32[]{:S(2)}, u32[]{:S(2)}) collective-permute-start(bf16[1024,768]{1,0:T(8,128)(2,1)S(1)} %copy-done.15), channel_id=1, source_target_pairs={{0,2},{1,3},{2,0},{3,1},{4,6},{5,7},{6,4},{7,5},{8,10},{9,11},{10,... | collective-permute-start | bytes 4718600 | tf_op jit(solution)/shard_map/ppermute | solution.py:878
  47.3 6.9 %collective-permute-start.8 = (bf16[16,768]{1,0:T(8,128)(2,1)}, bf16[16,768]{1,0:T(8,128)(2,1)S(1)}, u32[]{:S(2)}, u32[]{:S(2)}) collective-permute-start(bf16[16,768]{1,0:T(8,128)(2,1)} %get-tuple-element.109.refs_1_), channel_id=1, source_target_pairs={{0,1},{1,0},{2,3},{3,2},{4,5},{5,4},{6,7},{7,6},{8,9},{9,8},{10,11... | collective-permute-start | bytes 73736 | tf_op jit(solution)/shard_map/ppermute | solution.py:878
  57.0 38.7 %collective-permute-start.11 = (bf16[768,1536]{1,0:T(8,128)(2,1)}, bf16[768,1536]{1,0:T(8,128)(2,1)}, u32[]{:S(2)}, u32[]{:S(2)}) collective-permute-start(bf16[768,1536]{1,0:T(8,128)(2,1)} %get-tuple-element.117), channel_id=1, source_target_pairs={{1,2},{2,1},{5,6},{6,5},{9,10},{10,9},{13,14},{14,13},{17,18},{18,... | collective-permute-start | bytes 7077896 | tf_op jit(solution)/shard_map/ppermute | solution.py:878
  59.3 271.1 %reduce-scatter.2.cloned.1.call-start = ((), (), s32[]{:S(2)}) async-start(), calls=%async_computation.2 | async-start | bytes 5308416 | tf_op jit(solution)/shard_map/reduce_scatter | solution.py:915
  59.3 4.3 %collective-permute-start.9 = (f32[16,768]{1,0:T(8,128)}, f32[16,768]{1,0:T(8,128)S(1)}, u32[]{:S(2)}, u32[]{:S(2)}) collective-permute-start(f32[16,768]{1,0:T(8,128)} %get-tuple-element.112.refs_5_), channel_id=1, source_target_pairs={{0,2},{1,3},{2,0},{3,1},{4,6},{5,7},{6,4},{7,5},{8,10},{9,11},{10,... | collective-permute-start | bytes 147464 | tf_op jit(solution)/shard_map/ppermute | solution.py:878
  59.7 53.1 %collective-permute-start.12 = (bf16[768,1536]{1,0:T(8,128)(2,1)}, bf16[768,1536]{1,0:T(8,128)(2,1)}, u32[]{:S(2)}, u32[]{:S(2)}) collective-permute-start(bf16[768,1536]{1,0:T(8,128)(2,1)} %get-tuple-element.119), channel_id=1, source_target_pairs={{1,2},{2,1},{5,6},{6,5},{9,10},{10,9},{13,14},{14,13},{17,18},{18,... | collective-permute-start | bytes 7077896 | tf_op jit(solution)/shard_map/ppermute | solution.py:878
  64.2 19.3 %copy-start.11 = (bf16[1024,768]{1,0:T(8,128)(2,1)S(1)}, bf16[1024,768]{1,0:T(8,128)(2,1)}, u32[]{:S(2)}) copy-start(bf16[1024,768]{1,0:T(8,128)(2,1)} %refs_11_.2) | copy-start | bytes 4718596
  83.5 5.0 %collective-permute-start.10 = (bf16[1024,768]{1,0:T(8,128)(2,1)}, bf16[1024,768]{1,0:T(8,128)(2,1)S(1)}, u32[]{:S(2)}, u32[]{:S(2)}) collective-permute-start(bf16[1024,768]{1,0:T(8,128)(2,1)} %get-tuple-element.114.refs_1_), channel_id=1, source_target_pairs={{0,2},{1,3},{2,0},{3,1},{4,6},{5,7},{6,4},{7,5},{8,10},{9,11},{10,... | collective-permute-start | bytes 4718600 | tf_op jit(solution)/shard_map/ppermute | solution.py:878
  83.5 34.0 %collective-permute-start.14 = (bf16[1024,768]{1,0:T(8,128)(2,1)S(1)}, bf16[1024,768]{1,0:T(8,128)(2,1)}, u32[]{:S(2)}, u32[]{:S(2)}) collective-permute-start(bf16[1024,768]{1,0:T(8,128)(2,1)S(1)} %copy-done.11), channel_id=1, source_target_pairs={{0,2},{1,3},{2,0},{3,1},{4,6},{5,7},{6,4},{7,5},{8,10},{9,11},{10,... | collective-permute-start | bytes 4718600 | tf_op jit(solution)/shard_map/ppermute | solution.py:878
  99.1 13.7 %copy-start.4 = (bf16[768,1536]{1,0:T(8,128)(2,1)S(1)}, bf16[768,1536]{1,0:T(8,128)(2,1)}, u32[]{:S(2)}) copy-start(bf16[768,1536]{1,0:T(8,128)(2,1)} %get-tuple-element.119) | copy-start | bytes 7077892
  117.4 3.5 collective-permute-start.13
  157.7 3.5 collective-permute-start.16
  157.9 34.6 %collective-permute-start.15 = (bf16[1024,768]{1,0:T(8,128)(2,1)S(1)}, bf16[1024,768]{1,0:T(8,128)(2,1)S(1)}, u32[]{:S(2)}, u32[]{:S(2)}) collective-permute-start(bf16[1024,768]{1,0:T(8,128)(2,1)S(1)} %copy-done.12), channel_id=1, source_target_pairs={{1,2},{2,1},{5,6},{6,5},{9,10},{10,9},{13,14},{14,13},{17,18},{18,... | collective-permute-start | bytes 4718600 | tf_op jit(solution)/shard_map/ppermute | solution.py:878
  192.3 3.6 %collective-permute-start.17 = (bf16[1024,768]{1,0:T(8,128)(2,1)}, bf16[1024,768]{1,0:T(8,128)(2,1)S(1)}, u32[]{:S(2)}, u32[]{:S(2)}) collective-permute-start(bf16[1024,768]{1,0:T(8,128)(2,1)} %get-tuple-element.132.refs_4_), channel_id=1, source_target_pairs={{0,2},{1,3},{2,0},{3,1},{4,6},{5,7},{6,4},{7,5},{8,10},{9,11},{10,... | collective-permute-start | bytes 4718600 | tf_op jit(solution)/shard_map/ppermute | solution.py:878
  202.0 9.9 %collective-permute-start.18 = (f32[16,768]{1,0:T(8,128)}, f32[16,768]{1,0:T(8,128)S(1)}, u32[]{:S(2)}, u32[]{:S(2)}) collective-permute-start(f32[16,768]{1,0:T(8,128)} %get-tuple-element.134), channel_id=1, source_target_pairs={{1,2},{2,1},{5,6},{6,5},{9,10},{10,9},{13,14},{14,13},{17,18},{18,... | collective-permute-start | bytes 147464 | tf_op jit(solution)/shard_map/ppermute | solution.py:878
  216.8 2.9 collective-permute-start.19
  226.8 18.9 %collective-permute-start.22 = (f32[24,768]{1,0:T(8,128)}, f32[24,768]{1,0:T(8,128)S(1)}, u32[]{:S(2)}, u32[]{:S(2)}) collective-permute-start(f32[24,768]{1,0:T(8,128)} %pack_vectors.1), channel_id=1, source_target_pairs={{0,2},{1,3},{2,0},{3,1},{4,6},{5,7},{6,4},{7,5},{8,10},{9,11},{10,... | collective-permute-start | bytes 221192 | tf_op jit(solution)/shard_map/ppermute | solution.py:878
  227.0 18.7 %collective-permute-start.23 = (f32[24,768]{1,0:T(8,128)}, f32[24,768]{1,0:T(8,128)S(1)}, u32[]{:S(2)}, u32[]{:S(2)}) collective-permute-start(f32[24,768]{1,0:T(8,128)} %pack_vectors.1), channel_id=1, source_target_pairs={{0,1},{1,0},{2,3},{3,2},{4,5},{5,4},{6,7},{7,6},{8,9},{9,8},{10,11... | collective-permute-start | bytes 221192 | tf_op jit(solution)/shard_map/ppermute | solution.py:878
  230.7 58.1 %collective-permute-start.29 = (bf16[2,2,2,1,48,768]{5,4,3,2,1,0:T(8,128)(2,1)}, bf16[2,2,2,1,48,768]{5,4,3,2,1,0:T(8,128)(2,1)}, u32[]{:S(2)}, u32[]{:S(2)}) collective-permute-start(bf16[2,2,2,1,48,768]{5,4,3,2,1,0:T(8,128)(2,1)} %constant_dynamic-slice_fusion.1), channel_id=1, source_target_pairs={{0,1},{1,0},{2,3},{3,2},{4,5},{5,4},{6,7},{7,6},{8,9},{9,8},{10,11... | collective-permute-start | bytes 1769480 | tf_op jit(solution)/shard_map/ppermute | solution.py:878
  230.7 22.5 %collective-permute-start.21 = (bf16[208,768]{1,0:T(8,128)(2,1)}, bf16[208,768]{1,0:T(8,128)(2,1)S(1)}, u32[]{:S(2)}, u32[]{:S(2)}) collective-permute-start(bf16[208,768]{1,0:T(8,128)(2,1)} %get-tuple-element.158.refs_4_), channel_id=1, source_target_pairs={{0,1},{1,0},{2,3},{3,2},{4,5},{5,4},{6,7},{7,6},{8,9},{9,8},{10,11... | collective-permute-start | bytes 958472 | tf_op jit(solution)/shard_map/ppermute | solution.py:878
  233.0 20.2 %collective-permute-start.20 = (bf16[12,1024]{1,0:T(8,128)(2,1)S(1)}, bf16[12,1024]{1,0:T(8,128)(2,1)S(1)}, u32[]{:S(2)}, u32[]{:S(2)}) collective-permute-start(bf16[12,1024]{1,0:T(8,128)(2,1)S(1)} %convert_element_type.131.refs_2_), channel_id=1, source_target_pairs={{0,1},{1,0},{2,3},{3,2},{4,5},{5,4},{6,7},{7,6},{8,9},{9,8},{10,11... | collective-permute-start | bytes 73736 | tf_op jit(solution)/shard_map/ppermute | solution.py:878
  235.3 85.7 %all-to-all-start = ((bf16[16,336,128]{2,1,0:T(8,128)(2,1)}), bf16[16,336,128]{2,1,0:T(8,128)(2,1)}, u32[]{:S(2)}, u32[]{:S(2)}) async-start(bf16[16,336,128]{2,1,0:T(8,128)(2,1)} %pad_maximum_fusion), calls=%async_computation | async-start | bytes 2752512 | tf_op jit(solution)/shard_map/all_to_all | solution.py:1091
  245.7 17.8 %copy-start.1 = (bf16[2,2,2,2,48,768]{5,4,3,2,1,0:T(8,128)(2,1)S(1)}, bf16[2,2,2,2,48,768]{5,4,3,2,1,0:T(8,128)(2,1)}, u32[]{:S(2)}) copy-start(bf16[2,2,2,2,48,768]{5,4,3,2,1,0:T(8,128)(2,1)} %get-tuple-element.176) | copy-start | bytes 3538948
  253.9 22.7 %copy-start.9 = (bf16[256,2304]{1,0:T(8,128)(2,1)S(1)}, bf16[256,2304]{1,0:T(8,128)(2,1)}, u32[]{:S(2)}) copy-start(bf16[256,2304]{1,0:T(8,128)(2,1)} %all-gather.7.cloned.1.call-done) | copy-start | bytes 3538948
  258.3 30.5 %copy-start = (bf16[2,2,2,2,48,768]{5,4,3,2,1,0:T(8,128)(2,1)S(1)}, bf16[2,2,2,2,48,768]{5,4,3,2,1,0:T(8,128)(2,1)}, u32[]{:S(2)}) copy-start(bf16[2,2,2,2,48,768]{5,4,3,2,1,0:T(8,128)(2,1)} %get-tuple-element.175) | copy-start | bytes 3538948
  258.3 9.2 %collective-permute-start.25 = (f32[24,768]{1,0:T(8,128)}, f32[24,768]{1,0:T(8,128)S(1)}, u32[]{:S(2)}, u32[]{:S(2)}) collective-permute-start(f32[24,768]{1,0:T(8,128)} %get-tuple-element.174), channel_id=1, source_target_pairs={{0,4},{1,5},{2,6},{3,7},{4,0},{5,1},{6,2},{7,3},{8,12},{9,13},{10,... | collective-permute-start | bytes 221192 | tf_op jit(solution)/shard_map/ppermute | solution.py:878
  264.3 27.6 %collective-permute-start.33 = (bf16[2,2,2,1,48,768]{5,4,3,2,1,0:T(8,128)(2,1)}, bf16[2,2,2,1,48,768]{5,4,3,2,1,0:T(8,128)(2,1)}, u32[]{:S(2)}, u32[]{:S(2)}) collective-permute-start(bf16[2,2,2,1,48,768]{5,4,3,2,1,0:T(8,128)(2,1)} %constant_dynamic-slice_fusion), channel_id=1, source_target_pairs={{0,1},{1,0},{2,3},{3,2},{4,5},{5,4},{6,7},{7,6},{8,9},{9,8},{10,11... | collective-permute-start | bytes 1769480 | tf_op jit(solution)/shard_map/ppermute | solution.py:878
  268.3 7.7 %collective-permute-start.26 = (f32[24,768]{1,0:T(8,128)S(1)}, f32[24,768]{1,0:T(8,128)S(1)}, u32[]{:S(2)}, u32[]{:S(2)}) collective-permute-start(f32[24,768]{1,0:T(8,128)S(1)} %add.81), channel_id=1, source_target_pairs={{0,8},{1,9},{2,10},{3,11},{4,12},{5,13},{6,14},{7,15},{8,0},{9,1},... | collective-permute-start | bytes 221192 | tf_op jit(solution)/shard_map/ppermute | solution.py:878
  276.6 5.0 %collective-permute-start.27 = (f32[24,768]{1,0:T(8,128)}, f32[24,768]{1,0:T(8,128)}, u32[]{:S(2)}, u32[]{:S(2)}) collective-permute-start(f32[24,768]{1,0:T(8,128)} %add.82), channel_id=1, source_target_pairs={{0,16},{1,17},{2,18},{3,19},{4,20},{5,21},{6,22},{7,23},{8,24},{9,... | collective-permute-start | bytes 221192 | tf_op jit(solution)/shard_map/ppermute | solution.py:878
  277.4 40.4 %collective-permute-start.24 = (bf16[1024,768]{1,0:T(8,128)(2,1)}, bf16[1024,768]{1,0:T(8,128)(2,1)}, u32[]{:S(2)}, u32[]{:S(2)}) collective-permute-start(bf16[1024,768]{1,0:T(8,128)(2,1)} %get-tuple-element.171), channel_id=1, source_target_pairs={{1,2},{2,1},{5,6},{6,5},{9,10},{10,9},{13,14},{14,13},{17,18},{18,... | collective-permute-start | bytes 4718600 | tf_op jit(solution)/shard_map/ppermute | solution.py:878
  283.3 10.0 %collective-permute-start.38 = (f32[3,768]{1,0:T(4,128)}, f32[3,768]{1,0:T(4,128)}, u32[]{:S(2)}, u32[]{:S(2)}) collective-permute-start(f32[3,768]{1,0:T(4,128)} %slice.222), channel_id=1, source_target_pairs={{0,2},{1,3},{2,0},{3,1},{4,6},{5,7},{6,4},{7,5},{8,10},{9,11},{10,... | collective-permute-start | bytes 27656 | tf_op jit(solution)/shard_map/ppermute | solution.py:878
  289.8 9.4 %collective-permute-start.30 = (bf16[2,2,1,1,48,768]{5,4,3,2,1,0:T(8,128)(2,1)S(1)}, bf16[2,2,1,1,48,768]{5,4,3,2,1,0:T(8,128)(2,1)S(1)}, u32[]{:S(2)}, u32[]{:S(2)}) collective-permute-start(bf16[2,2,1,1,48,768]{5,4,3,2,1,0:T(8,128)(2,1)S(1)} %add_convert_fusion.1), channel_id=1, source_target_pairs={{0,4},{1,5},{2,6},{3,7},{4,0},{5,1},{6,2},{7,3},{8,12},{9,13},{10,... | collective-permute-start | bytes 884744 | tf_op jit(solution)/shard_map/ppermute | solution.py:878
  293.0 9.5 %collective-permute-start.34 = (bf16[2,1,2,1,48,768]{5,4,3,2,1,0:T(8,128)(2,1)S(1)}, bf16[2,1,2,1,48,768]{5,4,3,2,1,0:T(8,128)(2,1)S(1)}, u32[]{:S(2)}, u32[]{:S(2)}) collective-permute-start(bf16[2,1,2,1,48,768]{5,4,3,2,1,0:T(8,128)(2,1)S(1)} %add_convert_fusion), channel_id=1, source_target_pairs={{0,8},{1,9},{2,10},{3,11},{4,12},{5,13},{6,14},{7,15},{8,0},{9,1},... | collective-permute-start | bytes 884744 | tf_op jit(solution)/shard_map/ppermute | solution.py:878
  301.0 5.2 %collective-permute-start.31 = (bf16[2,1,1,1,48,768]{5,4,3,2,1,0:T(8,128)(2,1)}, bf16[2,1,1,1,48,768]{5,4,3,2,1,0:T(8,128)(2,1)}, u32[]{:S(2)}, u32[]{:S(2)}) collective-permute-start(bf16[2,1,1,1,48,768]{5,4,3,2,1,0:T(8,128)(2,1)} %add_convert_fusion.4), channel_id=1, source_target_pairs={{0,8},{1,9},{2,10},{3,11},{4,12},{5,13},{6,14},{7,15},{8,0},{9,1},... | collective-permute-start | bytes 442376 | tf_op jit(solution)/shard_map/ppermute | solution.py:878
  304.8 5.2 %collective-permute-start.35 = (bf16[2,1,1,1,48,768]{5,4,3,2,1,0:T(8,128)(2,1)}, bf16[2,1,1,1,48,768]{5,4,3,2,1,0:T(8,128)(2,1)}, u32[]{:S(2)}, u32[]{:S(2)}) collective-permute-start(bf16[2,1,1,1,48,768]{5,4,3,2,1,0:T(8,128)(2,1)} %add_convert_fusion.3), channel_id=1, source_target_pairs={{0,4},{1,5},{2,6},{3,7},{4,0},{5,1},{6,2},{7,3},{8,12},{9,13},{10,... | collective-permute-start | bytes 442376 | tf_op jit(solution)/shard_map/ppermute | solution.py:878
  307.3 5.4 %collective-permute-start.32 = (bf16[1,1,1,1,48,768]{5,4,3,2,1,0:T(8,128)(2,1)S(1)}, bf16[1,1,1,1,48,768]{5,4,3,2,1,0:T(8,128)(2,1)S(1)}, u32[]{:S(2)}, u32[]{:S(2)}) collective-permute-start(bf16[1,1,1,1,48,768]{5,4,3,2,1,0:T(8,128)(2,1)S(1)} %add_convert_fusion.8), channel_id=1, source_target_pairs={{0,16},{1,17},{2,18},{3,19},{4,20},{5,21},{6,22},{7,23},{8,24},{9,... | collective-permute-start | bytes 221192 | tf_op jit(solution)/shard_map/ppermute | solution.py:878
  311.0 5.1 %collective-permute-start.36 = (bf16[1,1,1,1,48,768]{5,4,3,2,1,0:T(8,128)(2,1)S(1)}, bf16[1,1,1,1,48,768]{5,4,3,2,1,0:T(8,128)(2,1)S(1)}, u32[]{:S(2)}, u32[]{:S(2)}) collective-permute-start(bf16[1,1,1,1,48,768]{5,4,3,2,1,0:T(8,128)(2,1)S(1)} %add_convert_fusion.6), channel_id=1, source_target_pairs={{0,16},{1,17},{2,18},{3,19},{4,20},{5,21},{6,22},{7,23},{8,24},{9,... | collective-permute-start | bytes 221192 | tf_op jit(solution)/shard_map/ppermute | solution.py:878
  331.4 6.9 %collective-permute-start.28 = (bf16[1,48,3072]{2,1,0:T(8,128)(2,1)S(1)}, bf16[1,48,3072]{2,1,0:T(8,128)(2,1)S(1)}, u32[]{:S(2)}, u32[]{:S(2)}) collective-permute-start(bf16[1,48,3072]{2,1,0:T(8,128)(2,1)S(1)} %constant_dynamic-slice_fusion.2), channel_id=1, source_target_pairs={{0,1},{1,0},{2,3},{3,2},{4,5},{5,4},{6,7},{7,6},{8,9},{9,8},{10,11... | collective-permute-start | bytes 884744 | tf_op jit(solution)/shard_map/ppermute | solution.py:878
  338.4 11.1 %collective-permute-start.37 = (bf16[48,4608]{1,0:T(8,128)(2,1)S(1)}, bf16[48,4608]{1,0:T(8,128)(2,1)S(1)}, u32[]{:S(2)}, u32[]{:S(2)}) collective-permute-start(bf16[48,4608]{1,0:T(8,128)(2,1)S(1)} %pad_maximum_fusion.1), channel_id=1, source_target_pairs={{1,2},{2,1},{5,6},{6,5},{9,10},{10,9},{13,14},{14,13},{17,18},{18,... | collective-permute-start | bytes 1327112 | tf_op jit(solution)/shard_map/ppermute | solution.py:878
  (40 other events, 161.4 us)
Sparse Core Ops, SparseCore 0:
  47.3 41.6 all-gather.6
  91.9 44.5 all-gather.4
Sparse Core Ops, SparseCore 1:
  151.5 95.2 reduce-scatter.1
